TPU v7x, 32 devices: a whole 2x2x4 slice. The times are simulated.
32 devices in a mesh: dp: 4 (over y, x), blk: 8 (over z, core).
Axes of the slice: x: 2, y: 2, z: 4, core: 2. Of those that a mesh axis runs over, the one named last changes fastest.
Arguments:
- latents: bfloat16 [2, 4, 1024, 1152], P(None, 'dp', 'blk'), may hold values from -6 to 6
- conditions: bfloat16 [2, 4, 4, 1152], P(None, 'dp'), may hold values from -6 to 6
- doc_lengths: int32 [2, 4, 4], P(None, 'dp'), may hold values from 0 to 1024, as said below
- cotangent: bfloat16 [2, 4, 1024, 1152], P(None, 'dp', 'blk'), may hold values from -6 to 6
- ada_weight: bfloat16 [1152, 6912], P('dp'), may hold values from -0.1875 to 0.1875
- ada_bias: bfloat16 [6912], P('dp'), may hold values from -1.75 to 1.75
- qkv_weight: bfloat16 [1152, 3456], P('dp'), may hold values from -0.1875 to 0.1875
- qv_bias: bfloat16 [2, 1152], P(None, 'dp'), may hold values from -0.3125 to 0.3125
- proj_weight: bfloat16 [1152, 1152], P('dp'), may hold values from -2 to 2
- proj_bias: bfloat16 [1152], P('dp'), may hold values from -1.75 to 1.75
- fc1_weight: bfloat16 [1152, 4608], P('dp'), may hold values from -0.1875 to 0.1875
- fc1_bias: bfloat16 [4608], P('dp'), may hold values from -3 to 3
- fc2_weight: bfloat16 [4608, 1152], P('dp'), may hold values from -0.09375 to 0.09375
- fc2_bias: bfloat16 [1152], P('dp'), may hold values from -1.75 to 1.75
Outputs:
- block_out: bfloat16 [2, 4, 1024, 1152], P(None, 'dp', 'blk')
- latent_grad: float32 [2, 4, 1024, 1152], P(None, 'dp', 'blk')
- cond_grad: float32 [2, 4, 4, 1152], P(None, 'dp')
- ada_wgrad: float32 [1152, 6912], P('dp')
- ada_bgrad: float32 [6912], P('dp')
- qkv_wgrad: float32 [1152, 3456], P('dp')
- qv_bgrad: float32 [2, 1152], P(None, 'dp')
- proj_wgrad: float32 [1152, 1152], P('dp')
- proj_bgrad: float32 [1152], P('dp')
- fc1_wgrad: float32 [1152, 4608], P('dp')
- fc1_bgrad: float32 [4608], P('dp')
- fc2_wgrad: float32 [4608, 1152], P('dp')
- fc2_bgrad: float32 [1152], P('dp')
Inputs may be any that keep to these rules, and one draw needn't show every extreme that they name: `doc_lengths`: in every row the 4 lengths sum to 1024; a row's positions are its slots' images in slot order, and a slot may be empty. Of the 2 rows that one index of dp holds over all micro-batches, exactly one is a single image in slot 0; every other row holds two or more images.
All inputs are finite; a program needn't handle non-finite values.
Results may differ from a plain program's by a relative error of at most 0.019.
Values may be sent and summed in bfloat16 or wider, within the bound.
No kernel may reach another device: no remote copies, remote signals or barrier semaphores. Data moves between devices by JAX's collectives and lax.ppermute only.
A program may use at most 208 MiB of HBM per device.

v0:
```python
import math

import jax
import jax.numpy as jnp
from jax import lax
from jax.sharding import PartitionSpec as P

HEADS = 16
HEAD = 72
DOCS = 4


norm_eps = 1e-06
masked_score = -1e30
highest = lax.Precision.HIGHEST


def layer_normalizer(values):
    center = jnp.mean(values, axis=-1, keepdims=True)
    centred = values - center
    inverse = lax.rsqrt(jnp.mean(centred * centred, axis=-1, keepdims=True) + norm_eps)
    return (centred * inverse, inverse)


def norm_backward_pass(grad_in, normed, inverse):
    first_mean = jnp.mean(grad_in, axis=-1, keepdims=True)
    second_mean = jnp.mean(grad_in * normed, axis=-1, keepdims=True)
    return inverse * (grad_in - first_mean - normed * second_mean)


def gelu_tanh(values):
    return jax.nn.gelu(values, approximate=True)


def doc_index(doc_ends, positions):
    return jnp.sum((positions[None, :, None] >= doc_ends[:, None, :]).astype(jnp.int32), axis=-1)


def by_blocks(step_fn, running, piece):
    count = piece[0].shape[1]
    width = math.gcd(count, 512)
    pieces = count // width
    divide_rows = tuple(
        (
            jnp.moveaxis(part.reshape((part.shape[0], pieces, width) + part.shape[2:]), 1, 0)
            for part in piece
        )
    )

    def inner(carry, item):
        index, sub_piece = item
        return (step_fn(carry, sub_piece, index * width), None)

    result, unused = lax.scan(inner, running, (jnp.arange(pieces, dtype=jnp.int32), divide_rows))
    return result


def micro_step(latent, conds, lengths, grad_out, weights):
    (
        ada_weight,
        ada_bias,
        qkv_weight,
        qv_bias,
        proj_weight,
        proj_bias,
        fc1_weight,
        fc1_bias,
        fc2_weight,
        fc2_bias,
    ) = weights
    row_count, seg_len, features = latent.shape
    tok_count = row_count * seg_len
    row_len = seg_len * lax.axis_size("blk")
    my_rank = lax.axis_index("blk")
    inv_root = HEAD ** (-0.5)
    doc_ends = jnp.cumsum(lengths, axis=-1)
    doc_query = doc_index(doc_ends, my_rank * seg_len + jnp.arange(seg_len, dtype=jnp.int32))
    doc_pick = (doc_query[:, :, None] == jnp.arange(DOCS, dtype=jnp.int32)[None, None, :]).astype(
        jnp.float32
    )
    cond_f = conds.astype(jnp.float32)
    cond_act = jax.nn.silu(cond_f).astype(jnp.bfloat16).reshape(row_count * DOCS, features)
    mod_all = jnp.dot(cond_act, ada_weight, preferred_element_type=jnp.float32) + ada_bias.astype(
        jnp.float32
    )
    mod_tok = jnp.einsum(
        "rsd,rdc->rsc", doc_pick, mod_all.reshape(row_count, DOCS, 6 * features), precision=highest
    )
    (
        selfattention_shift,
        selfattention_scale,
        selfattention_gate,
        feedforward_shift,
        feedforward_scale,
        feedforward_gate,
    ) = jnp.split(mod_tok.reshape(tok_count, 6 * features), 6, axis=-1)
    latent_float = latent.astype(jnp.float32).reshape(tok_count, features)
    selfattention_normed_input, selfattention_inverse_norm = layer_normalizer(latent_float)
    attention_input = (
        selfattention_normed_input * (1.0 + selfattention_scale) + selfattention_shift
    ).astype(jnp.bfloat16)
    proj_qkv = jnp.dot(attention_input, qkv_weight, preferred_element_type=jnp.float32)
    bias_f = qv_bias.astype(jnp.float32)
    query = (
        (proj_qkv[:, :features] + bias_f[0])
        .astype(jnp.bfloat16)
        .reshape(row_count, seg_len, HEADS, HEAD)
    )
    keys = (
        proj_qkv[:, features : 2 * features]
        .astype(jnp.bfloat16)
        .reshape(row_count, seg_len, features)
    )
    values = (
        (proj_qkv[:, 2 * features :] + bias_f[1])
        .astype(jnp.bfloat16)
        .reshape(row_count, seg_len, features)
    )

    def block_scores(kv_block, first_row):
        count = kv_block[0].shape[1]
        key_heads = kv_block[0].reshape(row_count, count, HEADS, HEAD)
        value_heads = kv_block[1].reshape(row_count, count, HEADS, HEAD)
        doc_key = doc_index(doc_ends, first_row + jnp.arange(count, dtype=jnp.int32))
        allowed = (doc_query[:, :, None] == doc_key[:, None, :])[:, :, None, :]
        scores = (
            jnp.einsum("rqhd,rkhd->rqhk", query, key_heads, preferred_element_type=jnp.float32)
            * inv_root
        )
        return (jnp.where(allowed, scores, masked_score), allowed, key_heads, value_heads, count)

    def attend(running, kv_block, first_row):
        maxima, totals, accum = running
        scores, allowed, key_heads, value_heads, count = block_scores(kv_block, first_row)
        new_max = jnp.maximum(maxima, jnp.max(scores, axis=-1))
        weight = jnp.where(allowed, jnp.exp(scores - new_max[..., None]), 0.0)
        rescale = jnp.exp(maxima - new_max)
        totals = totals * rescale + jnp.sum(weight, axis=-1)
        accum = accum * rescale[..., None] + jnp.einsum(
            "rqhk,rkhd->rqhd",
            weight.astype(jnp.bfloat16),
            value_heads,
            preferred_element_type=jnp.float32,
        )
        return (new_max, totals, accum)

    start_state = (
        jnp.full((row_count, seg_len, HEADS), masked_score, jnp.float32),
        jnp.zeros((row_count, seg_len, HEADS), jnp.float32),
        jnp.zeros((row_count, seg_len, HEADS, HEAD), jnp.float32),
    )
    maxima, totals, accum = by_blocks(
        attend,
        start_state,
        (
            lax.all_gather(keys, "blk", axis=1, tiled=True),
            lax.all_gather(values, "blk", axis=1, tiled=True),
        ),
    )
    attn_heads = accum / totals[..., None]
    log_total = maxima + jnp.log(totals)
    attn_low = attn_heads.reshape(tok_count, features).astype(jnp.bfloat16)
    attention_projection = jnp.dot(
        attn_low, proj_weight, preferred_element_type=jnp.float32
    ) + proj_bias.astype(jnp.float32)
    middle_state = latent_float + selfattention_gate * attention_projection
    normed_mlp, inverse_mlp = layer_normalizer(middle_state)
    mlp_in = (normed_mlp * (1.0 + feedforward_scale) + feedforward_shift).astype(jnp.bfloat16)
    fc1_out = jnp.dot(mlp_in, fc1_weight, preferred_element_type=jnp.float32) + fc1_bias.astype(
        jnp.float32
    )
    gelu_out, gelu_pull = jax.vjp(gelu_tanh, fc1_out)
    act_low = gelu_out.astype(jnp.bfloat16)
    fc2_out = jnp.dot(act_low, fc2_weight, preferred_element_type=jnp.float32) + fc2_bias.astype(
        jnp.float32
    )
    block_out = (middle_state + feedforward_gate * fc2_out).astype(jnp.bfloat16)
    grad_f = grad_out.astype(jnp.float32).reshape(tok_count, features)
    grad_gate_mlp = grad_f * fc2_out
    grad_fc2 = (feedforward_gate * grad_f).astype(jnp.bfloat16)
    fc2_wgrad = jnp.einsum("tf,td->fd", act_low, grad_fc2, preferred_element_type=jnp.float32)
    fc2_bgrad = jnp.sum(grad_fc2.astype(jnp.float32), axis=0)
    grad_act = jnp.einsum("td,fd->tf", grad_fc2, fc2_weight, preferred_element_type=jnp.float32)
    grad_fc1 = gelu_pull(grad_act)[0].astype(jnp.bfloat16)
    fc1_wgrad = jnp.einsum("tc,tf->cf", mlp_in, grad_fc1, preferred_element_type=jnp.float32)
    fc1_bgrad = jnp.sum(grad_fc1.astype(jnp.float32), axis=0)
    grad_mlp_in = jnp.einsum("tf,cf->tc", grad_fc1, fc1_weight, preferred_element_type=jnp.float32)
    middle_state_gradient = grad_f + norm_backward_pass(
        grad_mlp_in * (1.0 + feedforward_scale), normed_mlp, inverse_mlp
    )
    selfattention_gate_gradient = middle_state_gradient * attention_projection
    projection_gradient = (selfattention_gate * middle_state_gradient).astype(jnp.bfloat16)
    proj_wgrad = jnp.einsum(
        "tc,td->cd", attn_low, projection_gradient, preferred_element_type=jnp.float32
    )
    proj_bgrad = jnp.sum(projection_gradient.astype(jnp.float32), axis=0)
    grad_attn = jnp.einsum(
        "td,cd->tc", projection_gradient, proj_weight, preferred_element_type=jnp.float32
    ).astype(jnp.bfloat16)
    grad_heads = grad_attn.reshape(row_count, seg_len, HEADS, HEAD)
    row_dot = jnp.sum(grad_heads.astype(jnp.float32) * attn_heads, axis=-1)

    def score_grads(kv_block, first_row):
        scores, allowed, key_heads, value_heads, count = block_scores(kv_block, first_row)
        probs = jnp.where(allowed, jnp.exp(scores - log_total[..., None]), 0.0)
        grad_probs = jnp.einsum(
            "rqhd,rkhd->rqhk", grad_heads, value_heads, preferred_element_type=jnp.float32
        )
        grad_scores = (probs * (grad_probs - row_dot[..., None])).astype(jnp.bfloat16)
        return (probs, grad_scores, key_heads, count)

    def collect(running, kv_block, first_row):
        query_grad, key_buffer = running
        probs, grad_scores, key_heads, count = score_grads(kv_block, first_row)
        value_part = jnp.einsum(
            "rqhk,rqhd->rkhd",
            probs.astype(jnp.bfloat16),
            grad_heads,
            preferred_element_type=jnp.float32,
        )
        query_grad = (
            query_grad
            + jnp.einsum(
                "rqhk,rkhd->rqhd", grad_scores, key_heads, preferred_element_type=jnp.float32
            )
            * inv_root
        )
        key_part = (
            jnp.einsum("rqhk,rqhd->rkhd", grad_scores, query, preferred_element_type=jnp.float32)
            * inv_root
        )
        joined = jnp.concatenate(
            [
                key_part.reshape(row_count, count, features),
                value_part.reshape(row_count, count, features),
            ],
            axis=-1,
        )
        key_buffer = lax.dynamic_update_slice_in_dim(key_buffer, joined, first_row, 1)
        return (query_grad, key_buffer)

    query_zero = jnp.zeros((row_count, seg_len, HEADS, HEAD), jnp.float32)
    back_state = (query_zero, jnp.zeros((row_count, row_len, 2 * features), jnp.float32))
    back_result = by_blocks(
        collect,
        back_state,
        (
            lax.all_gather(keys, "blk", axis=1, tiled=True),
            lax.all_gather(values, "blk", axis=1, tiled=True),
        ),
    )
    query_grad = back_result[0]
    key_value_grad = lax.psum_scatter(
        back_result[1].astype(jnp.bfloat16), "blk", scatter_dimension=1, tiled=True
    ).astype(jnp.float32)
    grad_qkv = jnp.concatenate(
        [query_grad.reshape(tok_count, features), key_value_grad.reshape(tok_count, 2 * features)],
        axis=-1,
    ).astype(jnp.bfloat16)
    qkv_wgrad = jnp.einsum(
        "tc,tk->ck", attention_input, grad_qkv, preferred_element_type=jnp.float32
    )
    grad_qkv_f = grad_qkv.astype(jnp.float32)
    qv_bgrad = jnp.stack(
        [jnp.sum(grad_qkv_f[:, :features], axis=0), jnp.sum(grad_qkv_f[:, 2 * features :], axis=0)]
    )
    attention_input_gradient = jnp.einsum(
        "tk,ck->tc", grad_qkv, qkv_weight, preferred_element_type=jnp.float32
    )
    latent_rows_gradient = middle_state_gradient + norm_backward_pass(
        attention_input_gradient * (1.0 + selfattention_scale),
        selfattention_normed_input,
        selfattention_inverse_norm,
    )
    grad_mod_tok = jnp.concatenate(
        [
            attention_input_gradient,
            attention_input_gradient * selfattention_normed_input,
            selfattention_gate_gradient,
            grad_mlp_in,
            grad_mlp_in * normed_mlp,
            grad_gate_mlp,
        ],
        axis=-1,
    )
    mod_part = jnp.einsum(
        "rsd,rsc->rdc",
        doc_pick,
        grad_mod_tok.reshape(row_count, seg_len, 6 * features),
        precision=highest,
    )
    mod_grad = lax.psum(mod_part.astype(jnp.bfloat16), "blk").reshape(
        row_count * DOCS, 6 * features
    )
    ada_wgrad = jnp.einsum("nc,nk->ck", cond_act, mod_grad, preferred_element_type=jnp.float32)
    ada_bgrad = jnp.sum(mod_grad.astype(jnp.float32), axis=0)
    grad_cond_act = jnp.einsum(
        "nk,ck->nc", mod_grad, ada_weight, preferred_element_type=jnp.float32
    )
    silu_pull = jax.vjp(jax.nn.silu, cond_f)[1]
    cond_grad = silu_pull(grad_cond_act.reshape(row_count, DOCS, features))[0]
    grad_parts = (
        ada_wgrad,
        ada_bgrad,
        qkv_wgrad,
        qv_bgrad,
        proj_wgrad,
        proj_bgrad,
        fc1_wgrad,
        fc1_bgrad,
        fc2_wgrad,
        fc2_bgrad,
    )
    return (
        block_out.reshape(row_count, seg_len, features),
        latent_rows_gradient.reshape(row_count, seg_len, features),
        cond_grad,
        grad_parts,
    )


def local(
    latents,
    conditions,
    doc_lengths,
    cotangent,
    ada_weight,
    ada_bias,
    qkv_weight,
    qv_bias,
    proj_weight,
    proj_bias,
    fc1_weight,
    fc1_bias,
    fc2_weight,
    fc2_bias,
):
    outs_list = []
    latent_list = []
    cond_list = []
    summed = None
    for micro_index in range(latents.shape[0]):
        weights = (
            lax.all_gather(ada_weight, "dp", axis=0, tiled=True),
            lax.all_gather(ada_bias, "dp", axis=0, tiled=True),
            lax.all_gather(qkv_weight, "dp", axis=0, tiled=True),
            lax.all_gather(qv_bias, "dp", axis=1, tiled=True),
            lax.all_gather(proj_weight, "dp", axis=0, tiled=True),
            lax.all_gather(proj_bias, "dp", axis=0, tiled=True),
            lax.all_gather(fc1_weight, "dp", axis=0, tiled=True),
            lax.all_gather(fc1_bias, "dp", axis=0, tiled=True),
            lax.all_gather(fc2_weight, "dp", axis=0, tiled=True),
            lax.all_gather(fc2_bias, "dp", axis=0, tiled=True),
        )
        block_out, latent_rows_gradient, cond_grad, grad_parts = micro_step(
            latents[micro_index],
            conditions[micro_index],
            doc_lengths[micro_index],
            cotangent[micro_index],
            weights,
        )
        outs_list.append(block_out)
        latent_list.append(latent_rows_gradient)
        cond_list.append(cond_grad)
        shard_part = (
            lax.psum_scatter(
                grad_parts[0].astype(jnp.bfloat16), "dp", scatter_dimension=0, tiled=True
            ).astype(jnp.float32),
            lax.psum_scatter(
                grad_parts[1].astype(jnp.bfloat16), "dp", scatter_dimension=0, tiled=True
            ).astype(jnp.float32),
            lax.psum_scatter(
                grad_parts[2].astype(jnp.bfloat16), "dp", scatter_dimension=0, tiled=True
            ).astype(jnp.float32),
            lax.psum_scatter(
                grad_parts[3].astype(jnp.bfloat16), "dp", scatter_dimension=1, tiled=True
            ).astype(jnp.float32),
            lax.psum_scatter(
                grad_parts[4].astype(jnp.bfloat16), "dp", scatter_dimension=0, tiled=True
            ).astype(jnp.float32),
            lax.psum_scatter(
                grad_parts[5].astype(jnp.bfloat16), "dp", scatter_dimension=0, tiled=True
            ).astype(jnp.float32),
            lax.psum_scatter(
                grad_parts[6].astype(jnp.bfloat16), "dp", scatter_dimension=0, tiled=True
            ).astype(jnp.float32),
            lax.psum_scatter(
                grad_parts[7].astype(jnp.bfloat16), "dp", scatter_dimension=0, tiled=True
            ).astype(jnp.float32),
            lax.psum_scatter(
                grad_parts[8].astype(jnp.bfloat16), "dp", scatter_dimension=0, tiled=True
            ).astype(jnp.float32),
            lax.psum_scatter(
                grad_parts[9].astype(jnp.bfloat16), "dp", scatter_dimension=0, tiled=True
            ).astype(jnp.float32),
        )
        if summed is None:
            summed = tuple(shard_part)
        else:
            summed = tuple((left + right for left, right in zip(summed, shard_part)))
    shared = (
        lax.psum(summed[2].astype(jnp.bfloat16), "blk").astype(jnp.float32),
        lax.psum(summed[3].astype(jnp.bfloat16), "blk").astype(jnp.float32),
        lax.psum(summed[4].astype(jnp.bfloat16), "blk").astype(jnp.float32),
        lax.psum(summed[5].astype(jnp.bfloat16), "blk").astype(jnp.float32),
        lax.psum(summed[6].astype(jnp.bfloat16), "blk").astype(jnp.float32),
        lax.psum(summed[7].astype(jnp.bfloat16), "blk").astype(jnp.float32),
        lax.psum(summed[8].astype(jnp.bfloat16), "blk").astype(jnp.float32),
        lax.psum(summed[9].astype(jnp.bfloat16), "blk").astype(jnp.float32),
    )
    return (
        jnp.stack(outs_list),
        jnp.stack(latent_list),
        jnp.stack(cond_list),
        summed[0],
        summed[1],
        shared[0],
        shared[1],
        shared[2],
        shared[3],
        shared[4],
        shared[5],
        shared[6],
        shared[7],
    )


def solution(mesh):
    in_specs = (
        P(None, "dp", "blk", None),
        P(None, "dp", None, None),
        P(None, "dp", None),
        P(None, "dp", "blk", None),
        P("dp", None),
        P("dp"),
        P("dp", None),
        P(None, "dp"),
        P("dp", None),
        P("dp"),
        P("dp", None),
        P("dp"),
        P("dp", None),
        P("dp"),
    )
    out_specs = (
        P(None, "dp", "blk", None),
        P(None, "dp", "blk", None),
        P(None, "dp", None, None),
        P("dp", None),
        P("dp"),
        P("dp", None),
        P(None, "dp"),
        P("dp", None),
        P("dp"),
        P("dp", None),
        P("dp"),
        P("dp", None),
        P("dp"),
    )
    return jax.shard_map(local, mesh=mesh, in_specs=in_specs, out_specs=out_specs, check_vma=False)
```

profile of v0, /device:TPU:0, one launch (start us, length us, event | category | flops | bytes accessed | tf_op | source)
XLA Modules:
  0.0 2229.7 jit_solution(11251366641131959854)
XLA Ops:
  11.9 9.5 all-gather.4
  22.1 16.1 all-reduce.15
  39.8 123.6 %all-gather.16.cloned.1.call-done = bf16[1152,6912]{1,0:T(8,128)(2,1)} async-done(((bf16[288,6912]{1,0:T(8,128)(2,1)}), bf16[1152,6912]{1,0:T(8,128)(2,1)}) %all-gather.16.cloned.1.call-update) | async-done | bytes 15925264 | tf_op jit(solution)/shard_map/all_gather | solution.py:344
  163.4 7.7 convolution_add_fusion
  174.8 74.5 %all-gather.18.cloned.1.call-done = bf16[1152,3456]{1,0:T(8,128)(2,1)} async-done(((bf16[288,3456]{1,0:T(8,128)(2,1)}), bf16[1152,3456]{1,0:T(8,128)(2,1)}) %all-gather.18.cloned.1.call-update) | async-done | bytes 7962640 | tf_op jit(solution)/shard_map/all_gather | solution.py:346
  249.3 4.6 fusion.270
  257.1 8.3 all-gather.5
  268.7 7.8 convolution_add_fusion.1
  279.9 77.5 %all-gather.24.cloned.1.call-done = bf16[4608,1152]{1,0:T(8,128)(2,1)} async-done(((bf16[1152,1152]{1,0:T(8,128)(2,1)}), bf16[4608,1152]{1,0:T(8,128)(2,1)}) %all-gather.24.cloned.1.call-update) | async-done | bytes 10616848 | tf_op jit(solution)/shard_map/all_gather | solution.py:352
  357.4 8.9 fusion.272
  366.3 24.8 %all-gather.32.cloned.1.call-done = bf16[1024,1152]{1,0:T(8,128)(2,1)} async-done(((bf16[128,1152]{1,0:T(8,128)(2,1)}), bf16[1024,1152]{1,0:T(8,128)(2,1)}) %all-gather.32.cloned.1.call-update) | async-done | bytes 2359312 | tf_op jit(solution)/shard_map/all_gather | solution.py:157
  394.2 29.8 %all-gather.30.cloned.1.call-done = bf16[1024,1152]{1,0:T(8,128)(2,1)} async-done(((bf16[128,1152]{1,0:T(8,128)(2,1)}), bf16[1024,1152]{1,0:T(8,128)(2,1)}) %all-gather.30.cloned.1.call-update) | async-done | bytes 2359312 | tf_op jit(solution)/shard_map/all_gather | solution.py:156
  423.9 4.3 copy.127
  428.2 13.0 while.57
  441.3 23.4 %all-gather.20.cloned.1.call-done = bf16[1152,1152]{1,0:T(8,128)(2,1)} async-done(((bf16[288,1152]{1,0:T(8,128)(2,1)}), bf16[1152,1152]{1,0:T(8,128)(2,1)}) %all-gather.20.cloned.1.call-update) | async-done | bytes 2654224 | tf_op jit(solution)/shard_map/all_gather | solution.py:348
  470.5 102.2 %all-gather.22.cloned.1.call-done = bf16[1152,4608]{1,0:T(8,128)(2,1)} async-done(((bf16[288,4608]{1,0:T(8,128)(2,1)}), bf16[1152,4608]{1,0:T(8,128)(2,1)}) %all-gather.22.cloned.1.call-update) | async-done | bytes 10616848 | tf_op jit(solution)/shard_map/all_gather | solution.py:350
  572.7 9.9 fusion.260
  597.0 25.4 %while.59 = (s32[]{:T(128)}, f32[1,128,16,72]{1,3,2,0:T(8,128)S(1)}, bf16[1,1024,2304]{1,2,0:T(8,128)(2,1)}, bf16[2,1,512,1152]{2,3,1,0:T(8,128)(2,1)}, s32[1,12...) while((s32[]{:T(128)}, ...), condition=%wide.region_36.37_spmd.clone, body=%wide.region_34.36_spmd.clone.sunk | while | flops 773969920 | bytes 71041912 | solution.py:54
  622.5 21.3 copy.145
  643.8 6.6 copy.156
  650.6 55.0 %reduce-scatter.45.cloned.1.call-done = bf16[128,2304]{1,0:T(8,128)(2,1)} async-done(((bf16[1024,2304]{1,0:T(8,128)(2,1)}), bf16[128,2304]{1,0:T(8,128)(2,1)}) %reduce-scatter.45.cloned.1.call-update) | async-done | bytes 589840
  708.9 7.7 fusion.251
  718.8 4.8 fusion.269
  725.5 8.9 fusion.271
  734.6 19.9 all-gather.28.cloned.1.call-done
  757.4 30.0 %all-gather.26.cloned.1.call-done = bf16[1024,1152]{1,0:T(8,128)(2,1)} async-done(((bf16[128,1152]{1,0:T(8,128)(2,1)}), bf16[1024,1152]{1,0:T(8,128)(2,1)}) %all-gather.26.cloned.1.call-update) | async-done | bytes 2359312 | tf_op jit(solution)/shard_map/all_gather | solution.py:156
  787.4 4.3 copy.124
  791.7 13.0 while.56
  805.5 3.6 fusion.263
  809.6 9.2 fusion.258
  833.3 25.2 %while.58 = (s32[]{:T(128)}, f32[1,128,16,72]{1,3,2,0:T(8,128)}, bf16[1,1024,2304]{1,2,0:T(8,128)(2,1)}, bf16[2,1,512,1152]{2,3,1,0:T(8,128)(2,1)}, s32[1,128]{1...) while((s32[]{:T(128)}, f32[1,128,16,72]{1,3,2,0:T(8,128)}, ...), condition=%wide.region_27.28_spmd.clone, body=%wide.region_25.27_spmd.clone.sunk | while | flops 773969920 | bytes 75760560 | solution.py:54
  858.5 21.4 copy.143
  879.9 6.6 copy.157
  894.1 46.6 %reduce-scatter.43.cloned.1.call-done = bf16[128,2304]{1,0:T(8,128)(2,1)} async-done(((bf16[1024,2304]{1,0:T(8,128)(2,1)}), bf16[128,2304]{1,0:T(8,128)(2,1)}) %reduce-scatter.43.cloned.1.call-update) | async-done | bytes 589840
  948.4 8.8 convolution_convert_fusion.2
  958.2 8.7 convolution_convert_fusion.3
  967.9 8.2 convolution_convert_fusion.4
  977.1 8.1 convolution_convert_fusion.5
  986.1 5.5 convolution_convert_fusion.6
  992.6 5.6 convolution_convert_fusion.7
  1001.2 16.8 all-reduce.14
  1020.0 7.7 convolution_add_fusion.6
  1031.2 21.5 reduce-scatter.31.cloned.1.call-done
  1055.1 6.1 fusion.183
  1070.2 9.4 reduce-scatter.47.cloned.1.call-done
  1081.4 105.8 %reduce-scatter.41.cloned.1.call-done = bf16[1152,1152]{1,0:T(8,128)(2,1)} async-done(((bf16[4608,1152]{1,0:T(8,128)(2,1)}), bf16[1152,1152]{1,0:T(8,128)(2,1)}) %reduce-scatter.41.cloned.1.call-update) | async-done | bytes 2654224 | tf_op jit(solution)/shard_map/reduce_scatter | solution.py:390
  1187.1 107.6 %reduce-scatter.39.cloned.1.call-done = bf16[1152,1152]{1,0:T(8,128)(2,1)} async-done(((bf16[4608,1152]{1,0:T(8,128)(2,1)}), bf16[1152,1152]{1,0:T(8,128)(2,1)}) %reduce-scatter.39.cloned.1.call-update) | async-done | bytes 2654224 | tf_op jit(solution)/shard_map/reduce_scatter | solution.py:390
  1294.7 4.7 add_convert_fusion
  1299.4 102.9 %reduce-scatter.37.cloned.1.call-done = bf16[288,4608]{1,0:T(8,128)(2,1)} async-done(((bf16[1152,4608]{1,0:T(8,128)(2,1)}), bf16[288,4608]{1,0:T(8,128)(2,1)}) %reduce-scatter.37.cloned.1.call-update) | async-done | bytes 2654224 | tf_op jit(solution)/shard_map/reduce_scatter | solution.py:384
  1402.3 107.7 %reduce-scatter.35.cloned.1.call-done = bf16[288,4608]{1,0:T(8,128)(2,1)} async-done(((bf16[1152,4608]{1,0:T(8,128)(2,1)}), bf16[288,4608]{1,0:T(8,128)(2,1)}) %reduce-scatter.35.cloned.1.call-update) | async-done | bytes 2654224 | tf_op jit(solution)/shard_map/reduce_scatter | solution.py:384
  1510.1 4.7 add_convert_fusion.1
  1514.8 82.1 %reduce-scatter.29.cloned.1.call-done = bf16[288,3456]{1,0:T(8,128)(2,1)} async-done(((bf16[1152,3456]{1,0:T(8,128)(2,1)}), bf16[288,3456]{1,0:T(8,128)(2,1)}) %reduce-scatter.29.cloned.1.call-update) | async-done | bytes 1990672 | tf_op jit(solution)/shard_map/reduce_scatter | solution.py:372
  1596.9 86.7 %reduce-scatter.27.cloned.1.call-done = bf16[288,3456]{1,0:T(8,128)(2,1)} async-done(((bf16[1152,3456]{1,0:T(8,128)(2,1)}), bf16[288,3456]{1,0:T(8,128)(2,1)}) %reduce-scatter.27.cloned.1.call-update) | async-done | bytes 1990672 | tf_op jit(solution)/shard_map/reduce_scatter | solution.py:372
  1683.6 3.9 add_convert_fusion.2
  1687.6 52.6 %all-reduce.19.cloned.1.call-done = (bf16[1,4,6912]{2,1,0:T(4,128)(2,1)}, bf16[1,4,6912]{2,1,0:T(4,128)(2,1)}, bf16[2,288]{1,0:T(2,128)(2,1)}, bf16[288]{0:T(512...) async-done(((bf16[1,4,6912]{2,1,0:T(4,128)(2,1)}, bf16[1,4,6912]{2,1,0:T(4,128)(2,1)}, bf16[2,288]{1,0:T(2,128)(2,1)}, bf16[288]{0:T(512)(128)(2,1)}, ...) | async-done | bytes 115216 | tf_op jit(solution)/shard_map/psum | solution.py:292
  1740.3 8.7 convolution_convert_fusion.1
  1749.7 8.0 convolution_convert_fusion
  1763.0 16.2 all-reduce.13
  1780.0 9.9 fusion.209
  1789.9 9.9 fusion.206
  1800.4 114.2 %all-reduce.21.cloned.1.call-done = (bf16[288,3456]{1,0:T(8,128)(2,1)}, bf16[288,1152]{1,0:T(8,128)(2,1)}, bf16[288,4608]{1,0:T(8,128)(2,1)}, bf16[1152,1152]{1,0:T(8,128)(2,1)}) async-done(((bf16[288,3456]{1,0:T(8,128)(2,1)}, bf16[288,1152]{1,0:T(8,128)(2,1)}, bf16[288,4608]{1,0:T(8,128)(2,1)}, bf16[1152,1152]{1,0:T(8,128)(2,1)}), (bf16[288,3456]{1,0:T(8,128)(2,1)}, bf16[288,1152]{1,0:T(8,128)(2,1)}, ...) | async-done | bytes 7962640 | tf_op jit(solution)/shard_map/psum | solution.py:402
  1925.9 139.0 %reduce-scatter.23.cloned.1.call-done = bf16[288,6912]{1,0:T(8,128)(2,1)} async-done(((bf16[1152,6912]{1,0:T(8,128)(2,1)}), bf16[288,6912]{1,0:T(8,128)(2,1)}) %reduce-scatter.23.cloned.1.call-update) | async-done | bytes 3981328 | tf_op jit(solution)/shard_map/reduce_scatter | solution.py:366
  2064.9 150.7 %reduce-scatter.25.cloned.1.call-done = bf16[288,6912]{1,0:T(8,128)(2,1)} async-done(((bf16[1152,6912]{1,0:T(8,128)(2,1)}), bf16[288,6912]{1,0:T(8,128)(2,1)}) %reduce-scatter.25.cloned.1.call-update) | async-done | bytes 3981328 | tf_op jit(solution)/shard_map/reduce_scatter | solution.py:366
  2215.6 7.4 convert_add_fusion
  (603 shorter events, 195.4 us)
Async XLA Ops:
  7.2 156.2 %all-gather.16.cloned.1.call-start = ((), (), s32[]{:S(2)}) async-start(), calls=%async_computation.14 | async-start | bytes 19906560 | tf_op jit(solution)/shard_map/all_gather | solution.py:344
  7.9 13.6 copy-start.134
  8.0 13.8 copy-start.123
  8.0 30.9 %copy-start.15 = (bf16[2,1,128,1152]{3,2,1,0:T(8,128)(2,1)S(1)}, bf16[2,1,128,1152]{3,2,1,0:T(8,128)(2,1)}, u32[]{:S(2)}) copy-start(bf16[2,1,128,1152]{3,2,1,0:T(8,128)(2,1)} %param.22) | copy-start | bytes 1769476
  8.0 155.4 %copy-start.72 = (bf16[2,1,4,1152]{3,2,1,0:T(4,128)(2,1)S(1)}, bf16[2,1,4,1152]{3,2,1,0:T(4,128)(2,1)}, u32[]{:S(2)}) copy-start(bf16[2,1,4,1152]{3,2,1,0:T(4,128)(2,1)} %param.23) | copy-start | bytes 55300
  8.0 241.4 %all-gather.18.cloned.1.call-start = ((), (), s32[]{:S(2)}) async-start(), calls=%async_computation.15 | async-start | bytes 9953280 | tf_op jit(solution)/shard_map/all_gather | solution.py:346
  8.7 348.6 %all-gather.24.cloned.1.call-start = ((), (), s32[]{:S(2)}) async-start(), calls=%async_computation.18 | async-start | bytes 13271040 | tf_op jit(solution)/shard_map/all_gather | solution.py:352
  9.5 381.6 %all-gather.32.cloned.1.call-start = ((), (), s32[]{:S(2)}) async-start(), calls=%async_computation.32 | async-start | bytes 2654208 | tf_op jit(solution)/shard_map/all_gather | solution.py:157
  11.7 159.4 %copy-start.91 = (s32[1,4]{1,0:T(1,128)}, s32[1,4]{1,0:T(1,128)S(1)}, u32[]{:S(2)}) copy-start(s32[1,4]{1,0:T(1,128)S(1)} %reduce_window_sum.18) | copy-start | bytes 52
  11.9 159.2 %copy-start.88 = (s32[1,4]{1,0:T(1,128)}, s32[1,4]{1,0:T(1,128)S(1)}, u32[]{:S(2)}) copy-start(s32[1,4]{1,0:T(1,128)S(1)} %reduce_window_sum.17) | copy-start | bytes 52
  38.1 133.0 %copy-start.70 = (f32[6912]{0:T(1024)}, f32[6912]{0:T(1024)S(1)}, u32[]{:S(2)}) copy-start(f32[6912]{0:T(1024)S(1)} %convert_element_type.474) | copy-start | bytes 82948
  38.2 215.8 %copy-start.83 = (f32[1152]{0:T(1024)}, f32[1152]{0:T(1024)S(1)}, u32[]{:S(2)}) copy-start(f32[1152]{0:T(1024)S(1)} %get-tuple-element.636) | copy-start | bytes 13828
  38.2 215.8 %copy-start.85 = (f32[1152]{0:T(1024)}, f32[1152]{0:T(1024)S(1)}, u32[]{:S(2)}) copy-start(f32[1152]{0:T(1024)S(1)} %get-tuple-element.637) | copy-start | bytes 13828
  38.8 132.3 %copy-start.75 = (s32[128]{0:T(128)}, s32[128]{0:T(128)S(1)}, u32[]{:S(2)}) copy-start(s32[128]{0:T(128)S(1)} %get-tuple-element.639) | copy-start | bytes 1540
  39.6 133.1 %copy-start.113 = (f32[128]{0:T(128)}, f32[128]{0:T(128)S(1)}, u32[]{:S(2)}) copy-start(f32[128]{0:T(128)S(1)} %get-tuple-element.814) | copy-start | bytes 1540
  39.8 132.9 %copy-start.125 = (f32[128]{0:T(128)}, f32[128]{0:T(128)S(1)}, u32[]{:S(2)}) copy-start(f32[128]{0:T(128)S(1)} %add_rsqrt_fusion.1) | copy-start | bytes 1540
  174.8 79.2 %copy-start.34 = (bf16[128,1152]{1,0:T(8,128)(2,1)}, bf16[128,1152]{1,0:T(8,128)(2,1)S(1)}, u32[]{:S(2)}) copy-start(bf16[128,1152]{1,0:T(8,128)(2,1)S(1)} %fusion.147) | copy-start | bytes 884740
  254.8 169.1 %all-gather.30.cloned.1.call-start = ((), (), s32[]{:S(2)}) async-start(), calls=%async_computation.31 | async-start | bytes 2654208 | tf_op jit(solution)/shard_map/all_gather | solution.py:156
  255.6 13.0 copy-start.71
  255.7 209.0 %all-gather.20.cloned.1.call-start = ((), (), s32[]{:S(2)}) async-start(), calls=%async_computation.16 | async-start | bytes 3317760 | tf_op jit(solution)/shard_map/all_gather | solution.py:348
  256.2 316.5 %all-gather.22.cloned.1.call-start = ((), (), s32[]{:S(2)}) async-start(), calls=%async_computation.17 | async-start | bytes 13271040 | tf_op jit(solution)/shard_map/all_gather | solution.py:350
  257.0 448.6 %reduce-scatter.45.cloned.1.call-start = ((), (), s32[]{:S(2)}) async-start(), calls=%async_computation.34 | async-start | bytes 5308416
  268.7 88.7 %copy-start.51 = (bf16[128,1152]{1,0:T(8,128)(2,1)}, bf16[128,1152]{1,0:T(8,128)(2,1)S(1)}, u32[]{:S(2)}) copy-start(bf16[128,1152]{1,0:T(8,128)(2,1)S(1)} %get-tuple-element.756) | copy-start | bytes 884740
  394.2 34.1 %copy-start.76 = (s32[128]{0:T(128)S(1)}, s32[128]{0:T(128)}, u32[]{:S(2)}) copy-start(s32[128]{0:T(128)} %copy-done.75) | copy-start | bytes 1540
  394.2 34.1 %copy-start.92 = (s32[1,4]{1,0:T(1,128)S(1)}, s32[1,4]{1,0:T(1,128)}, u32[]{:S(2)}) copy-start(s32[1,4]{1,0:T(1,128)} %copy-done.91) | copy-start | bytes 52
  441.2 23.5 %copy-start.58 = (f32[1,128,16,72]{1,3,2,0:T(8,128)}, f32[1,128,16,72]{1,3,2,0:T(8,128)S(1)}, u32[]{:S(2)}) copy-start(f32[1,128,16,72]{1,3,2,0:T(8,128)S(1)} %get-tuple-element.249) | copy-start | bytes 1769476
  441.3 27.1 %copy-start.43 = (bf16[1,128,16,72]{1,3,2,0:T(8,128)(2,1)}, bf16[1,128,16,72]{1,3,2,0:T(8,128)(2,1)S(1)}, u32[]{:S(2)}) copy-start(bf16[1,128,16,72]{1,3,2,0:T(8,128)(2,1)S(1)} %fusion.185) | copy-start | bytes 884740
  468.2 118.0 %copy-start.5 = (f32[128,1152]{1,0:T(8,128)}, f32[128,1152]{1,0:T(8,128)S(1)}, u32[]{:S(2)}) copy-start(f32[128,1152]{1,0:T(8,128)S(1)} %get-tuple-element.770) | copy-start | bytes 1769476
  470.5 112.1 %copy-start.61 = (bf16[128,1152]{1,0:T(8,128)(2,1)}, bf16[128,1152]{1,0:T(8,128)(2,1)S(1)}, u32[]{:S(2)}) copy-start(bf16[128,1152]{1,0:T(8,128)(2,1)S(1)} %fusion.168) | copy-start | bytes 884740
  470.5 112.1 %copy-start.100 = (f32[128]{0:T(128)S(1)}, f32[128]{0:T(128)}, u32[]{:S(2)}) copy-start(f32[128]{0:T(128)} %copy-done.99) | copy-start | bytes 1540
  470.5 112.1 %copy-start.109 = (f32[128]{0:T(128)S(1)}, f32[128]{0:T(128)}, u32[]{:S(2)}) copy-start(f32[128]{0:T(128)} %copy-done.108) | copy-start | bytes 1540
  589.3 136.2 %copy-start.49 = (bf16[128,1152]{1,0:T(8,128)(2,1)}, bf16[128,1152]{1,0:T(8,128)(2,1)S(1)}, u32[]{:S(2)}) copy-start(bf16[128,1152]{1,0:T(8,128)(2,1)S(1)} %get-tuple-element.754) | copy-start | bytes 884740
  622.5 21.3 copy-start.78
  650.4 58.5 %copy-start.16 = (bf16[2,1,128,1152]{3,2,1,0:T(8,128)(2,1)S(1)}, bf16[2,1,128,1152]{3,2,1,0:T(8,128)(2,1)}, u32[]{:S(2)}) copy-start(bf16[2,1,128,1152]{3,2,1,0:T(8,128)(2,1)} %param.22) | copy-start | bytes 1769476
  650.4 58.4 %copy-start.111 = (f32[128]{0:T(128)S(1)}, f32[128]{0:T(128)}, u32[]{:S(2)}) copy-start(f32[128]{0:T(128)} %get-tuple-element.815) | copy-start | bytes 1540
  650.5 58.4 %copy-start.114 = (f32[128]{0:T(128)S(1)}, f32[128]{0:T(128)}, u32[]{:S(2)}) copy-start(f32[128]{0:T(128)} %copy-done.113) | copy-start | bytes 1540
  650.5 58.4 %copy-start.126 = (f32[128]{0:T(128)S(1)}, f32[128]{0:T(128)}, u32[]{:S(2)}) copy-start(f32[128]{0:T(128)} %copy-done.125) | copy-start | bytes 1540
  650.5 104.1 %all-gather.28.cloned.1.call-start = ((), (), s32[]{:S(2)}) async-start(), calls=%async_computation.30 | async-start | bytes 2654208 | tf_op jit(solution)/shard_map/all_gather | solution.py:157
  650.6 66.1 %copy-start.41 = (bf16[1,128,16,72]{1,3,2,0:T(8,128)(2,1)}, bf16[1,128,16,72]{1,3,2,0:T(8,128)(2,1)S(1)}, u32[]{:S(2)}) copy-start(bf16[1,128,16,72]{1,3,2,0:T(8,128)(2,1)S(1)} %convert.49) | copy-start | bytes 884740
  724.4 63.0 %all-gather.26.cloned.1.call-start = ((), (), s32[]{:S(2)}) async-start(), calls=%async_computation.29 | async-start | bytes 2654208 | tf_op jit(solution)/shard_map/all_gather | solution.py:156
  725.2 215.5 %reduce-scatter.43.cloned.1.call-start = ((), (), s32[]{:S(2)}) async-start(), calls=%async_computation.33 | async-start | bytes 5308416
  757.4 34.3 %copy-start.81 = (s32[128]{0:T(128)S(1)}, s32[128]{0:T(128)}, u32[]{:S(2)}) copy-start(s32[128]{0:T(128)} %get-tuple-element.638) | copy-start | bytes 1540
  757.4 34.2 %copy-start.89 = (s32[1,4]{1,0:T(1,128)S(1)}, s32[1,4]{1,0:T(1,128)}, u32[]{:S(2)}) copy-start(s32[1,4]{1,0:T(1,128)} %copy-done.88) | copy-start | bytes 52
  791.7 13.8 copy-start.87
  805.5 13.4 slice-start.3
  809.1 13.4 copy-start.102
  809.3 13.1 copy-start.118
  886.5 113.6 %reduce-scatter.49.cloned.1.call-start = ((), (), s32[]{:S(2)}) async-start(), calls=%async_computation.36 | async-start | bytes 368640
  889.1 142.1 %reduce-scatter.33.cloned.1.call-start = ((), (), s32[]{:S(2)}) async-start(), calls=%async_computation.24 | async-start | bytes 3317760 | tf_op jit(solution)/shard_map/reduce_scatter | solution.py:378
  891.6 161.1 %reduce-scatter.31.cloned.1.call-start = ((), (), s32[]{:S(2)}) async-start(), calls=%async_computation.23 | async-start | bytes 3317760 | tf_op jit(solution)/shard_map/reduce_scatter | solution.py:378
  894.0 185.5 %reduce-scatter.47.cloned.1.call-start = ((), (), s32[]{:S(2)}) async-start(), calls=%async_computation.35 | async-start | bytes 368640
  946.4 45.3 %copy-start.18 = (bf16[1,128,2304]{1,2,0:T(8,128)(2,1)}, bf16[1,128,2304]{1,2,0:T(8,128)(2,1)S(1)}, u32[]{:S(2)}) copy-start(bf16[1,128,2304]{1,2,0:T(8,128)(2,1)S(1)} %copy.144) | copy-start | bytes 1769476
  947.9 239.2 %reduce-scatter.41.cloned.1.call-start = ((), (), s32[]{:S(2)}) async-start(), calls=%async_computation.28 | async-start | bytes 13271040 | tf_op jit(solution)/shard_map/reduce_scatter | solution.py:390
  957.3 337.5 %reduce-scatter.39.cloned.1.call-start = ((), (), s32[]{:S(2)}) async-start(), calls=%async_computation.27 | async-start | bytes 13271040 | tf_op jit(solution)/shard_map/reduce_scatter | solution.py:390
  966.9 435.4 %reduce-scatter.37.cloned.1.call-start = ((), (), s32[]{:S(2)}) async-start(), calls=%async_computation.26 | async-start | bytes 13271040 | tf_op jit(solution)/shard_map/reduce_scatter | solution.py:384
  976.1 534.0 %reduce-scatter.35.cloned.1.call-start = ((), (), s32[]{:S(2)}) async-start(), calls=%async_computation.25 | async-start | bytes 13271040 | tf_op jit(solution)/shard_map/reduce_scatter | solution.py:384
  985.2 611.7 %reduce-scatter.29.cloned.1.call-start = ((), (), s32[]{:S(2)}) async-start(), calls=%async_computation.22 | async-start | bytes 9953280 | tf_op jit(solution)/shard_map/reduce_scatter | solution.py:372
  991.7 692.0 %reduce-scatter.27.cloned.1.call-start = ((), (), s32[]{:S(2)}) async-start(), calls=%async_computation.21 | async-start | bytes 9953280 | tf_op jit(solution)/shard_map/reduce_scatter | solution.py:372
  998.2 29.4 %slice-start = ((s8[10616832]{0:T(1024)(128)(4,1)}), s8[2228224]{0:T(1024)(128)(4,1)S(1)}, s32[]{:S(2)}) async-start(s8[10616832]{0:T(1024)(128)(4,1)} %bitcast.705), calls=%async_computation.39 | async-start | bytes 4456448
  998.3 742.0 %all-reduce.19.cloned.1.call-start = ((), (), s32[]{:S(2)}) async-start(), calls=%async_computation.37 | async-start | bytes 236544 | tf_op jit(solution)/shard_map/psum | solution.py:292
  1081.1 833.5 %all-reduce.21.cloned.1.call-start = ((), (), s32[]{:S(2)}) async-start(), calls=%async_computation.38 | async-start | bytes 15925248 | tf_op jit(solution)/shard_map/psum | solution.py:402
  1687.5 52.7 %copy-start.74 = (bf16[2,1,4,1152]{3,2,1,0:T(4,128)(2,1)S(1)}, bf16[2,1,4,1152]{3,2,1,0:T(4,128)(2,1)}, u32[]{:S(2)}) copy-start(bf16[2,1,4,1152]{3,2,1,0:T(4,128)(2,1)} %param.23) | copy-start | bytes 55300
  1687.6 377.3 %reduce-scatter.23.cloned.1.call-start = ((), (), s32[]{:S(2)}) async-start(), calls=%async_computation.19 | async-start | bytes 19906560 | tf_op jit(solution)/shard_map/reduce_scatter | solution.py:366
  1749.0 466.6 %reduce-scatter.25.cloned.1.call-start = ((), (), s32[]{:S(2)}) async-start(), calls=%async_computation.20 | async-start | bytes 19906560 | tf_op jit(solution)/shard_map/reduce_scatter | solution.py:366
  (121 other events, 432.6 us)
Sparse Core Ops, SparseCore 0:
  9.9 153.4 all-gather.15
  165.2 84.0 all-gather.17
  251.2 106.1 all-gather.23
  359.5 31.6 all-gather.31
  393.2 30.7 all-gather.29
  425.6 39.0 all-gather.19
  466.5 106.1 all-gather.21
  650.6 54.9 reduce-scatter.44
  724.5 29.9 all-gather.27
  756.6 30.7 all-gather.25
  886.6 54.0 reduce-scatter.42
  943.4 22.5 reduce-scatter.48
  969.0 40.4 reduce-scatter.32
  1012.4 40.2 reduce-scatter.30
  1055.3 24.1 reduce-scatter.46
  1082.5 104.5 reduce-scatter.40
  1190.1 104.5 reduce-scatter.38
  1297.7 104.5 reduce-scatter.36
  1405.4 104.5 reduce-scatter.34
  1513.6 83.2 reduce-scatter.28
  1600.3 83.2 reduce-scatter.26
  1687.6 52.6 all-reduce.18
  1744.2 170.3 all-reduce.20
  1917.6 147.2 reduce-scatter.22
  2068.3 147.2 reduce-scatter.24
where the time goes:
time: 2240 us; the launch traced here: 2230 us
  waiting for transfers between devices  1690 us (75%)
  matrix products  232 us (10%)
  local copies, waits for them, and re-layouts  138 us (6%)
  other arithmetic  73 us (3%)
  blocking collectives  66.9 us (3%)
    reduce_scatter x2, waiting for transfers between devices, local(): lax.psum_scatter(grad_parts[0].astype(jnp.bfloat16), 'dp', scatter_dimens...  290 us
    reduce_scatter x2, waiting for transfers between devices, local(): lax.psum_scatter(grad_parts[8].astype(jnp.bfloat16), 'dp', scatter_dimens...  213 us
    reduce_scatter x2, waiting for transfers between devices, local(): lax.psum_scatter(grad_parts[6].astype(jnp.bfloat16), 'dp', scatter_dimens...  211 us
    reduce_scatter x2, waiting for transfers between devices, local(): lax.psum_scatter(grad_parts[2].astype(jnp.bfloat16), 'dp', scatter_dimens...  169 us
    all_gather x1, waiting for transfers between devices, local(): lax.all_gather(ada_weight, 'dp', axis=0, tiled=True)  124 us
    unnamed x29, waiting for transfers between devices  115 us
    psum x1, waiting for transfers between devices, local(): lax.psum(summed[2].astype(jnp.bfloat16), 'blk').astype(jnp.float32)  114 us
    all_gather x1, waiting for transfers between devices, local(): lax.all_gather(fc1_weight, 'dp', axis=0, tiled=True)  102 us
  transfers between devices with their start and end apart: 25, of which 23 were waited for; matrix products, arithmetic and copies ran while one was open for 11% of the time, Pallas kernels for 0%

commit v1 on v0

v1 whole, which is shorter than its diff:
```python
import functools

import jax
import jax.numpy as jnp
from jax import lax
from jax.experimental import pallas as pl
from jax.experimental.pallas import tpu as pltpu
from jax.sharding import PartitionSpec as P

HEADS = 16
HEAD = 72
DOCS = 4
NORM_EPS = 1e-06
MASKED = -1e30
LOG2E = 1.4426950408889634
SCALE = HEAD ** (-0.5)
VMEM_LIMIT = 56 * 1024 * 1024
HIGHEST = lax.Precision.HIGHEST
BF = jnp.bfloat16
F32 = jnp.float32


def normalize(values):
    center = jnp.mean(values, axis=-1, keepdims=True)
    centred = values - center
    inverse = lax.rsqrt(jnp.mean(centred * centred, axis=-1, keepdims=True) + NORM_EPS)
    return centred * inverse, inverse


def normalize_back(grad, normed, inverse):
    first = jnp.mean(grad, axis=-1, keepdims=True)
    second = jnp.mean(grad * normed, axis=-1, keepdims=True)
    return inverse * (grad - first - normed * second)


def dot_nn(a, b):
    return lax.dot_general(a, b, (((1,), (0,)), ((), ())), preferred_element_type=F32)


def dot_nt(a, b):
    return lax.dot_general(a, b, (((1,), (1,)), ((), ())), preferred_element_type=F32)


def dot_tn(a, b):
    return lax.dot_general(a, b, (((0,), (0,)), ((), ())), preferred_element_type=F32)


def swap(x, axis, mask):
    count = lax.axis_size(axis)
    return lax.ppermute(x, axis, [(i, i ^ mask) for i in range(count)])


def bits_of(low, high):
    out = []
    while low < high:
        out.append(low)
        low *= 2
    return out


def spread_dp(x):
    n = lax.axis_size("dp")
    blocks = {0: x}
    if n == 4:
        cut = x.shape[0] // 2
        blocks[1] = swap(x, "dp", 1)
        blocks[2] = swap(x, "dp", 2)
        upper = swap(blocks[1][:cut], "dp", 2)
        lower = swap(blocks[2][cut:], "dp", 1)
        blocks[3] = jnp.concatenate([upper, lower], axis=0)
        return blocks
    for bit in bits_of(1, n):
        for mask in list(blocks):
            blocks[mask | bit] = swap(blocks[mask], "dp", bit)
    return blocks


def collect_dp(blocks):
    n = lax.axis_size("dp")

    def add(a, b):
        return (a.astype(F32) + b.astype(F32)).astype(BF)

    if n == 4:
        cut = blocks[3].shape[0] // 2
        r1 = swap(blocks[3][:cut], "dp", 1)
        r2 = swap(blocks[3][cut:], "dp", 2)
        b2 = jnp.concatenate([add(blocks[2][:cut], r1), blocks[2][cut:]], axis=0)
        b1 = jnp.concatenate([blocks[1][:cut], add(blocks[1][cut:], r2)], axis=0)
        s1 = swap(b1, "dp", 1)
        s2 = swap(b2, "dp", 2)
        return blocks[0].astype(F32) + s1.astype(F32) + s2.astype(F32)
    blocks = dict(blocks)
    for bit in reversed(bits_of(1, n)):
        for mask in [m for m in blocks if m & bit]:
            blocks[mask ^ bit] = add(blocks[mask ^ bit], swap(blocks.pop(mask), "dp", bit))
    return blocks[0].astype(F32)


def direct(blocks, axis):
    return {m: (b if m == 0 else swap(b, axis, m)) for m, b in blocks.items()}


def spread_group(x, group):
    blocks = {0: x}
    for bit in bits_of(2, group):
        for mask in list(blocks):
            blocks[mask | bit] = swap(blocks[mask], "blk", bit)
    for mask in list(blocks):
        blocks[mask | 1] = swap(blocks[mask], "blk", 1)
    return blocks


def collect_group(blocks, group):
    blocks = dict(blocks)
    for mask in [m for m in blocks if m & 1]:
        got = swap(blocks.pop(mask), "blk", 1)
        blocks[mask ^ 1] = (blocks[mask ^ 1].astype(F32) + got.astype(F32)).astype(BF)
    for bit in reversed(bits_of(2, group)):
        for mask in [m for m in blocks if m & bit]:
            got = swap(blocks.pop(mask), "blk", bit)
            total = blocks[mask ^ bit].astype(F32) + got.astype(F32)
            blocks[mask ^ bit] = total if bit == 2 and group > 2 else total.astype(BF)
    return blocks[0].astype(F32)


def sum_line(x):
    count = lax.axis_size("blk")
    chips = count // 2
    place = lax.axis_index("blk") // 2
    mid = chips // 2

    def both(pairs):
        return [(2 * a + c, 2 * b + c) for a, b in pairs for c in range(2)]

    def add(a, b):
        return (a.astype(F32) + b.astype(F32)).astype(BF)

    for s in range(mid - 1):
        x = add(x, lax.ppermute(x, "blk", both([(s, s + 1), (chips - 1 - s, chips - 2 - s)])))
    x = add(x, lax.ppermute(x, "blk", both([(mid - 1, mid), (mid, mid - 1)])))
    for s in range(mid - 1):
        low, high = mid - 1 - s, mid + s
        got = lax.ppermute(x, "blk", both([(low, low - 1), (high, high + 1)]))
        x = jnp.where((place == low - 1) | (place == high + 1), got, x)
    return x


def in_order(blocks, mine):
    stack = jnp.stack([blocks[m] for m in range(len(blocks))])
    return [lax.dynamic_index_in_dim(stack, k ^ mine, 0, False) for k in range(len(blocks))]


def rows_in_order(blocks, mine):
    size = blocks[0].shape[0]
    out = jnp.zeros((size * len(blocks),) + blocks[0].shape[1:], blocks[0].dtype)
    for m in range(len(blocks)):
        out = lax.dynamic_update_slice_in_dim(out, blocks[m], (m ^ mine) * size, 0)
    return out


def allowed_mask(dock_ref, docq_ref, width):
    keys = dock_ref[...]
    keys = jnp.concatenate([keys] * (width // keys.shape[1]), axis=1)
    return keys == docq_ref[...]


def attend_kernel(hpd, block, qkv_ref, docq_ref, dock_ref, out_ref, outt_ref, peak_ref, vt_ref):
    i = pl.program_id(0)
    width = hpd * HEAD
    rows = pl.ds(pl.multiple_of(i * block, block), block)

    @pl.when(i == 0)
    def _():
        for h in range(hpd):
            v = qkv_ref[:, 2 * width + h * HEAD : 2 * width + (h + 1) * HEAD]
            vt_ref[h] = v.astype(F32).T.astype(BF)

    allowed = allowed_mask(dock_ref, docq_ref, block)
    outs, peaks = [], []
    for h in range(hpd):
        q = qkv_ref[rows, h * HEAD : (h + 1) * HEAD]
        k = qkv_ref[:, width + h * HEAD : width + (h + 1) * HEAD]
        scores = jnp.where(allowed, dot_nt(k, q), MASKED)
        peak = jnp.max(scores, axis=0, keepdims=True)
        weight = jnp.exp2((scores - peak) * (SCALE * LOG2E))
        total = jnp.sum(weight, axis=0, keepdims=True)
        outs.append(dot_nn(vt_ref[h], weight.astype(BF)) / total)
        peaks.append(peak + jnp.log(total) * (1.0 / SCALE))
    out = jnp.concatenate(outs, axis=0)
    outt_ref[...] = out
    out_ref[...] = out.T.astype(BF)
    peaks.append(jnp.zeros((8 - hpd, block), F32))
    peak_ref[...] = jnp.concatenate(peaks, axis=0)


def attend_back_kernel(
    hpd, block, steps, qkv_ref, do_ref, outt_ref, peak_ref, docq_ref, dock_ref, grad_ref, kt_ref, dk_ref, dv_ref
):
    i = pl.program_id(0)
    width = hpd * HEAD
    rows = pl.ds(pl.multiple_of(i * block, block), block)

    @pl.when(i == 0)
    def _():
        for h in range(hpd):
            k = qkv_ref[:, width + h * HEAD : width + (h + 1) * HEAD]
            kt_ref[h] = k.astype(F32).T.astype(BF)
        dk_ref[...] = jnp.zeros_like(dk_ref)
        dv_ref[...] = jnp.zeros_like(dv_ref)

    allowed = allowed_mask(dock_ref, docq_ref, block)
    dots = do_ref[rows, :].astype(F32).T * outt_ref[...]
    dqs = []
    for h in range(hpd):
        part = slice(h * HEAD, (h + 1) * HEAD)
        q = qkv_ref[rows, part]
        k = qkv_ref[:, width + h * HEAD : width + (h + 1) * HEAD]
        v = qkv_ref[:, 2 * width + h * HEAD : 2 * width + (h + 1) * HEAD]
        do = do_ref[rows, part]
        row_dot = jnp.sum(dots[part], axis=0, keepdims=True)
        scores = jnp.where(allowed, dot_nt(k, q), MASKED)
        probs = jnp.exp2((scores - peak_ref[h : h + 1, :]) * (SCALE * LOG2E))
        grad_scores = (probs * (dot_nt(v, do) - row_dot)).astype(BF)
        dv_ref[h] += dot_nn(probs.astype(BF), do)
        dk_ref[h] += dot_nn(grad_scores, q)
        dqs.append(dot_nn(kt_ref[h], grad_scores))
    grad_ref[rows, :width] = (jnp.concatenate(dqs, axis=0) * SCALE).T.astype(BF)

    @pl.when(i == steps - 1)
    def _():
        dk = jnp.concatenate([dk_ref[h] for h in range(hpd)], axis=1) * SCALE
        dv = jnp.concatenate([dv_ref[h] for h in range(hpd)], axis=1)
        grad_ref[:, width : 2 * width] = dk.astype(BF)
        grad_ref[:, 2 * width :] = dv.astype(BF)


def params():
    return pltpu.CompilerParams(vmem_limit_bytes=VMEM_LIMIT, dimension_semantics=("arbitrary",))


def attend(qkv, docq, dock, hpd):
    length, width = qkv.shape[0], hpd * HEAD
    block = min(256, length)
    cost = pl.CostEstimate(
        flops=4 * length * length * hpd * 128, bytes_accessed=16 * length * width, transcendentals=length * length * hpd
    )
    return pl.pallas_call(
        functools.partial(attend_kernel, hpd, block),
        grid=(length // block,),
        in_specs=[
            pl.BlockSpec((length, 3 * width), lambda i: (0, 0)),
            pl.BlockSpec((1, block), lambda i: (0, i)),
            pl.BlockSpec((length, 128), lambda i: (0, 0)),
        ],
        out_specs=[
            pl.BlockSpec((block, width), lambda i: (i, 0)),
            pl.BlockSpec((width, block), lambda i: (0, i)),
            pl.BlockSpec((8, block), lambda i: (0, i)),
        ],
        out_shape=[
            jax.ShapeDtypeStruct((length, width), BF),
            jax.ShapeDtypeStruct((width, length), F32),
            jax.ShapeDtypeStruct((8, length), F32),
        ],
        scratch_shapes=[pltpu.VMEM((hpd, HEAD, length), BF)],
        compiler_params=params(),
        cost_estimate=cost,
        name="attend",
    )(qkv, docq, dock)


def attend_back(qkv, grad_out, outt, peak, docq, dock, hpd):
    length, width = qkv.shape[0], hpd * HEAD
    block = min(256, length)
    steps = length // block
    cost = pl.CostEstimate(
        flops=10 * length * length * hpd * 128, bytes_accessed=20 * length * width, transcendentals=length * length * hpd
    )
    return pl.pallas_call(
        functools.partial(attend_back_kernel, hpd, block, steps),
        grid=(steps,),
        in_specs=[
            pl.BlockSpec((length, 3 * width), lambda i: (0, 0)),
            pl.BlockSpec((length, width), lambda i: (0, 0)),
            pl.BlockSpec((width, block), lambda i: (0, i)),
            pl.BlockSpec((8, block), lambda i: (0, i)),
            pl.BlockSpec((1, block), lambda i: (0, i)),
            pl.BlockSpec((length, 128), lambda i: (0, 0)),
        ],
        out_specs=pl.BlockSpec((length, 3 * width), lambda i: (0, 0)),
        out_shape=jax.ShapeDtypeStruct((length, 3 * width), BF),
        scratch_shapes=[
            pltpu.VMEM((hpd, HEAD, length), BF),
            pltpu.VMEM((hpd, length, HEAD), F32),
            pltpu.VMEM((hpd, length, HEAD), F32),
        ],
        compiler_params=params(),
        cost_estimate=cost,
        name="attend_back",
    )(qkv, grad_out, outt, peak, docq, dock)


def mlp_kernel(x_ref, g_ref, w1_ref, b1_ref, w2_ref, act_ref, gf1_ref, part_ref, back_ref):
    u = dot_nn(x_ref[...], w1_ref[...]) + b1_ref[...]
    root = 0.7978845608028654
    squared = u * u
    t = jnp.tanh(root * u * (1.0 + 0.044715 * squared))
    act = (0.5 * u * (1.0 + t)).astype(BF)
    slope = 0.5 * (1.0 + t) + 0.5 * u * (1.0 - t * t) * (root * (1.0 + 3 * 0.044715 * squared))
    gf1 = (dot_nt(g_ref[...], w2_ref[...]) * slope).astype(BF)
    act_ref[...] = act
    gf1_ref[...] = gf1
    back_ref[...] = dot_nt(gf1, w1_ref[...]).astype(BF)
    part_ref[...] = dot_nn(act, w2_ref[...]).astype(BF)


def mlp(x, g, w1, b1, w2):
    tokens, features = x.shape
    hidden = w1.shape[1]
    block = 256
    cost = pl.CostEstimate(
        flops=8 * tokens * features * hidden, bytes_accessed=8 * tokens * features, transcendentals=tokens * hidden
    )
    return pl.pallas_call(
        mlp_kernel,
        grid=(tokens // block,),
        in_specs=[
            pl.BlockSpec((block, features), lambda i: (i, 0)),
            pl.BlockSpec((block, features), lambda i: (i, 0)),
            pl.BlockSpec((features, hidden), lambda i: (0, 0)),
            pl.BlockSpec((1, hidden), lambda i: (0, 0)),
            pl.BlockSpec((hidden, features), lambda i: (0, 0)),
        ],
        out_specs=[
            pl.BlockSpec((block, hidden), lambda i: (i, 0)),
            pl.BlockSpec((block, hidden), lambda i: (i, 0)),
            pl.BlockSpec((block, features), lambda i: (i, 0)),
            pl.BlockSpec((block, features), lambda i: (i, 0)),
        ],
        out_shape=[
            jax.ShapeDtypeStruct((tokens, hidden), BF),
            jax.ShapeDtypeStruct((tokens, hidden), BF),
            jax.ShapeDtypeStruct((tokens, features), BF),
            jax.ShapeDtypeStruct((tokens, features), BF),
        ],
        compiler_params=params(),
        cost_estimate=cost,
        name="mlp",
    )(x, g, w1, b1, w2)


def place_qkv_kernel(group, rows, parts_ref, mine_ref, out_ref, bias_ref):
    mine = mine_ref[0]
    size = parts_ref.shape[2] // 3
    for j in range(group):
        got = parts_ref[j ^ mine].astype(F32)
        for p in range(3):
            at = p * group * size + j * size
            out_ref[:, at : at + size] = got[:rows, p * size : (p + 1) * size]
            bias_ref[:, at : at + size] = got[rows : rows + 8, p * size : (p + 1) * size]


def place_qkv(parts, mine, rows):
    group, total, width = parts.shape
    return pl.pallas_call(
        functools.partial(place_qkv_kernel, group, rows),
        in_specs=[pl.BlockSpec(memory_space=pltpu.VMEM), pl.BlockSpec(memory_space=pltpu.SMEM)],
        out_specs=[pl.BlockSpec(memory_space=pltpu.VMEM), pl.BlockSpec(memory_space=pltpu.VMEM)],
        out_shape=[
            jax.ShapeDtypeStruct((rows, group * width), F32),
            jax.ShapeDtypeStruct((8, group * width), F32),
        ],
        compiler_params=pltpu.CompilerParams(vmem_limit_bytes=VMEM_LIMIT),
        name="place_qkv",
    )(parts, jnp.reshape(mine, (1,)).astype(jnp.int32))


def local(
    latents,
    conditions,
    doc_lengths,
    cotangent,
    ada_weight,
    ada_bias,
    qkv_weight,
    qv_bias,
    proj_weight,
    proj_bias,
    fc1_weight,
    fc1_bias,
    fc2_weight,
    fc2_bias,
):
    n_dp, n_blk = lax.axis_size("dp"), lax.axis_size("blk")
    dp, blk = lax.axis_index("dp"), lax.axis_index("blk")
    half = n_blk // 2
    group = half
    core, micro, place = blk % 2, blk // half, blk % half
    seg, features = latents.shape[2], latents.shape[3]
    hidden = fc1_weight.shape[1]
    dshard = features // n_dp
    hpd = HEADS // group
    width = hpd * HEAD
    fslice = hidden // (2 * n_dp)
    hshard = dshard // 2

    def pick(x, index):
        return lax.dynamic_index_in_dim(x, index, 0, False)

    def rows_of(x, start, size):
        return lax.dynamic_slice_in_dim(x, start, size, 0)

    def take_row(x):
        other = swap(pick(x, 1 - micro)[0], "blk", half)
        return jnp.concatenate([pick(x, micro)[0], other], axis=0)

    latent = take_row(latents).astype(F32)
    cot = take_row(cotangent).astype(F32)

    ends = jnp.cumsum(pick(doc_lengths, micro)[0])

    def docs_at(index):
        spot = jnp.arange(seg, dtype=jnp.int32)
        spots = jnp.concatenate([index * seg + spot, (index ^ half) * seg + spot])
        return jnp.sum((spots[:, None] >= ends[None, :]).astype(jnp.int32), axis=1)

    cond = conditions[:, 0].astype(F32)
    cond_act = jax.nn.silu(cond).astype(BF).reshape(2 * DOCS, features)
    cond_from = direct({m: cond_act for m in range(n_dp)}, "dp")
    biases = jnp.concatenate([ada_bias, proj_bias, fc2_bias, qv_bias[0], qv_bias[1]])[None]
    biases = in_order(direct({m: biases for m in range(n_dp)}, "dp"), dp)
    cuts = [0, ada_bias.shape[0], dshard, dshard, dshard, dshard]
    cuts = [sum(cuts[: i + 1]) for i in range(len(cuts))]
    ada_b, proj_b, fc2_b, q_b, v_b = (
        jnp.concatenate([b[:, cuts[i] : cuts[i + 1]] for b in biases], axis=1).astype(F32) for i in range(5)
    )
    my_cond = {
        m: lax.dynamic_slice(c, (0, dp * dshard), (2 * DOCS, dshard)) for m, c in cond_from.items()
    }
    cond_cols = jnp.concatenate([my_cond[m] for m in range(n_dp)], axis=0)
    cond_rows = jnp.concatenate([rows_of(my_cond[m], micro * DOCS, DOCS) for m in range(n_dp)], axis=0)
    mod_part = dot_nn(cond_rows, ada_weight)
    mod_from = direct({m: mod_part[m * DOCS : (m + 1) * DOCS] for m in range(n_dp)}, "dp")
    mod_all = sum(mod_from[m] for m in range(n_dp)) + ada_b

    my_docs = docs_at(blk)
    doc_pick = (my_docs[:, None] == jnp.arange(DOCS, dtype=jnp.int32)[None, :]).astype(F32)

    def mod(k):
        piece = mod_all[:, k * features : (k + 1) * features]
        return sum(doc_pick[:, d : d + 1] * piece[d : d + 1] for d in range(DOCS))

    qkv_cols = jnp.concatenate(
        [
            lax.dynamic_slice(qkv_weight, (0, p * features + place * width), (dshard, width))
            for p in range(3)
        ],
        axis=1,
    )
    qkv_w = rows_in_order(spread_dp(qkv_cols), dp)
    q_bias = lax.dynamic_slice(q_b, (0, place * width), (1, width))
    v_bias = lax.dynamic_slice(v_b, (0, place * width), (1, width))
    qkv_bias = jnp.concatenate([q_bias, jnp.zeros_like(q_bias), v_bias], axis=1)

    proj_mine = spread_dp(rows_of(proj_weight, core * hshard, hshard))
    proj_w = jnp.zeros((n_dp, 2, hshard, features), BF)
    for m, b in proj_mine.items():
        pair = swap(b, "blk", 1)
        proj_w = lax.dynamic_update_slice(proj_w, b[None, None], (dp ^ m, core, 0, 0))
        proj_w = lax.dynamic_update_slice(proj_w, pair[None, None], (dp ^ m, 1 - core, 0, 0))
    proj_w = proj_w.reshape(features, features)
    proj_x = jnp.concatenate([rows_of(proj_w, (place ^ m) * width, width) for m in range(group)], axis=0)

    fc1_w = rows_in_order(
        direct(
            {
                m: lax.dynamic_slice(fc1_weight, (0, ((dp ^ m) * 2 + core) * fslice), (dshard, fslice))
                for m in range(n_dp)
            },
            "dp",
        ),
        dp,
    )
    fc1_b = lax.dynamic_slice(fc1_bias, (core * fslice,), (fslice,)).astype(F32)[None]
    fc2_w = rows_of(fc2_weight, core * fslice, fslice)

    normed, inverse = normalize(latent)
    attn_in = (normed * (1.0 + mod(1)) + mod(0)).astype(BF)
    grad_fc2 = (mod(5) * cot).astype(BF)
    row_in = spread_group(attn_in, group)
    row_in = jnp.concatenate([row_in[m] for m in range(group)], axis=0)
    row_docs = jnp.concatenate([docs_at(blk ^ m) for m in range(group)])
    docq = row_docs[None, :]
    dock = jnp.broadcast_to(row_docs[:, None], (row_docs.shape[0], 128))
    qkv = (dot_nn(row_in, qkv_w) + qkv_bias).astype(BF)
    out, outt, peak = attend(qkv, docq, dock, hpd)
    tokens = 2 * seg
    got = direct({m: out[m * tokens : (m + 1) * tokens] for m in range(group)}, "blk")
    attn_low = jnp.concatenate([got[m] for m in range(group)], axis=1)
    attn_proj = dot_nn(attn_low, proj_x) + proj_b
    mid = latent + mod(2) * attn_proj

    mid_normed, mid_inverse = normalize(mid)
    mlp_in = (mid_normed * (1.0 + mod(4)) + mod(3)).astype(BF)

    def spread_tokens(x):
        blocks = spread_dp(x)
        mine = jnp.concatenate([blocks[m] for m in range(n_dp)], axis=0)
        return jnp.concatenate([mine, swap(mine, "blk", 1)], axis=0)

    def collect_tokens(x):
        count = x.shape[0] // 2
        mine = x[:count].astype(F32) + swap(x[count:], "blk", 1).astype(F32)
        mine = mine.astype(BF)
        return collect_dp({m: mine[m * tokens : (m + 1) * tokens] for m in range(n_dp)})

    all_grad = spread_tokens(grad_fc2)
    all_in = spread_tokens(mlp_in)
    act, grad_fc1, fc2_part, mlp_back = mlp(all_in, all_grad, fc1_w, fc1_b, fc2_w)
    grad_mlp_in = collect_tokens(mlp_back)

    grad_mid = cot + normalize_back(grad_mlp_in * (1.0 + mod(4)), mid_normed, mid_inverse)
    grad_proj = (mod(2) * grad_mid).astype(BF)
    grad_attn = direct(
        {m: dot_nt(grad_proj, proj_x[m * width : (m + 1) * width]).astype(BF) for m in range(group)}, "blk"
    )
    grad_attn = jnp.concatenate([grad_attn[m] for m in range(group)], axis=0)
    grad_qkv = attend_back(qkv, grad_attn, outt, peak, docq, dock, hpd)
    attn_back = dot_nt(grad_qkv, qkv_w).astype(BF)
    grad_attn_in = collect_group({m: attn_back[m * tokens : (m + 1) * tokens] for m in range(group)}, group)
    latent_grad = grad_mid + normalize_back(grad_attn_in * (1.0 + mod(1)), normed, inverse)

    fc2_out = collect_tokens(fc2_part) + fc2_b
    block_out = (mid + mod(5) * fc2_out).astype(BF)

    def hand_back(x):
        other = swap(x[seg:].astype(BF), "blk", half).astype(x.dtype)
        both = jnp.stack([x[:seg], other])
        return jnp.where(micro == 0, both, both[::-1])[:, None]

    block_out = hand_back(block_out)
    latent_grad = hand_back(latent_grad)

    def extra_rows(rows, count=16):
        return jnp.pad(rows, ((0, count - rows.shape[0]), (0, 0))).astype(BF)

    fc2_bsum = jnp.sum(all_grad.astype(F32), axis=0, keepdims=True)
    fc1_bsum = jnp.sum(grad_fc1.astype(F32), axis=0, keepdims=True)
    both_b = jnp.concatenate([fc2_bsum, jnp.pad(fc1_bsum, ((0, 0), (0, features - fslice)))], axis=0)
    fc2_g = jnp.concatenate([dot_tn(act, all_grad).astype(BF), extra_rows(both_b)], axis=0)
    fc2_g = sum_line(fc2_g)

    fc1_g = dot_tn(all_in, grad_fc1).astype(BF).reshape(n_dp, dshard, fslice)
    fc1_g = direct({m: pick(fc1_g, dp ^ m) for m in range(n_dp)}, "dp")
    fc1_g = sum_line(jnp.concatenate([fc1_g[m] for m in range(n_dp)], axis=0))

    def core_pair(x):
        got = swap(x, "blk", 1)
        return jnp.where(core == 0, x, got), jnp.where(core == 0, got, x)

    fc2_lo, fc2_hi = core_pair(fc2_g)
    fc2_wgrad = jnp.concatenate([fc2_lo[:fslice], fc2_hi[:fslice]], axis=0).astype(F32)
    fc2_bgrad = lax.dynamic_slice(fc2_lo[fslice].astype(F32), (dp * dshard,), (dshard,))
    fc1_bgrad = jnp.concatenate([fc2_lo[fslice + 1, :fslice], fc2_hi[fslice + 1, :fslice]]).astype(F32)
    fc1_lo, fc1_hi = core_pair(fc1_g)
    fc1_wgrad = jnp.zeros((dshard, hidden), F32)
    for m in range(n_dp):
        rows = slice(m * dshard, (m + 1) * dshard)
        piece = jnp.concatenate([fc1_lo[rows], fc1_hi[rows]], axis=1).astype(F32)
        fc1_wgrad = lax.dynamic_update_slice(fc1_wgrad, piece, (0, (dp ^ m) * 2 * fslice))

    proj_g = dot_tn(attn_low, grad_proj).astype(BF).reshape(group, width, features)
    proj_g = jnp.concatenate([pick(proj_g, k ^ place) for k in range(group)], axis=0)
    proj_bsum = extra_rows(jnp.sum(grad_proj.astype(F32), axis=0, keepdims=True))
    proj_g = proj_g.reshape(n_dp, 2, hshard, features)
    proj_g = jnp.concatenate(
        [proj_g, jnp.broadcast_to(proj_bsum[None, None], (n_dp, 2) + proj_bsum.shape)], axis=2
    )
    keep = lax.dynamic_index_in_dim(proj_g, core, 1, False)
    send = lax.dynamic_index_in_dim(proj_g, 1 - core, 1, False)
    proj_g = (keep.astype(F32) + swap(send, "blk", 1).astype(F32)).astype(BF)
    proj_g = collect_dp({m: pick(proj_g, dp ^ m) for m in range(n_dp)}).astype(BF)
    proj_g = sum_line(proj_g)
    proj_lo, proj_hi = core_pair(proj_g)
    proj_wgrad = jnp.concatenate([proj_lo[:hshard], proj_hi[:hshard]], axis=0).astype(F32)
    proj_bgrad = lax.dynamic_slice(proj_lo[hshard].astype(F32), (dp * dshard,), (dshard,))

    qkv_bsum = extra_rows(jnp.sum(grad_qkv.astype(F32), axis=0, keepdims=True))
    qkv_g = dot_tn(row_in, grad_qkv).astype(BF).reshape(n_dp, dshard, 3 * width)
    qkv_g = collect_dp(
        {m: jnp.concatenate([pick(qkv_g, dp ^ m), qkv_bsum], axis=0) for m in range(n_dp)}
    ).astype(BF)
    qkv_g = (qkv_g.astype(F32) + swap(qkv_g, "blk", half).astype(F32)).astype(BF)
    qkv_g = spread_group(qkv_g, group)
    qkv_wgrad, qkv_rows = place_qkv(jnp.stack([qkv_g[m] for m in range(group)]), place, dshard)
    qv_bgrad = jnp.stack(
        [
            lax.dynamic_slice(qkv_rows[0], (p * features + dp * dshard,), (dshard,))
            for p in (0, 2)
        ]
    )

    grad_tok = jnp.concatenate(
        [
            grad_attn_in,
            grad_attn_in * normed,
            grad_mid * attn_proj,
            grad_mlp_in,
            grad_mlp_in * mid_normed,
            cot * fc2_out,
        ],
        axis=1,
    )
    grad_mod = lax.dot_general(
        doc_pick, grad_tok, (((0,), (0,)), ((), ())), precision=HIGHEST, preferred_element_type=F32
    )
    for bit in bits_of(1, group):
        grad_mod = grad_mod + swap(grad_mod, "blk", bit)
    grad_mod = grad_mod.astype(BF)
    other = swap(grad_mod, "blk", half)
    both = jnp.where(micro == 0, jnp.concatenate([grad_mod, other]), jnp.concatenate([other, grad_mod]))
    slots = direct({m: both for m in range(n_dp)}, "dp")
    slots = jnp.concatenate([slots[m] for m in range(n_dp)], axis=0)
    ada_wgrad = dot_tn(cond_cols, slots)
    ada_bgrad = jnp.sum(slots.astype(F32), axis=0)
    ada_bgrad = lax.dynamic_slice(ada_bgrad, (dp * ada_bias.shape[0],), ada_bias.shape)
    cond_part = dot_nt(slots, ada_weight)
    count = 2 * DOCS
    cond_got = in_order(direct({m: cond_part[m * count : (m + 1) * count] for m in range(n_dp)}, "dp"), dp)
    cond_act_grad = jnp.concatenate(cond_got, axis=1).reshape(2, 1, DOCS, features)
    sig = jax.nn.sigmoid(cond)[:, None]
    cond_grad = cond_act_grad * (sig * (1.0 + cond[:, None] * (1.0 - sig)))

    return (
        block_out,
        latent_grad,
        cond_grad,
        ada_wgrad,
        ada_bgrad,
        qkv_wgrad,
        qv_bgrad,
        proj_wgrad,
        proj_bgrad,
        fc1_wgrad,
        fc1_bgrad,
        fc2_wgrad,
        fc2_bgrad,
    )


def solution(mesh):
    in_specs = (
        P(None, "dp", "blk", None),
        P(None, "dp", None, None),
        P(None, "dp", None),
        P(None, "dp", "blk", None),
        P("dp", None),
        P("dp"),
        P("dp", None),
        P(None, "dp"),
        P("dp", None),
        P("dp"),
        P("dp", None),
        P("dp"),
        P("dp", None),
        P("dp"),
    )
    out_specs = (
        P(None, "dp", "blk", None),
        P(None, "dp", "blk", None),
        P(None, "dp", None, None),
        P("dp", None),
        P("dp"),
        P("dp", None),
        P(None, "dp"),
        P("dp", None),
        P("dp"),
        P("dp", None),
        P("dp"),
        P("dp", None),
        P("dp"),
    )
    return jax.shard_map(local, mesh=mesh, in_specs=in_specs, out_specs=out_specs, check_vma=False)
```

time: 2240 us -> 663 us (0.30)
  waiting for transfers between devices: 1690 us -> 225 us
  matrix products: 232 us -> 50 us
  starting transfers between devices: 2.04 us -> 105 us
  blocking collectives: 66.9 us -> 0 us
  Pallas kernels: 0 us -> 58.8 us
  other arithmetic: 73 us -> 102 us
  local copies, waits for them, and re-layouts: 138 us -> 109 us
    reduce_scatter x10 -> x0, waiting for transfers between devices: 904 us -> none  [the longest x2 290 us: local(): lax.psum_scatter(grad_parts[0].astype(jnp.bfloat16), 'dp', scatter_dimens...]
    all_gather x9 -> x0, waiting for transfers between devices: 506 us -> none  [the longest x1 124 us: local(): lax.all_gather(ada_weight, 'dp', axis=0, tiled=True)]
    ppermute x0 -> x97, waiting for transfers between devices: none -> 225 us  [the longest x88 170 us: swap(): return lax.ppermute(x, axis, [(i, i ^ mask) for i in range(count)])]
    dot_general x62 -> x15, matrix products: 232 us -> 50 us  [the longest x5 26.5 us: dot_tn(): lax.dot_general(a, b, (((0,), (0,)), ((), ())), preferred_element_type=F32)]
    psum x2 -> x0, waiting for transfers between devices: 167 us -> none  [the longest x1 114 us: local(): lax.psum(summed[2].astype(jnp.bfloat16), 'blk').astype(jnp.float32)]
    unnamed x29 -> x0, waiting for transfers between devices: 115 us -> none
    ppermute x0 -> x97, starting transfers between devices: none -> 105 us  [the longest x88 83.3 us: swap(): return lax.ppermute(x, axis, [(i, i ^ mask) for i in range(count)])]
    unnamed x298 -> x276, local copies, waits for them, and re-layouts: 98 us -> 17 us
  transfers between devices with their start and end apart: 25 -> 97, of which waited for: 23 -> 36; matrix products, arithmetic and copies ran while one was open for 11% -> 34% of each run, Pallas kernels for 0% -> 6%
where the time goes in v1:
time: 663 us; the launch traced here: 653 us
  waiting for transfers between devices  225 us (34%)
  local copies, waits for them, and re-layouts  109 us (16%)
  starting transfers between devices  105 us (16%)
  other arithmetic  102 us (15%)
  Pallas kernels  58.8 us (9%)
  matrix products  50 us (8%)
    ppermute x88, waiting for transfers between devices, swap(): return lax.ppermute(x, axis, [(i, i ^ mask) for i in range(count)])  170 us
    ppermute x88, starting transfers between devices, swap(): return lax.ppermute(x, axis, [(i, i ^ mask) for i in range(count)])  83.3 us
    ppermute x3, waiting for transfers between devices, sum_line(): got = lax.ppermute(x, 'blk', both([(low, low - 1), (high, high + 1)]))  30.9 us
    dot_general x5, matrix products, dot_tn(): lax.dot_general(a, b, (((0,), (0,)), ((), ())), preferred_element_type=F32)  26.5 us
    ppermute x3, waiting for transfers between devices, sum_line(): lax.ppermute(x, 'blk', both([(s, s + 1), (chips - 1 - s, chips - 2 - s)]))  24.6 us
    pallas_call x1, Pallas kernels, mlp(): pl.pallas_call(mlp_kernel, grid=(tokens // block,), in_specs=[pl.BlockSpe...  21.8 us
    pallas_call x1, Pallas kernels, attend_back(): pl.pallas_call(functools.partial(attend_back_kernel, hpd, block, steps),...  17.6 us
    unnamed x276, local copies, waits for them, and re-layouts  17 us
  transfers between devices with their start and end apart: 97, of which 36 were waited for; matrix products, arithmetic and copies ran while one was open for 34% of the time, Pallas kernels for 6%

profile of v1, /device:TPU:0, one launch (start us, length us, event | category | flops | bytes accessed | tf_op | source)
XLA Modules:
  0.0 653.3 jit_solution(2293413416344368624)
XLA Ops:
  3.7 3.0 collective-permute-start.7
  29.7 2.9 fusion.53
  40.2 2.6 collective-permute-start.33
  45.4 22.0 %collective-permute-done = bf16[128,1152]{1,0:T(8,128)(2,1)S(1)} collective-permute-done((bf16[128,1152]{1,0:T(8,128)(2,1)S(1)}, bf16[128,1152]{1,0:T(8,128)(2,1)S(1)}, u32[]{:S(2)}, u32[]{:S(2)}) %collective-permute-start) | collective-permute-done | bytes 294944 | tf_op jit(solution)/shard_map/ppermute | solution.py:50
  69.3 3.3 fusion.21
  81.5 9.4 %collective-permute-done.25 = bf16[72,1152]{1,0:T(8,128)(2,1)S(1)} collective-permute-done((bf16[72,1152]{1,0:T(8,128)(2,1)S(1)}, bf16[72,1152]{1,0:T(8,128)(2,1)S(1)}, u32[]{:S(2)}, u32[]{:S(2)}) %collective-permute-start.25) | collective-permute-done | bytes 165920 | tf_op jit(solution)/shard_map/ppermute | solution.py:50
  91.6 4.6 collective-permute-done.26
  100.0 6.7 %collective-permute-done.15 = bf16[144,864]{1,0:T(8,128)(2,1)S(1)} collective-permute-done((bf16[144,864]{1,0:T(8,128)(2,1)S(1)}, bf16[144,864]{1,0:T(8,128)(2,1)S(1)}, u32[]{:S(2)}, u32[]{:S(2)}) %collective-permute-start.15) | collective-permute-done | bytes 248864 | tf_op jit(solution)/shard_map/ppermute | solution.py:50
  108.6 13.0 %collective-permute-done.11 = bf16[256,1152]{1,0:T(8,128)(2,1)S(1)} collective-permute-done((bf16[256,1152]{1,0:T(8,128)(2,1)S(1)}, bf16[256,1152]{1,0:T(8,128)(2,1)S(1)}, u32[]{:S(2)}, u32[]{:S(2)}) %collective-permute-start.11) | collective-permute-done | bytes 589856 | tf_op jit(solution)/shard_map/ppermute | solution.py:50
  127.6 6.3 add_convert_fusion.2.qkv_ref
  134.9 15.3 %attend.1 = (bf16[1024,288]{1,0:T(8,128)(2,1)}, f32[288,1024]{1,0:T(8,128)}, f32[8,1024]{1,0:T(8,128)}) custom-call(bf16[1024,864]{1,0:T(8,128)(2,1)} %add_convert_fusion.2.qkv_ref, s32[1,1024]{1,0:T(1,128)} %bitcast.198, s32[1024,128]{1,0:T(8,128)} %broadcast_in_dim.110.dock_ref), custom_call_target="tpu_custom_call" | custom-call | flops 2147483648 | bytes 4718592 | tf_op jit(solution)/shard_map/attend/pallas_call | solution.py:248
  155.8 4.1 collective-permute-done.18
  159.9 3.4 collective-permute-done.19
  166.5 4.1 fusion.91
  180.6 7.5 %collective-permute-done.28 = bf16[256,1152]{1,0:T(8,128)(2,1)S(1)} collective-permute-done((bf16[256,1152]{1,0:T(8,128)(2,1)S(1)}, bf16[256,1152]{1,0:T(8,128)(2,1)S(1)}, u32[]{:S(2)}, u32[]{:S(2)}) %collective-permute-start.28) | collective-permute-done | bytes 589856 | tf_op jit(solution)/shard_map/ppermute | solution.py:50
  193.2 3.4 collective-permute-done.30
  202.1 3.2 constant_dynamic-slice_fusion.13
  210.6 6.4 collective-permute-done.39
  218.8 6.9 %collective-permute-done.40 = bf16[288,576]{1,0:T(8,128)(2,1)} collective-permute-done((bf16[288,576]{1,0:T(8,128)(2,1)}, bf16[288,576]{1,0:T(8,128)(2,1)}, u32[]{:S(2)}, u32[]{:S(2)}) %collective-permute-start.40) | collective-permute-done | bytes 331808 | tf_op jit(solution)/shard_map/ppermute | solution.py:50
  229.3 3.7 fusion.92
  237.3 21.8 %mlp.1 = (bf16[2048,576]{1,0:T(8,128)(2,1)}, bf16[2048,576]{1,0:T(8,128)(2,1)}, bf16[2048,1152]{1,0:T(8,128)(2,1)}, bf16[2048,1152]{1,0:T(8,128)(2,1)}) custom-call(bf16[2048,1152]{1,0:T(8,128)(2,1)} %copy-done.73, bf16[2048,1152]{1,0:T(8,128)(2,1)} %get-tuple-element.186.g_ref, bf16[1152,576]{1,0:T(8,128)(2,1)} %constant_dynamic-update-slice_fusion.24.w1_ref, ...), custom_call_target="tpu_custom_call" | custom-call | flops 10871635968 | bytes 18874368 | tf_op jit(solution)/shard_map/mlp/pallas_call | solution.py:325
  261.6 6.8 %convolution_convert_fusion.4 = bf16[1152,576]{0,1:T(8,128)(2,1)} fusion(bf16[2048,1152]{1,0:T(8,128)(2,1)} %copy-done.73, bf16[2048,576]{1,0:T(8,128)(2,1)S(1)} %copy-done.35), kind=kOutput, calls=%fused_computation.9 | convolution fusion | flops 2718572544 | bytes 8404992 | tf_op jit(solution)/shard_map/dot_general | solution.py:45
  268.4 6.7 %convolution_convert_fusion.3 = bf16[576,1152]{1,0:T(8,128)(2,1)} fusion(bf16[2048,576]{1,0:T(8,128)(2,1)S(1)} %copy-done.134, bf16[2048,1152]{1,0:T(8,128)(2,1)} %get-tuple-element.186.g_ref), kind=kOutput, calls=%fused_computation.8 | convolution fusion | flops 2718572544 | bytes 8404992 | tf_op jit(solution)/shard_map/dot_general | solution.py:45
  278.4 2.5 collective-permute-start.88
  282.1 4.7 collective-permute-start.93
  286.9 3.2 slice.580
  290.1 4.0 collective-permute-done.87
  296.9 4.8 collective-permute-start.89
  307.8 3.4 slice.565
  311.2 5.2 collective-permute-done.93
  316.4 2.8 add_convert_fusion.6
  321.0 19.3 %collective-permute-done.89 = bf16[1152,576]{0,1:T(8,128)(2,1)} collective-permute-done((bf16[1152,576]{0,1:T(8,128)(2,1)}, bf16[1152,576]{0,1:T(8,128)(2,1)}, u32[]{:S(2)}, u32[]{:S(2)}) %collective-permute-start.89) | collective-permute-done | bytes 1327136 | tf_op jit(solution)/shard_map/ppermute | solution.py:140
  340.3 2.6 copy.105
  348.6 3.0 add_convert_fusion
  354.1 3.0 add_convert_fusion.1
  358.2 2.6 collective-permute-done.49
  366.4 4.4 collective-permute-done.45
  375.5 3.1 add_convert_fusion.5
  378.7 2.6 copy.107
  390.1 2.5 convolution_convert_fusion
  401.4 4.6 collective-permute-start.54
  408.9 4.8 pad_maximum_fusion
  419.6 17.6 %attend_back.1 = bf16[1024,864]{1,0:T(8,128)(2,1)} custom-call(bf16[1024,864]{1,0:T(8,128)(2,1)} %add_convert_fusion.2.qkv_ref, bf16[1024,288]{1,0:T(8,128)(2,1)} %pad_maximum_fusion.5.do_ref, f32[288,1024]{1,0:T(8,128)} %get-tuple-element.25.outt_ref, f32[8,1024]{1,0:T(8,128)} %get-tuple-element.26.peak_ref, s32[1,1024]{1,0:T(1,128)} %bitcast.199, ...), custom_call_target="tpu_custom_call" | custom-call | flops 5368709120 | bytes 5898240 | tf_op jit(solution)/shard_map/attend_back/pallas_call | solution.py:280
  439.0 6.0 convolution_convert_fusion.2
  445.0 4.1 copy.102
  452.0 3.2 convolution_convert_fusion.1
  458.1 5.9 collective-permute-done.69
  470.0 2.6 broadcast_select_fusion.3
  472.6 8.9 %collective-permute-done.70 = bf16[304,864]{1,0:T(8,128)(2,1)S(1)} collective-permute-done((bf16[304,864]{1,0:T(8,128)(2,1)S(1)}, bf16[304,864]{1,0:T(8,128)(2,1)S(1)}, u32[]{:S(2)}, u32[]{:S(2)}) %collective-permute-start.70) | collective-permute-done | bytes 525344 | tf_op jit(solution)/shard_map/ppermute | solution.py:50
  484.0 14.7 %collective-permute-done.91 = bf16[1152,576]{0,1:T(8,128)(2,1)S(1)} collective-permute-done((bf16[1152,576]{0,1:T(8,128)(2,1)S(1)}, bf16[1152,576]{0,1:T(8,128)(2,1)S(1)}, u32[]{:S(2)}, u32[]{:S(2)}) %collective-permute-start.91) | collective-permute-done | bytes 1327136 | tf_op jit(solution)/shard_map/ppermute | solution.py:144
  499.8 2.6 copy.109
  506.0 8.6 %collective-permute-done.58 = bf16[256,1152]{1,0:T(8,128)(2,1)} collective-permute-done((bf16[256,1152]{1,0:T(8,128)(2,1)}, bf16[256,1152]{1,0:T(8,128)(2,1)}, u32[]{:S(2)}, u32[]{:S(2)}) %collective-permute-start.58) | collective-permute-done | bytes 589856 | tf_op jit(solution)/shard_map/ppermute | solution.py:50
  530.4 2.9 collective-permute-start.59
  533.4 13.1 %collective-permute-done.73 = bf16[304,864]{1,0:T(8,128)(2,1)S(1)} collective-permute-done((bf16[304,864]{1,0:T(8,128)(2,1)}, bf16[304,864]{1,0:T(8,128)(2,1)S(1)}, u32[]{:S(2)}, u32[]{:S(2)}) %collective-permute-start.73) | collective-permute-done | bytes 525344 | tf_op jit(solution)/shard_map/ppermute | solution.py:50
  551.0 4.5 collective-permute-done.61
  557.9 9.8 %collective-permute-done.62 = bf16[4,6912]{1,0:T(4,128)(2,1)S(1)} collective-permute-done((bf16[4,6912]{1,0:T(4,128)(2,1)S(1)}, bf16[4,6912]{1,0:T(4,128)(2,1)S(1)}, u32[]{:S(2)}, u32[]{:S(2)}) %collective-permute-start.62) | collective-permute-done | bytes 55328 | tf_op jit(solution)/shard_map/ppermute | solution.py:50
  587.5 4.5 fusion.45
  595.5 7.8 %collective-permute-done.75 = bf16[304,864]{1,0:T(8,128)(2,1)} collective-permute-done((bf16[304,864]{1,0:T(8,128)(2,1)}, bf16[304,864]{1,0:T(8,128)(2,1)}, u32[]{:S(2)}, u32[]{:S(2)}) %collective-permute-start.75) | collective-permute-done | bytes 525344 | tf_op jit(solution)/shard_map/ppermute | solution.py:50
  605.0 3.2 collective-permute-start.82
  611.4 2.7 maximum_convert_fusion
  614.2 2.7 copy.111
  623.6 16.2 %collective-permute-done.84 = bf16[160,1152]{1,0:T(8,128)(2,1)S(1)} collective-permute-done((bf16[160,1152]{1,0:T(8,128)(2,1)S(1)}, bf16[160,1152]{1,0:T(8,128)(2,1)S(1)}, u32[]{:S(2)}, u32[]{:S(2)}) %collective-permute-start.84) | collective-permute-done | bytes 368672 | tf_op jit(solution)/shard_map/ppermute | solution.py:144
  640.0 3.3 pad_maximum_fusion.2.parts_ref
  643.3 4.2 place_qkv.1
  (664 shorter events, 250.7 us)
Async XLA Ops:
  3.7 20.3 %collective-permute-start.7 = (bf16[1,2880]{1,0:T(2,128)(2,1)S(1)}, bf16[1,2880]{1,0:T(2,128)(2,1)S(1)}, u32[]{:S(2)}, u32[]{:S(2)}) collective-permute-start(bf16[1,2880]{1,0:T(2,128)(2,1)S(1)} %broadcast_in_dim.106), channel_id=1, source_target_pairs={{0,8},{8,0},{16,24},{24,16},{1,9},{9,1},{17,25},{25,17},{2,10},{10... | collective-permute-start | bytes 17288 | tf_op jit(solution)/shard_map/ppermute | solution.py:50
  6.7 17.3 %collective-permute-start.8 = (bf16[1,2880]{1,0:T(2,128)(2,1)S(1)}, bf16[1,2880]{1,0:T(2,128)(2,1)S(1)}, u32[]{:S(2)}, u32[]{:S(2)}) collective-permute-start(bf16[1,2880]{1,0:T(2,128)(2,1)S(1)} %broadcast_in_dim.106), channel_id=1, source_target_pairs={{0,16},{8,24},{16,0},{24,8},{1,17},{9,25},{17,1},{25,9},{2,18},{10... | collective-permute-start | bytes 17288 | tf_op jit(solution)/shard_map/ppermute | solution.py:50
  8.2 15.9 %collective-permute-start.9 = (bf16[1,2880]{1,0:T(2,128)(2,1)S(1)}, bf16[1,2880]{1,0:T(2,128)(2,1)S(1)}, u32[]{:S(2)}, u32[]{:S(2)}) collective-permute-start(bf16[1,2880]{1,0:T(2,128)(2,1)S(1)} %broadcast_in_dim.106), channel_id=1, source_target_pairs={{0,24},{8,16},{16,8},{24,0},{1,25},{9,17},{17,9},{25,1},{2,26},{10... | collective-permute-start | bytes 17288 | tf_op jit(solution)/shard_map/ppermute | solution.py:50
  9.0 20.4 %collective-permute-start.1 = (bf16[8,1152]{1,0:T(8,128)(2,1)S(1)}, bf16[8,1152]{1,0:T(8,128)(2,1)S(1)}, u32[]{:S(2)}, u32[]{:S(2)}) collective-permute-start(bf16[8,1152]{1,0:T(8,128)(2,1)S(1)} %multiply_convert_fusion.1), channel_id=1, source_target_pairs={{0,8},{8,0},{16,24},{24,16},{1,9},{9,1},{17,25},{25,17},{2,10},{10... | collective-permute-start | bytes 55304 | tf_op jit(solution)/shard_map/ppermute | solution.py:50
  11.0 18.5 %collective-permute-start.2 = (bf16[8,1152]{1,0:T(8,128)(2,1)S(1)}, bf16[8,1152]{1,0:T(8,128)(2,1)S(1)}, u32[]{:S(2)}, u32[]{:S(2)}) collective-permute-start(bf16[8,1152]{1,0:T(8,128)(2,1)S(1)} %multiply_convert_fusion.1), channel_id=1, source_target_pairs={{0,16},{8,24},{16,0},{24,8},{1,17},{9,25},{17,1},{25,9},{2,18},{10... | collective-permute-start | bytes 55304 | tf_op jit(solution)/shard_map/ppermute | solution.py:50
  24.0 53.1 %collective-permute-start.20 = (bf16[144,1152]{1,0:T(8,128)(2,1)}, bf16[144,1152]{1,0:T(8,128)(2,1)}, u32[]{:S(2)}, u32[]{:S(2)}) collective-permute-start(bf16[144,1152]{1,0:T(8,128)(2,1)} %get-tuple-element.163), channel_id=1, source_target_pairs={{0,1},{1,0},{2,3},{3,2},{4,5},{5,4},{6,7},{7,6},{8,9},{9,8},{10,11... | collective-permute-start | bytes 995336 | tf_op jit(solution)/shard_map/ppermute | solution.py:50
  24.1 51.3 %collective-permute-start.21 = (bf16[144,1152]{1,0:T(8,128)(2,1)}, bf16[144,1152]{1,0:T(8,128)(2,1)}, u32[]{:S(2)}, u32[]{:S(2)}) collective-permute-start(bf16[144,1152]{1,0:T(8,128)(2,1)} %get-tuple-element.163), channel_id=1, source_target_pairs={{0,8},{8,0},{16,24},{24,16},{1,9},{9,1},{17,25},{25,17},{2,10},{10... | collective-permute-start | bytes 995336 | tf_op jit(solution)/shard_map/ppermute | solution.py:50
  38.6 42.3 %collective-permute-start.23 = (bf16[144,1152]{1,0:T(8,128)(2,1)S(1)}, bf16[144,1152]{1,0:T(8,128)(2,1)S(1)}, u32[]{:S(2)}, u32[]{:S(2)}) collective-permute-start(bf16[144,1152]{1,0:T(8,128)(2,1)S(1)} %copy-done.51), channel_id=1, source_target_pairs={{0,16},{8,24},{16,0},{24,8},{1,17},{9,25},{17,1},{25,9},{2,18},{10... | collective-permute-start | bytes 995336 | tf_op jit(solution)/shard_map/ppermute | solution.py:50
  40.2 32.4 %collective-permute-start.33 = (bf16[128,1152]{1,0:T(8,128)(2,1)}, bf16[128,1152]{1,0:T(8,128)(2,1)S(1)}, u32[]{:S(2)}, u32[]{:S(2)}) collective-permute-start(bf16[128,1152]{1,0:T(8,128)(2,1)} %get-tuple-element.245), channel_id=1, source_target_pairs={{0,4},{1,5},{2,6},{3,7},{4,0},{5,1},{6,2},{7,3},{8,12},{9,13},{10,... | collective-permute-start | bytes 884744 | tf_op jit(solution)/shard_map/ppermute | solution.py:50
  42.8 24.7 %collective-permute-start = (bf16[128,1152]{1,0:T(8,128)(2,1)S(1)}, bf16[128,1152]{1,0:T(8,128)(2,1)S(1)}, u32[]{:S(2)}, u32[]{:S(2)}) collective-permute-start(bf16[128,1152]{1,0:T(8,128)(2,1)S(1)} %copy-done.52), channel_id=1, source_target_pairs={{0,4},{1,5},{2,6},{3,7},{4,0},{5,1},{6,2},{7,3},{8,12},{9,13},{10,... | collective-permute-start | bytes 884744 | tf_op jit(solution)/shard_map/ppermute | solution.py:50
  67.4 28.9 %collective-permute-start.13 = (bf16[288,864]{1,0:T(8,128)(2,1)S(1)}, bf16[288,864]{1,0:T(8,128)(2,1)S(1)}, u32[]{:S(2)}, u32[]{:S(2)}) collective-permute-start(bf16[288,864]{1,0:T(8,128)(2,1)S(1)} %copy-done.50), channel_id=1, source_target_pairs={{0,8},{8,0},{16,24},{24,16},{1,9},{9,1},{17,25},{25,17},{2,10},{10... | collective-permute-start | bytes 1493000 | tf_op jit(solution)/shard_map/ppermute | solution.py:50
  72.6 24.3 %collective-permute-start.14 = (bf16[288,864]{1,0:T(8,128)(2,1)S(1)}, bf16[288,864]{1,0:T(8,128)(2,1)S(1)}, u32[]{:S(2)}, u32[]{:S(2)}) collective-permute-start(bf16[288,864]{1,0:T(8,128)(2,1)S(1)} %copy-done.50), channel_id=1, source_target_pairs={{0,16},{8,24},{16,0},{24,8},{1,17},{9,25},{17,1},{25,9},{2,18},{10... | collective-permute-start | bytes 1493000 | tf_op jit(solution)/shard_map/ppermute | solution.py:50
  75.4 47.9 %collective-permute-start.34 = (bf16[256,1152]{1,0:T(8,128)(2,1)S(1)}, bf16[256,1152]{1,0:T(8,128)(2,1)S(1)}, u32[]{:S(2)}, u32[]{:S(2)}) collective-permute-start(bf16[256,1152]{1,0:T(8,128)(2,1)S(1)} %get-tuple-element.152), channel_id=1, source_target_pairs={{0,8},{8,0},{16,24},{24,16},{1,9},{9,1},{17,25},{25,17},{2,10},{10... | collective-permute-start | bytes 1769480 | tf_op jit(solution)/shard_map/ppermute | solution.py:50
  77.2 13.8 %collective-permute-start.25 = (bf16[72,1152]{1,0:T(8,128)(2,1)S(1)}, bf16[72,1152]{1,0:T(8,128)(2,1)S(1)}, u32[]{:S(2)}, u32[]{:S(2)}) collective-permute-start(bf16[72,1152]{1,0:T(8,128)(2,1)S(1)} %slice.667), channel_id=1, source_target_pairs={{0,16},{8,24},{16,0},{24,8},{1,17},{9,25},{17,1},{25,9},{2,18},{10... | collective-permute-start | bytes 497672 | tf_op jit(solution)/shard_map/ppermute | solution.py:50
  80.9 43.6 %collective-permute-start.35 = (bf16[256,1152]{1,0:T(8,128)(2,1)S(1)}, bf16[256,1152]{1,0:T(8,128)(2,1)S(1)}, u32[]{:S(2)}, u32[]{:S(2)}) collective-permute-start(bf16[256,1152]{1,0:T(8,128)(2,1)S(1)} %get-tuple-element.152), channel_id=1, source_target_pairs={{0,16},{8,24},{16,0},{24,8},{1,17},{9,25},{17,1},{25,9},{2,18},{10... | collective-permute-start | bytes 1769480 | tf_op jit(solution)/shard_map/ppermute | solution.py:50
  96.9 11.7 %collective-permute-start.27 = (bf16[144,1152]{1,0:T(8,128)(2,1)S(1)}, bf16[144,1152]{1,0:T(8,128)(2,1)S(1)}, u32[]{:S(2)}, u32[]{:S(2)}) collective-permute-start(bf16[144,1152]{1,0:T(8,128)(2,1)S(1)} %constant_dynamic-update-slice_fusion), channel_id=1, source_target_pairs={{0,1},{1,0},{2,3},{3,2},{4,5},{5,4},{6,7},{7,6},{8,9},{9,8},{10,11... | collective-permute-start | bytes 995336 | tf_op jit(solution)/shard_map/ppermute | solution.py:50
  106.7 14.9 %collective-permute-start.11 = (bf16[256,1152]{1,0:T(8,128)(2,1)S(1)}, bf16[256,1152]{1,0:T(8,128)(2,1)S(1)}, u32[]{:S(2)}, u32[]{:S(2)}) collective-permute-start(bf16[256,1152]{1,0:T(8,128)(2,1)S(1)} %fusion.21), channel_id=1, source_target_pairs={{0,2},{1,3},{2,0},{3,1},{4,6},{5,7},{6,4},{7,5},{8,10},{9,11},{10,... | collective-permute-start | bytes 1769480 | tf_op jit(solution)/shard_map/ppermute | solution.py:50
  108.5 19.1 %collective-permute-start.10 = (bf16[256,1152]{1,0:T(8,128)(2,1)S(1)}, bf16[256,1152]{1,0:T(8,128)(2,1)S(1)}, u32[]{:S(2)}, u32[]{:S(2)}) collective-permute-start(bf16[256,1152]{1,0:T(8,128)(2,1)S(1)} %fusion.21), channel_id=1, source_target_pairs={{0,1},{1,0},{2,3},{3,2},{4,5},{5,4},{6,7},{7,6},{8,9},{9,8},{10,11... | collective-permute-start | bytes 1769480 | tf_op jit(solution)/shard_map/ppermute | solution.py:50
  124.1 51.7 %collective-permute-start.36 = (bf16[128,1152]{1,0:T(8,128)(2,1)}, bf16[128,1152]{1,0:T(8,128)(2,1)}, u32[]{:S(2)}, u32[]{:S(2)}) collective-permute-start(bf16[128,1152]{1,0:T(8,128)(2,1)} %slice.687), channel_id=1, source_target_pairs={{0,16},{8,24},{16,0},{24,8},{1,17},{9,25},{17,1},{25,9},{2,18},{10... | collective-permute-start | bytes 884744 | tf_op jit(solution)/shard_map/ppermute | solution.py:50
  125.3 52.8 %collective-permute-start.37 = (bf16[128,1152]{1,0:T(8,128)(2,1)}, bf16[128,1152]{1,0:T(8,128)(2,1)}, u32[]{:S(2)}, u32[]{:S(2)}) collective-permute-start(bf16[128,1152]{1,0:T(8,128)(2,1)} %slice.688), channel_id=1, source_target_pairs={{0,8},{8,0},{16,24},{24,16},{1,9},{9,1},{17,25},{25,17},{2,10},{10... | collective-permute-start | bytes 884744 | tf_op jit(solution)/shard_map/ppermute | solution.py:50
  172.7 15.4 %collective-permute-start.28 = (bf16[256,1152]{1,0:T(8,128)(2,1)S(1)}, bf16[256,1152]{1,0:T(8,128)(2,1)S(1)}, u32[]{:S(2)}, u32[]{:S(2)}) collective-permute-start(bf16[256,1152]{1,0:T(8,128)(2,1)S(1)} %get-tuple-element.159), channel_id=1, source_target_pairs={{0,8},{8,0},{16,24},{24,16},{1,9},{9,1},{17,25},{25,17},{2,10},{10... | collective-permute-start | bytes 1769480 | tf_op jit(solution)/shard_map/ppermute | solution.py:50
  174.2 15.6 %collective-permute-start.29 = (bf16[256,1152]{1,0:T(8,128)(2,1)S(1)}, bf16[256,1152]{1,0:T(8,128)(2,1)S(1)}, u32[]{:S(2)}, u32[]{:S(2)}) collective-permute-start(bf16[256,1152]{1,0:T(8,128)(2,1)S(1)} %get-tuple-element.159), channel_id=1, source_target_pairs={{0,16},{8,24},{16,0},{24,8},{1,17},{9,25},{17,1},{25,9},{2,18},{10... | collective-permute-start | bytes 1769480 | tf_op jit(solution)/shard_map/ppermute | solution.py:50
  180.6 48.7 %collective-permute-start.38 = (bf16[1024,1152]{1,0:T(8,128)(2,1)}, bf16[1024,1152]{1,0:T(8,128)(2,1)}, u32[]{:S(2)}, u32[]{:S(2)}) collective-permute-start(bf16[1024,1152]{1,0:T(8,128)(2,1)} %get-tuple-element.262), channel_id=1, source_target_pairs={{0,1},{1,0},{2,3},{3,2},{4,5},{5,4},{6,7},{7,6},{8,9},{9,8},{10,11... | collective-permute-start | bytes 7077896 | tf_op jit(solution)/shard_map/ppermute | solution.py:50
  200.8 32.2 %collective-permute-start.32 = (bf16[1024,1152]{1,0:T(8,128)(2,1)}, bf16[1024,1152]{1,0:T(8,128)(2,1)}, u32[]{:S(2)}, u32[]{:S(2)}) collective-permute-start(bf16[1024,1152]{1,0:T(8,128)(2,1)} %get-tuple-element.263), channel_id=1, source_target_pairs={{0,1},{1,0},{2,3},{3,2},{4,5},{5,4},{6,7},{7,6},{8,9},{9,8},{10,11... | collective-permute-start | bytes 7077896 | tf_op jit(solution)/shard_map/ppermute | solution.py:50
  205.3 11.7 %collective-permute-start.39 = (bf16[288,576]{1,0:T(8,128)(2,1)}, bf16[288,576]{1,0:T(8,128)(2,1)}, u32[]{:S(2)}, u32[]{:S(2)}) collective-permute-start(bf16[288,576]{1,0:T(8,128)(2,1)} %get-tuple-element.178), channel_id=1, source_target_pairs={{0,8},{8,0},{16,24},{24,16},{1,9},{9,1},{17,25},{25,17},{2,10},{10... | collective-permute-start | bytes 995336 | tf_op jit(solution)/shard_map/ppermute | solution.py:50
  206.8 18.9 %collective-permute-start.40 = (bf16[288,576]{1,0:T(8,128)(2,1)}, bf16[288,576]{1,0:T(8,128)(2,1)}, u32[]{:S(2)}, u32[]{:S(2)}) collective-permute-start(bf16[288,576]{1,0:T(8,128)(2,1)} %get-tuple-element.180), channel_id=1, source_target_pairs={{0,16},{8,24},{16,0},{24,8},{1,17},{9,25},{17,1},{25,9},{2,18},{10... | collective-permute-start | bytes 995336 | tf_op jit(solution)/shard_map/ppermute | solution.py:50
  207.7 19.7 %collective-permute-start.41 = (bf16[288,576]{1,0:T(8,128)(2,1)}, bf16[288,576]{1,0:T(8,128)(2,1)}, u32[]{:S(2)}, u32[]{:S(2)}) collective-permute-start(bf16[288,576]{1,0:T(8,128)(2,1)} %get-tuple-element.177), channel_id=1, source_target_pairs={{0,24},{8,16},{16,8},{24,0},{1,25},{9,17},{17,9},{25,1},{2,26},{10... | collective-permute-start | bytes 995336 | tf_op jit(solution)/shard_map/ppermute | solution.py:50
  277.4 12.8 %collective-permute-start.86 = (bf16[288,576]{1,0:T(8,128)(2,1)S(1)}, bf16[288,576]{1,0:T(8,128)(2,1)S(1)}, u32[]{:S(2)}, u32[]{:S(2)}) collective-permute-start(bf16[288,576]{1,0:T(8,128)(2,1)S(1)} %get-tuple-element.221), channel_id=1, source_target_pairs={{0,8},{8,0},{16,24},{24,16},{1,9},{9,1},{17,25},{25,17},{2,10},{10... | collective-permute-start | bytes 995336 | tf_op jit(solution)/shard_map/ppermute | solution.py:50
  277.4 16.7 %collective-permute-start.87 = (bf16[288,576]{1,0:T(8,128)(2,1)S(1)}, bf16[288,576]{1,0:T(8,128)(2,1)S(1)}, u32[]{:S(2)}, u32[]{:S(2)}) collective-permute-start(bf16[288,576]{1,0:T(8,128)(2,1)S(1)} %get-tuple-element.220), channel_id=1, source_target_pairs={{0,16},{8,24},{16,0},{24,8},{1,17},{9,25},{17,1},{25,9},{2,18},{10... | collective-permute-start | bytes 995336 | tf_op jit(solution)/shard_map/ppermute | solution.py:50
  278.4 15.7 %collective-permute-start.88 = (bf16[288,576]{1,0:T(8,128)(2,1)S(1)}, bf16[288,576]{1,0:T(8,128)(2,1)S(1)}, u32[]{:S(2)}, u32[]{:S(2)}) collective-permute-start(bf16[288,576]{1,0:T(8,128)(2,1)S(1)} %get-tuple-element.219), channel_id=1, source_target_pairs={{0,24},{8,16},{16,8},{24,0},{1,25},{9,17},{17,9},{25,1},{2,26},{10... | collective-permute-start | bytes 995336 | tf_op jit(solution)/shard_map/ppermute | solution.py:50
  282.1 34.3 %collective-permute-start.93 = (bf16[592,1152]{1,0:T(8,128)(2,1)}, bf16[592,1152]{1,0:T(8,128)(2,1)}, u32[]{:S(2)}, u32[]{:S(2)}) collective-permute-start(bf16[592,1152]{1,0:T(8,128)(2,1)} %fusion.19), channel_id=1, source_target_pairs={{0,2},{1,3},{6,4},{7,5},{8,10},{9,11},{14,12},{15,13},{16,18},{17,... | collective-permute-start | bytes 4091912 | tf_op jit(solution)/shard_map/ppermute | solution.py:140
  290.1 58.5 %collective-permute-start.48 = (bf16[1024,1152]{1,0:T(8,128)(2,1)}, bf16[1024,1152]{1,0:T(8,128)(2,1)}, u32[]{:S(2)}, u32[]{:S(2)}) collective-permute-start(bf16[1024,1152]{1,0:T(8,128)(2,1)} %slice.580), channel_id=1, source_target_pairs={{0,1},{1,0},{2,3},{3,2},{4,5},{5,4},{6,7},{7,6},{8,9},{9,8},{10,11... | collective-permute-start | bytes 7077896 | tf_op jit(solution)/shard_map/ppermute | solution.py:50
  296.9 43.4 %collective-permute-start.89 = (bf16[1152,576]{0,1:T(8,128)(2,1)}, bf16[1152,576]{0,1:T(8,128)(2,1)}, u32[]{:S(2)}, u32[]{:S(2)}) collective-permute-start(bf16[1152,576]{0,1:T(8,128)(2,1)} %copy.104), channel_id=1, source_target_pairs={{0,2},{1,3},{6,4},{7,5},{8,10},{9,11},{14,12},{15,13},{16,18},{17,... | collective-permute-start | bytes 3981320 | tf_op jit(solution)/shard_map/ppermute | solution.py:140
  311.2 42.9 %collective-permute-start.42 = (bf16[1024,1152]{1,0:T(8,128)(2,1)}, bf16[1024,1152]{1,0:T(8,128)(2,1)}, u32[]{:S(2)}, u32[]{:S(2)}) collective-permute-start(bf16[1024,1152]{1,0:T(8,128)(2,1)} %slice.565), channel_id=1, source_target_pairs={{0,1},{1,0},{2,3},{3,2},{4,5},{5,4},{6,7},{7,6},{8,9},{9,8},{10,11... | collective-permute-start | bytes 7077896 | tf_op jit(solution)/shard_map/ppermute | solution.py:50
  319.2 55.5 %collective-permute-start.94 = (bf16[592,1152]{1,0:T(8,128)(2,1)}, bf16[592,1152]{1,0:T(8,128)(2,1)}, u32[]{:S(2)}, u32[]{:S(2)}) collective-permute-start(bf16[592,1152]{1,0:T(8,128)(2,1)} %add_convert_fusion.6), channel_id=1, source_target_pairs={{2,4},{3,5},{4,2},{5,3},{10,12},{11,13},{12,10},{13,11},{18,20},{1... | collective-permute-start | bytes 4091912 | tf_op jit(solution)/shard_map/ppermute | solution.py:141
  346.5 32.2 %collective-permute-start.90 = (bf16[1152,576]{0,1:T(8,128)(2,1)}, bf16[1152,576]{0,1:T(8,128)(2,1)}, u32[]{:S(2)}, u32[]{:S(2)}) collective-permute-start(bf16[1152,576]{0,1:T(8,128)(2,1)} %copy.106), channel_id=1, source_target_pairs={{2,4},{3,5},{4,2},{5,3},{10,12},{11,13},{12,10},{13,11},{18,20},{1... | collective-permute-start | bytes 3981320 | tf_op jit(solution)/shard_map/ppermute | solution.py:141
  352.7 10.1 %collective-permute-start.51 = (bf16[128,1152]{1,0:T(8,128)(2,1)S(1)}, bf16[128,1152]{1,0:T(8,128)(2,1)S(1)}, u32[]{:S(2)}, u32[]{:S(2)}) collective-permute-start(bf16[128,1152]{1,0:T(8,128)(2,1)S(1)} %get-tuple-element.191), channel_id=1, source_target_pairs={{0,8},{8,0},{16,24},{24,16},{1,9},{9,1},{17,25},{25,17},{2,10},{10... | collective-permute-start | bytes 884744 | tf_op jit(solution)/shard_map/ppermute | solution.py:50
  363.8 21.5 %collective-permute-start.50 = (bf16[256,1152]{1,0:T(8,128)(2,1)}, bf16[256,1152]{1,0:T(8,128)(2,1)}, u32[]{:S(2)}, u32[]{:S(2)}) collective-permute-start(bf16[256,1152]{1,0:T(8,128)(2,1)} %pad_maximum_fusion.11), channel_id=1, source_target_pairs={{0,8},{8,0},{16,24},{24,16},{1,9},{9,1},{17,25},{25,17},{2,10},{10... | collective-permute-start | bytes 1769480 | tf_op jit(solution)/shard_map/ppermute | solution.py:50
  365.6 19.8 %collective-permute-start.52 = (bf16[256,1152]{1,0:T(8,128)(2,1)}, bf16[256,1152]{1,0:T(8,128)(2,1)}, u32[]{:S(2)}, u32[]{:S(2)}) collective-permute-start(bf16[256,1152]{1,0:T(8,128)(2,1)} %pad_maximum_fusion.12), channel_id=1, source_target_pairs={{0,16},{8,24},{16,0},{24,8},{1,17},{9,25},{17,1},{25,9},{2,18},{10... | collective-permute-start | bytes 1769480 | tf_op jit(solution)/shard_map/ppermute | solution.py:50
  371.8 152.4 %collective-permute-start.44 = (bf16[256,1152]{1,0:T(8,128)(2,1)}, bf16[256,1152]{1,0:T(8,128)(2,1)}, u32[]{:S(2)}, u32[]{:S(2)}) collective-permute-start(bf16[256,1152]{1,0:T(8,128)(2,1)} %pad_maximum_fusion.8), channel_id=1, source_target_pairs={{0,8},{8,0},{16,24},{24,16},{1,9},{9,1},{17,25},{25,17},{2,10},{10... | collective-permute-start | bytes 1769480 | tf_op jit(solution)/shard_map/ppermute | solution.py:50
  374.6 149.6 %collective-permute-start.46 = (bf16[256,1152]{1,0:T(8,128)(2,1)}, bf16[256,1152]{1,0:T(8,128)(2,1)}, u32[]{:S(2)}, u32[]{:S(2)}) collective-permute-start(bf16[256,1152]{1,0:T(8,128)(2,1)} %pad_maximum_fusion.9), channel_id=1, source_target_pairs={{0,16},{8,24},{16,0},{24,8},{1,17},{9,25},{17,1},{25,9},{2,18},{10... | collective-permute-start | bytes 1769480 | tf_op jit(solution)/shard_map/ppermute | solution.py:50
  399.7 16.1 %collective-permute-start.53 = (bf16[256,288]{1,0:T(8,128)(2,1)}, bf16[256,288]{1,0:T(8,128)(2,1)}, u32[]{:S(2)}, u32[]{:S(2)}) collective-permute-start(bf16[256,288]{1,0:T(8,128)(2,1)} %copy.98), channel_id=1, source_target_pairs={{0,1},{1,0},{2,3},{3,2},{4,5},{5,4},{6,7},{7,6},{8,9},{9,8},{10,11... | collective-permute-start | bytes 442376 | tf_op jit(solution)/shard_map/ppermute | solution.py:50
  401.4 16.2 %collective-permute-start.54 = (bf16[256,288]{1,0:T(8,128)(2,1)}, bf16[256,288]{1,0:T(8,128)(2,1)}, u32[]{:S(2)}, u32[]{:S(2)}) collective-permute-start(bf16[256,288]{1,0:T(8,128)(2,1)} %copy.99), channel_id=1, source_target_pairs={{0,2},{1,3},{2,0},{3,1},{4,6},{5,7},{6,4},{7,5},{8,10},{9,11},{10,... | collective-permute-start | bytes 442376 | tf_op jit(solution)/shard_map/ppermute | solution.py:50
  406.8 10.8 %collective-permute-start.55 = (bf16[256,288]{1,0:T(8,128)(2,1)}, bf16[256,288]{1,0:T(8,128)(2,1)S(1)}, u32[]{:S(2)}, u32[]{:S(2)}) collective-permute-start(bf16[256,288]{1,0:T(8,128)(2,1)} %copy.100), channel_id=1, source_target_pairs={{0,3},{1,2},{2,1},{3,0},{4,7},{5,6},{6,5},{7,4},{8,11},{9,10},{10,... | collective-permute-start | bytes 442376 | tf_op jit(solution)/shard_map/ppermute | solution.py:50
  416.1 52.8 %collective-permute-start.95 = (bf16[592,1152]{1,0:T(8,128)(2,1)S(1)}, bf16[592,1152]{1,0:T(8,128)(2,1)}, u32[]{:S(2)}, u32[]{:S(2)}) collective-permute-start(bf16[592,1152]{1,0:T(8,128)(2,1)S(1)} %copy-done.17), channel_id=1, source_target_pairs={{2,0},{3,1},{4,6},{5,7},{10,8},{11,9},{12,14},{13,15},{18,16},{19,... | collective-permute-start | bytes 4091912 | tf_op jit(solution)/shard_map/ppermute | solution.py:144
  464.8 33.8 %collective-permute-start.91 = (bf16[1152,576]{0,1:T(8,128)(2,1)S(1)}, bf16[1152,576]{0,1:T(8,128)(2,1)S(1)}, u32[]{:S(2)}, u32[]{:S(2)}) collective-permute-start(bf16[1152,576]{0,1:T(8,128)(2,1)S(1)} %copy-done.44), channel_id=1, source_target_pairs={{2,0},{3,1},{4,6},{5,7},{10,8},{11,9},{12,14},{13,15},{18,16},{19,... | collective-permute-start | bytes 3981320 | tf_op jit(solution)/shard_map/ppermute | solution.py:144
  467.2 14.2 %collective-permute-start.70 = (bf16[304,864]{1,0:T(8,128)(2,1)S(1)}, bf16[304,864]{1,0:T(8,128)(2,1)S(1)}, u32[]{:S(2)}, u32[]{:S(2)}) collective-permute-start(bf16[304,864]{1,0:T(8,128)(2,1)S(1)} %pad_maximum_fusion.13), channel_id=1, source_target_pairs={{0,8},{8,0},{16,24},{24,16},{1,9},{9,1},{17,25},{25,17},{2,10},{10... | collective-permute-start | bytes 1575944 | tf_op jit(solution)/shard_map/ppermute | solution.py:50
  468.9 14.1 %collective-permute-start.72 = (bf16[304,864]{1,0:T(8,128)(2,1)S(1)}, bf16[304,864]{1,0:T(8,128)(2,1)S(1)}, u32[]{:S(2)}, u32[]{:S(2)}) collective-permute-start(bf16[304,864]{1,0:T(8,128)(2,1)S(1)} %pad_maximum_fusion.14), channel_id=1, source_target_pairs={{0,16},{8,24},{16,0},{24,8},{1,17},{9,25},{17,1},{25,9},{2,18},{10... | collective-permute-start | bytes 1575944 | tf_op jit(solution)/shard_map/ppermute | solution.py:50
  481.4 66.0 %collective-permute-start.77 = (bf16[4,160,1152]{2,1,0:T(8,128)(2,1)}, bf16[4,160,1152]{2,1,0:T(8,128)(2,1)}, u32[]{:S(2)}, u32[]{:S(2)}) collective-permute-start(bf16[4,160,1152]{2,1,0:T(8,128)(2,1)} %fusion.10), channel_id=1, source_target_pairs={{0,1},{1,0},{2,3},{3,2},{4,5},{5,4},{6,7},{7,6},{8,9},{9,8},{10,11... | collective-permute-start | bytes 4423688 | tf_op jit(solution)/shard_map/ppermute | solution.py:50
  483.0 22.9 %collective-permute-start.56 = (bf16[256,1152]{1,0:T(8,128)(2,1)}, bf16[256,1152]{1,0:T(8,128)(2,1)}, u32[]{:S(2)}, u32[]{:S(2)}) collective-permute-start(bf16[256,1152]{1,0:T(8,128)(2,1)} %get-tuple-element.187), channel_id=1, source_target_pairs={{0,1},{1,0},{2,3},{3,2},{4,5},{5,4},{6,7},{7,6},{8,9},{9,8},{10,11... | collective-permute-start | bytes 1769480 | tf_op jit(solution)/shard_map/ppermute | solution.py:50
  499.8 14.9 %collective-permute-start.58 = (bf16[256,1152]{1,0:T(8,128)(2,1)}, bf16[256,1152]{1,0:T(8,128)(2,1)}, u32[]{:S(2)}, u32[]{:S(2)}) collective-permute-start(bf16[256,1152]{1,0:T(8,128)(2,1)} %add_convert_fusion.7), channel_id=1, source_target_pairs={{0,2},{1,3},{2,0},{3,1},{4,6},{5,7},{6,4},{7,5},{8,10},{9,11},{10,... | collective-permute-start | bytes 1769480 | tf_op jit(solution)/shard_map/ppermute | solution.py:50
  505.9 102.3 %collective-permute-start.96 = (bf16[592,1152]{1,0:T(8,128)(2,1)}, bf16[592,1152]{1,0:T(8,128)(2,1)}, u32[]{:S(2)}, u32[]{:S(2)}) collective-permute-start(bf16[592,1152]{1,0:T(8,128)(2,1)} %broadcast_select_fusion.3), channel_id=1, source_target_pairs={{0,1},{1,0},{2,3},{3,2},{4,5},{5,4},{6,7},{7,6},{8,9},{9,8},{10,11... | collective-permute-start | bytes 4091912 | tf_op jit(solution)/shard_map/ppermute | solution.py:50
  514.6 31.9 %collective-permute-start.73 = (bf16[304,864]{1,0:T(8,128)(2,1)}, bf16[304,864]{1,0:T(8,128)(2,1)S(1)}, u32[]{:S(2)}, u32[]{:S(2)}) collective-permute-start(bf16[304,864]{1,0:T(8,128)(2,1)} %add_convert_fusion.12), channel_id=1, source_target_pairs={{0,4},{1,5},{2,6},{3,7},{4,0},{5,1},{6,2},{7,3},{8,12},{9,13},{10,... | collective-permute-start | bytes 1575944 | tf_op jit(solution)/shard_map/ppermute | solution.py:50
  524.2 90.0 %collective-permute-start.92 = (bf16[1152,576]{0,1:T(8,128)(2,1)}, bf16[1152,576]{0,1:T(8,128)(2,1)}, u32[]{:S(2)}, u32[]{:S(2)}) collective-permute-start(bf16[1152,576]{0,1:T(8,128)(2,1)} %copy.110), channel_id=1, source_target_pairs={{0,1},{1,0},{2,3},{3,2},{4,5},{5,4},{6,7},{7,6},{8,9},{9,8},{10,11... | collective-permute-start | bytes 3981320 | tf_op jit(solution)/shard_map/ppermute | solution.py:50
  530.4 39.1 %collective-permute-start.59 = (bf16[128,1152]{1,0:T(8,128)(2,1)S(1)}, bf16[128,1152]{1,0:T(8,128)(2,1)S(1)}, u32[]{:S(2)}, u32[]{:S(2)}) collective-permute-start(bf16[128,1152]{1,0:T(8,128)(2,1)S(1)} %slice.818), channel_id=1, source_target_pairs={{0,4},{1,5},{2,6},{3,7},{4,0},{5,1},{6,2},{7,3},{8,12},{9,13},{10,... | collective-permute-start | bytes 884744 | tf_op jit(solution)/shard_map/ppermute | solution.py:50
  546.5 24.4 %collective-permute-start.47 = (bf16[128,1152]{1,0:T(8,128)(2,1)S(1)}, bf16[128,1152]{1,0:T(8,128)(2,1)S(1)}, u32[]{:S(2)}, u32[]{:S(2)}) collective-permute-start(bf16[128,1152]{1,0:T(8,128)(2,1)S(1)} %get-tuple-element.241), channel_id=1, source_target_pairs={{0,4},{1,5},{2,6},{3,7},{4,0},{5,1},{6,2},{7,3},{8,12},{9,13},{10,... | collective-permute-start | bytes 884744 | tf_op jit(solution)/shard_map/ppermute | solution.py:50
  555.6 12.2 %collective-permute-start.62 = (bf16[4,6912]{1,0:T(4,128)(2,1)S(1)}, bf16[4,6912]{1,0:T(4,128)(2,1)S(1)}, u32[]{:S(2)}, u32[]{:S(2)}) collective-permute-start(bf16[4,6912]{1,0:T(4,128)(2,1)S(1)} %add_convert_fusion.20), channel_id=1, source_target_pairs={{0,4},{1,5},{2,6},{3,7},{4,0},{5,1},{6,2},{7,3},{8,12},{9,13},{10,... | collective-permute-start | bytes 165896 | tf_op jit(solution)/shard_map/ppermute | solution.py:50
  592.8 10.5 %collective-permute-start.75 = (bf16[304,864]{1,0:T(8,128)(2,1)}, bf16[304,864]{1,0:T(8,128)(2,1)}, u32[]{:S(2)}, u32[]{:S(2)}) collective-permute-start(bf16[304,864]{1,0:T(8,128)(2,1)} %add_convert_fusion.11), channel_id=1, source_target_pairs={{0,2},{1,3},{2,0},{3,1},{4,6},{5,7},{6,4},{7,5},{8,10},{9,11},{10,... | collective-permute-start | bytes 1575944 | tf_op jit(solution)/shard_map/ppermute | solution.py:50
  592.8 10.5 %collective-permute-start.79 = (bf16[160,1152]{1,0:T(8,128)(2,1)S(1)}, bf16[160,1152]{1,0:T(8,128)(2,1)S(1)}, u32[]{:S(2)}, u32[]{:S(2)}) collective-permute-start(bf16[160,1152]{1,0:T(8,128)(2,1)S(1)} %pad_maximum_fusion.19), channel_id=1, source_target_pairs={{0,8},{8,0},{16,24},{24,16},{1,9},{9,1},{17,25},{25,17},{2,10},{10... | collective-permute-start | bytes 1105928 | tf_op jit(solution)/shard_map/ppermute | solution.py:50
  593.0 10.8 %collective-permute-start.81 = (bf16[160,1152]{1,0:T(8,128)(2,1)S(1)}, bf16[160,1152]{1,0:T(8,128)(2,1)}, u32[]{:S(2)}, u32[]{:S(2)}) collective-permute-start(bf16[160,1152]{1,0:T(8,128)(2,1)S(1)} %pad_maximum_fusion.20), channel_id=1, source_target_pairs={{0,16},{8,24},{16,0},{24,8},{1,17},{9,25},{17,1},{25,9},{2,18},{10... | collective-permute-start | bytes 1105928 | tf_op jit(solution)/shard_map/ppermute | solution.py:50
  603.3 36.7 %collective-permute-start.74 = (bf16[304,864]{1,0:T(8,128)(2,1)}, bf16[304,864]{1,0:T(8,128)(2,1)}, u32[]{:S(2)}, u32[]{:S(2)}) collective-permute-start(bf16[304,864]{1,0:T(8,128)(2,1)} %add_convert_fusion.11), channel_id=1, source_target_pairs={{0,1},{1,0},{2,3},{3,2},{4,5},{5,4},{6,7},{7,6},{8,9},{9,8},{10,11... | collective-permute-start | bytes 1575944 | tf_op jit(solution)/shard_map/ppermute | solution.py:50
  603.3 36.7 %collective-permute-start.76 = (bf16[304,864]{1,0:T(8,128)(2,1)}, bf16[304,864]{1,0:T(8,128)(2,1)}, u32[]{:S(2)}, u32[]{:S(2)}) collective-permute-start(bf16[304,864]{1,0:T(8,128)(2,1)} %collective-permute-done.75), channel_id=1, source_target_pairs={{0,1},{1,0},{2,3},{3,2},{4,5},{5,4},{6,7},{7,6},{8,9},{9,8},{10,11... | collective-permute-start | bytes 1575944 | tf_op jit(solution)/shard_map/ppermute | solution.py:50
  605.0 13.8 %collective-permute-start.82 = (bf16[160,1152]{1,0:T(8,128)(2,1)S(1)}, bf16[160,1152]{1,0:T(8,128)(2,1)}, u32[]{:S(2)}, u32[]{:S(2)}) collective-permute-start(bf16[160,1152]{1,0:T(8,128)(2,1)S(1)} %fusion.36), channel_id=1, source_target_pairs={{0,2},{1,3},{6,4},{7,5},{8,10},{9,11},{14,12},{15,13},{16,18},{17,... | collective-permute-start | bytes 1105928 | tf_op jit(solution)/shard_map/ppermute | solution.py:140
  621.8 18.0 %collective-permute-start.84 = (bf16[160,1152]{1,0:T(8,128)(2,1)S(1)}, bf16[160,1152]{1,0:T(8,128)(2,1)S(1)}, u32[]{:S(2)}, u32[]{:S(2)}) collective-permute-start(bf16[160,1152]{1,0:T(8,128)(2,1)S(1)} %add_convert_fusion.13), channel_id=1, source_target_pairs={{2,0},{3,1},{4,6},{5,7},{10,8},{11,9},{12,14},{13,15},{18,16},{19,... | collective-permute-start | bytes 1105928 | tf_op jit(solution)/shard_map/ppermute | solution.py:144
  (168 other events, 1513.6 us)

commit v2 on v1

v2 whole, which is shorter than its diff:
```python
import functools
import math
import types

import jax
import jax.numpy as jnp
from jax import lax
from jax.experimental import pallas as pl
from jax.experimental.pallas import tpu as pltpu
from jax.sharding import PartitionSpec as P

HEADS = 16
HEAD = 72
DOCS = 4
NORM_EPS = 1e-06
MASKED = -1e30
LOG2E = 1.4426950408889634
SCALE = HEAD ** (-0.5)
VMEM_LIMIT = 56 * 1024 * 1024
HIGHEST = lax.Precision.HIGHEST
BF = jnp.bfloat16
F32 = jnp.float32


def normalize(values):
    center = jnp.mean(values, axis=-1, keepdims=True)
    centred = values - center
    inverse = lax.rsqrt(jnp.mean(centred * centred, axis=-1, keepdims=True) + NORM_EPS)
    return centred * inverse, inverse


def normalize_back(grad, normed, inverse):
    first = jnp.mean(grad, axis=-1, keepdims=True)
    second = jnp.mean(grad * normed, axis=-1, keepdims=True)
    return inverse * (grad - first - normed * second)


def dot_nn(a, b):
    return lax.dot_general(a, b, (((1,), (0,)), ((), ())), preferred_element_type=F32)


def dot_nt(a, b):
    return lax.dot_general(a, b, (((1,), (1,)), ((), ())), preferred_element_type=F32)


def dot_tn(a, b):
    return lax.dot_general(a, b, (((0,), (0,)), ((), ())), preferred_element_type=F32)


def swap(x, axis, mask):
    count = lax.axis_size(axis)
    return lax.ppermute(x, axis, [(i, i ^ mask) for i in range(count)])


def bits_of(low, high):
    out = []
    while low < high:
        out.append(low)
        low *= 2
    return out


def direct(blocks, axis):
    return {m: (b if m == 0 else swap(b, axis, m)) for m, b in blocks.items()}


def spread_dp(x):
    n = lax.axis_size("dp")
    blocks = {0: [x]}
    if n == 4:
        cut = x.shape[0] // 2
        one, two = swap(x, "dp", 1), swap(x, "dp", 2)
        blocks[1], blocks[2] = [one], [two]
        blocks[3] = [swap(one[:cut], "dp", 2), swap(two[cut:], "dp", 1)]
        return [blocks[m] for m in range(n)]
    for bit in bits_of(1, n):
        for mask in list(blocks):
            blocks[mask | bit] = [swap(blocks[mask][0], "dp", bit)]
    return [blocks[m] for m in range(n)]


def line_pairs():
    chips = lax.axis_size("blk") // 2
    mid = chips // 2
    inward = [[(s, s + 1), (chips - 1 - s, chips - 2 - s)] for s in range(mid - 1)]
    outward = [[(mid - 1 - s, mid - 2 - s), (mid + s, mid + s + 1)] for s in range(mid - 1)]
    return inward, [(mid - 1, mid), (mid, mid - 1)], outward


def along(x, pairs):
    return lax.ppermute(x, "blk", [(2 * a + c, 2 * b + c) for a, b in pairs for c in range(2)])


class LineSum:
    def __init__(self, x, name):
        inward, middle, outward = line_pairs()
        self.steps = [("add", p) for p in inward] + [("add", middle)] + [("take", p) for p in outward]
        self.x, self.name, self.at = x, name, 0
        self.got = along(x, self.steps[0][1])

    def step(self):
        kind, pairs = self.steps[self.at]
        if kind == "add":
            self.x = sum_of([self.x, self.got], self.name)
        else:
            self.x = take_from(self.x, self.got, [b for _, b in pairs], self.name)
        self.at += 1
        if self.at < len(self.steps):
            self.got = along(self.x, self.steps[self.at][1])

    def until(self, left):
        while len(self.steps) - self.at > left:
            self.step()


class CubeSum:
    def __init__(self, keep, send, bits, name):
        self.x, self.bits, self.name = keep, bits, name
        self.got = swap(send, "blk", bits[0])

    def fold(self):
        for bit in self.bits[1:]:
            self.x, send = fold_sum([self.x, self.got], bit, self.name)
            self.got = swap(send, "blk", bit)

    def total(self):
        self.x = sum_of([self.x, self.got], self.name)
        self.got = swap(self.x, "blk", self.bits[-1])

    def join(self):
        for i in range(len(self.bits) - 1, 0, -1):
            self.x = join_rows(self.x, self.got, self.bits[i], self.name)
            self.got = swap(self.x, "blk", self.bits[i - 1])


def allowed_mask(dock_ref, docq_ref, width):
    keys = dock_ref[...]
    keys = jnp.concatenate([keys] * (width // keys.shape[1]), axis=1)
    return keys == docq_ref[...]


def attend_kernel(hpd, block, qkv_ref, docq_ref, dock_ref, out_ref, outt_ref, peak_ref, vt_ref):
    i = pl.program_id(0)
    width = hpd * HEAD
    rows = pl.ds(pl.multiple_of(i * block, block), block)

    @pl.when(i == 0)
    def _():
        for h in range(hpd):
            v = qkv_ref[:, 2 * width + h * HEAD : 2 * width + (h + 1) * HEAD]
            vt_ref[h] = v.astype(F32).T.astype(BF)

    allowed = allowed_mask(dock_ref, docq_ref, block)
    outs, peaks = [], []
    for h in range(hpd):
        q = qkv_ref[rows, h * HEAD : (h + 1) * HEAD]
        k = qkv_ref[:, width + h * HEAD : width + (h + 1) * HEAD]
        scores = jnp.where(allowed, dot_nt(k, q), MASKED)
        peak = jnp.max(scores, axis=0, keepdims=True)
        weight = jnp.exp2((scores - peak) * (SCALE * LOG2E))
        total = jnp.sum(weight, axis=0, keepdims=True)
        outs.append(dot_nn(vt_ref[h], weight.astype(BF)) / total)
        peaks.append(peak + jnp.log(total) * (1.0 / SCALE))
    out = jnp.concatenate(outs, axis=0)
    outt_ref[...] = out
    out_ref[...] = out.T.astype(BF)
    peaks.append(jnp.zeros((8 - hpd, block), F32))
    peak_ref[...] = jnp.concatenate(peaks, axis=0)


def attend_back_kernel(
    hpd, block, steps, qkv_ref, do_ref, outt_ref, peak_ref, docq_ref, dock_ref, grad_ref, kt_ref, dk_ref, dv_ref
):
    i = pl.program_id(0)
    width = hpd * HEAD
    rows = pl.ds(pl.multiple_of(i * block, block), block)

    @pl.when(i == 0)
    def _():
        for h in range(hpd):
            k = qkv_ref[:, width + h * HEAD : width + (h + 1) * HEAD]
            kt_ref[h] = k.astype(F32).T.astype(BF)
        dk_ref[...] = jnp.zeros_like(dk_ref)
        dv_ref[...] = jnp.zeros_like(dv_ref)

    allowed = allowed_mask(dock_ref, docq_ref, block)
    dots = do_ref[rows, :].astype(F32).T * outt_ref[...]
    dqs = []
    for h in range(hpd):
        part = slice(h * HEAD, (h + 1) * HEAD)
        q = qkv_ref[rows, part]
        k = qkv_ref[:, width + h * HEAD : width + (h + 1) * HEAD]
        v = qkv_ref[:, 2 * width + h * HEAD : 2 * width + (h + 1) * HEAD]
        do = do_ref[rows, part]
        row_dot = jnp.sum(dots[part], axis=0, keepdims=True)
        scores = jnp.where(allowed, dot_nt(k, q), MASKED)
        probs = jnp.exp2((scores - peak_ref[h : h + 1, :]) * (SCALE * LOG2E))
        grad_scores = (probs * (dot_nt(v, do) - row_dot)).astype(BF)
        dv_ref[h] += dot_nn(probs.astype(BF), do)
        dk_ref[h] += dot_nn(grad_scores, q)
        dqs.append(dot_nn(kt_ref[h], grad_scores))
    grad_ref[rows, :width] = (jnp.concatenate(dqs, axis=0) * SCALE).T.astype(BF)

    @pl.when(i == steps - 1)
    def _():
        dk = jnp.concatenate([dk_ref[h] for h in range(hpd)], axis=1) * SCALE
        dv = jnp.concatenate([dv_ref[h] for h in range(hpd)], axis=1)
        grad_ref[:, width : 2 * width] = dk.astype(BF)
        grad_ref[:, 2 * width :] = dv.astype(BF)


WORK = {"attend": 6, "attend_back": 8, "mlp": 4, "qkv_wgrad": 12, "mod_part": 8}


def params(name, grid, arrays, scratch):
    held = sum(a.size * a.dtype.itemsize for a in arrays) * (1 if grid is None or grid == (1,) else 2)
    held += sum(math.prod(x.shape) * jnp.dtype(x.dtype).itemsize for x in scratch)
    limit = min(VMEM_LIMIT, held + WORK.get(name, 6) * 1024 * 1024)
    return pltpu.CompilerParams(
        vmem_limit_bytes=limit, dimension_semantics=None if grid is None else ("arbitrary",)
    )


LIGHT = pl.CostEstimate(flops=1000, bytes_accessed=1000, transcendentals=0)
VM = pl.BlockSpec(memory_space=pltpu.VMEM)
SM = pl.BlockSpec(memory_space=pltpu.SMEM)
ANY = pl.BlockSpec(memory_space=pl.ANY)


def sds(shape, dtype):
    return jax.ShapeDtypeStruct(shape, dtype)


LAST = []


def launch(name, kernel, args, in_specs, out_specs, out_shape, scratch=(), grid=None):
    count, after = len(args), list(LAST)

    def body(*refs):
        kernel(*refs[:count], *refs[count + len(after) :])

    got = pl.pallas_call(
        body,
        **({} if grid is None else {"grid": grid}),
        in_specs=list(in_specs) + [ANY] * len(after),
        out_specs=list(out_specs),
        out_shape=list(out_shape),
        scratch_shapes=list(scratch),
        compiler_params=params(name, grid, list(args) + list(out_shape), scratch),
        cost_estimate=LIGHT,
        name=name,
    )(*args, *after)
    LAST[:] = [min(got, key=lambda a: a.size)]
    return got


def whole_call(kernel, name, outs, args, scratch=()):
    specs = [SM if a.dtype == jnp.int32 and a.ndim != 2 else VM for a in args]
    return launch(name, kernel, args, specs, [VM] * len(outs), outs, scratch)


CHUNK = 32


def by_rows(count, step):
    def inner(i, carry):
        step(pl.ds(pl.multiple_of(i * CHUNK, CHUNK), CHUNK))
        return carry

    lax.fori_loop(0, count // CHUNK, inner, 0, unroll=2)


def doc_sums(pick, grads):
    high = grads.astype(BF)
    low = (grads - high.astype(F32)).astype(BF)
    return dot_nn(pick, high) + dot_nn(pick, low)


def by_index(index, count, step):
    for i in range(count):

        @pl.when(index == i)
        def _():
            step(i)


def open_kernel(half, cond_ref, bias_ref, qv_ref, lat_ref, cot_ref, lengths_ref, *refs):
    pack_ref, lat_own, cot_own, send_ref, docq_ref, dock_ref, mod_ref, sum_ref = refs
    blk = lax.axis_index("blk")
    micro = blk // half
    group = half
    seg, features = lat_own.shape
    tokens = 2 * seg
    dshard = qv_ref.shape[1]
    cond = jnp.concatenate([cond_ref[0, 0], cond_ref[1, 0]], axis=0).astype(F32)
    silu = cond / (1.0 + jnp.exp(-cond))
    small = jnp.concatenate(
        [bias_ref[...].astype(F32).reshape(1, dshard), qv_ref[0:1, :].astype(F32), qv_ref[1:2, :].astype(F32)], axis=1
    )
    small = jnp.pad(small, ((0, 7), (0, features - 3 * dshard)))
    pack_ref[...] = jnp.concatenate([silu, small], axis=0).astype(BF)
    lat_own[...] = lat_ref[micro, 0]
    cot_own[...] = cot_ref[micro, 0]
    send_ref[:seg, :] = lat_ref[1 - micro, 0]
    send_ref[seg:, :] = cot_ref[1 - micro, 0]
    ends, last = [], 0
    for d in range(DOCS):
        last = last + lengths_ref[micro, 0, d]
        ends.append(last)

    def docs(index, shape, dim):
        spot = lax.broadcasted_iota(jnp.int32, shape, dim) + index * seg
        found = jnp.zeros(shape, jnp.int32)
        for d in range(DOCS):
            found = found + jnp.where(spot >= ends[d], 1, 0)
        return found

    for i in range(group):
        mask = 2 * (i % (group // 2)) + i // (group // 2)
        for part in range(2):
            at = i * tokens + part * seg
            index = (blk ^ mask) ^ (half * part)
            dock_ref[at : at + seg, :] = docs(index, (seg, 128), 0)
            docq_ref[:, at : at + seg] = docs(index, (8, seg), 1)[:1]
    for part in range(2):
        at = part * seg
        index = blk ^ (half * part)
        col = lax.broadcasted_iota(jnp.int32, (seg, 32), 1)
        same = (col % DOCS == docs(index, (seg, 32), 0)) & (col < 3 * DOCS)
        mod_ref[at : at + seg, :] = jnp.where(same, 1.0, 0.0).astype(BF)
        row = lax.broadcasted_iota(jnp.int32, (16, seg), 0)
        same = (row == docs(index, (16, seg), 1)) | (row == DOCS)
        sum_ref[:, at : at + seg] = jnp.where(same, 1.0, 0.0).astype(BF)


def qkv_cols_kernel(group, w_ref, out_ref):
    width = out_ref.shape[1] // 3

    def step(j):
        for p in range(3):
            at = p * group * width + j * width
            out_ref[:, p * width : (p + 1) * width] = w_ref[:, at : at + width]

    by_index(lax.axis_index("blk") % group, group, step)


def cuts_kernel(n, fc1_ref, proj_ref, *outs):
    core = lax.axis_index("blk") % 2
    size = outs[0].shape[0] // 2
    hidden = fc1_ref.shape[1] // n

    def half(ref, cols):
        return jnp.where(core == 0, ref[:size, cols], ref[size:, cols])

    def step(d):
        for m in range(n):
            outs[m][:size, :hidden] = half(fc1_ref, slice((d ^ m) * hidden, ((d ^ m) + 1) * hidden))

    by_index(lax.axis_index("dp"), n, step)
    for m in range(n):
        outs[m][size:, :] = half(proj_ref, slice(None))


def stack_kernel(n, *refs):
    for m in range(n):
        refs[-1][m] = refs[m][...]


def whole_rows(own_ref, other_ref, out_ref, rows, cols):
    dp, core = lax.axis_index("dp"), lax.axis_index("blk") % 2
    n, size = own_ref.shape[0], rows.stop - rows.start
    for k in range(n):
        own, other = own_ref[k ^ dp, rows, cols], other_ref[k ^ dp, rows, cols]
        out_ref[2 * k * size : (2 * k + 1) * size, :] = jnp.where(core == 0, own, other)
        out_ref[(2 * k + 1) * size : (2 * k + 2) * size, :] = jnp.where(core == 0, other, own)


def mod_part_kernel(n, group, *refs):
    packs = refs[:n]
    w_ref, bias_ref = refs[n : n + 2]
    parts = refs[n + 2 : 2 * n + 2]
    cols_ref, projb_ref, qkvb_ref, add_ref, slab_ref = refs[2 * n + 2 :]
    dp, blk = lax.axis_index("dp"), lax.axis_index("blk")
    micro = blk // group
    dshard, span = w_ref.shape[0], bias_ref.shape[0]
    features = dshard * n
    width = features // group
    add_ref[...] = jnp.zeros_like(add_ref)
    bias = jnp.broadcast_to(bias_ref[...].astype(F32).reshape(1, span), (8, span))

    def mine(d):
        add_ref[:, d * span : (d + 1) * span] = bias
        for m in range(n):
            cols_ref[8 * m : 8 * m + 8, :] = packs[m][:8, d * dshard : (d + 1) * dshard].astype(F32)

    by_index(dp, n, mine)
    lhs = []
    for m in range(n):
        slab_ref[m] = packs[m][8:16, :].astype(F32)
        low, high = cols_ref[8 * m : 8 * m + 4, :], cols_ref[8 * m + 4 : 8 * m + 8, :]
        lhs.append(jnp.where(micro == 0, low, high))
    product = dot_nn(jnp.concatenate(lhs, axis=0).astype(BF), w_ref[...])
    for m in range(n):
        parts[m][...] = product[4 * m : 4 * m + 4, :] + add_ref[:4, :]
    rows = [slab_ref[k ^ dp][:1] for k in range(n)]
    projb_ref[...] = jnp.concatenate([r[:, :dshard] for r in rows], axis=1)
    q_bias = jnp.concatenate([r[:, dshard : 2 * dshard] for r in rows], axis=1)
    v_bias = jnp.concatenate([r[:, 2 * dshard : 3 * dshard] for r in rows], axis=1)

    def step(j):
        part = slice(j * width, (j + 1) * width)
        qkvb_ref[...] = jnp.concatenate([q_bias[:, part], jnp.zeros((1, width), F32), v_bias[:, part]], axis=1)

    by_index(blk % group, group, step)


def mod_all_kernel(*refs):
    parts, out_ref = refs[:-1], refs[-1]
    total = parts[0][...]
    for p in parts[1:]:
        total = total + p[...]
    high = total.astype(BF).astype(F32)
    middle = (total - high).astype(BF).astype(F32)
    low = total - high - middle
    blank = jnp.zeros((32 - 3 * DOCS, total.shape[1]), F32)
    out_ref[...] = jnp.concatenate([high, middle, low, blank], axis=0).astype(BF)


def attn_in_kernel(own_ref, got_ref, pick_ref, mod_ref, out_ref, lat_ref, shift_ref, scale_ref):
    seg, features = own_ref.shape
    lat_ref[:seg, :] = own_ref[...]
    lat_ref[seg:, :] = got_ref[:seg, :]
    shift_ref[...] = dot_nn(pick_ref[...], mod_ref[:, :features])
    scale_ref[...] = dot_nn(pick_ref[...], mod_ref[:, features : 2 * features])

    def step(rows):
        normed, _ = normalize(lat_ref[rows, :].astype(F32))
        out_ref[rows, :] = (normed * (1.0 + scale_ref[rows, :]) + shift_ref[rows, :]).astype(BF)

    by_rows(lat_ref.shape[0], step)


def grad_fc2_kernel(own_ref, got_ref, pick_ref, pickt_ref, mod_ref, out_ref, cot_ref, sums_ref):
    seg, features = own_ref.shape
    cot_ref[:seg, :] = own_ref[...]
    cot_ref[seg:, :] = got_ref[seg:, :]
    gate = dot_nn(pick_ref[...], mod_ref[:, 5 * features : 6 * features])
    out_ref[...] = (gate * cot_ref[...].astype(F32)).astype(BF)
    sums_ref[...] = dot_nn(pickt_ref[...], out_ref[...])


def mix_kernel(group, *refs):
    outs = refs[:group]
    own, other, bias_ref, lat_ref, pick_ref, mod_ref = refs[group : group + 6]
    low_ref, proj_ref, mid_ref, in_ref, heads_ref, w_ref, slab_ref, gate_ref, shift_ref, scale_ref = refs[group + 6 :]
    features = lat_ref.shape[1]
    width = features // group
    mine = lax.axis_index("blk") % group
    size = own.shape[1] // 2
    whole_rows(own, other, w_ref, slice(size, 2 * size), slice(0, features))
    for k in range(group):
        heads_ref[k] = w_ref[k * width : (k + 1) * width, :]
    for m in range(group):
        slab_ref[m] = outs[m][...]
    low_ref[...] = jnp.concatenate([slab_ref[k ^ mine] for k in range(group)], axis=1)
    proj_ref[...] = dot_nn(low_ref[...], w_ref[...]) + bias_ref[...]
    gate_ref[...] = dot_nn(pick_ref[...], mod_ref[:, 2 * features : 3 * features])
    shift_ref[...] = dot_nn(pick_ref[...], mod_ref[:, 3 * features : 4 * features])
    scale_ref[...] = dot_nn(pick_ref[...], mod_ref[:, 4 * features : 5 * features])

    def step(rows):
        mid = lat_ref[rows, :].astype(F32) + gate_ref[rows, :] * proj_ref[rows, :]
        mid_ref[rows, :] = mid
        normed, _ = normalize(mid)
        in_ref[rows, :] = (normed * (1.0 + scale_ref[rows, :]) + shift_ref[rows, :]).astype(BF)

    by_rows(lat_ref.shape[0], step)


def turn_kernel(pieces, group, *refs):
    parts = refs[:pieces]
    cot_ref, mid_ref, proj_ref, heads_ref, pick_ref, pickt_ref, mod_ref = refs[pieces : pieces + 7]
    gmid_ref, gproj_ref, sums_ref = refs[pieces + 7 : pieces + 10]
    grads = refs[pieces + 10 : pieces + 10 + group]
    gate_ref, scale_ref, a_ref, b_ref, c_ref = refs[pieces + 10 + group :]
    features = cot_ref.shape[1]
    mine = lax.axis_index("blk") % group
    gate_ref[...] = dot_nn(pick_ref[...], mod_ref[:, 2 * features : 3 * features])
    scale_ref[...] = dot_nn(pick_ref[...], mod_ref[:, 4 * features : 5 * features])

    def step(rows):
        grad_in = parts[0][rows, :].astype(F32)
        for p in parts[1:]:
            grad_in = grad_in + p[rows, :].astype(F32)
        normed, inverse = normalize(mid_ref[rows, :])
        gmid = cot_ref[rows, :].astype(F32) + normalize_back(
            grad_in * (1.0 + scale_ref[rows, :]), normed, inverse
        )
        gmid_ref[rows, :] = gmid
        gproj_ref[rows, :] = (gate_ref[rows, :] * gmid).astype(BF)
        a_ref[rows, :] = gmid * proj_ref[rows, :]
        b_ref[rows, :] = grad_in
        c_ref[rows, :] = grad_in * normed

    by_rows(cot_ref.shape[0], step)
    for m in range(group):
        grads[m][...] = dot_nt(gproj_ref[...], heads_ref[m ^ mine]).astype(BF)
    pick = pickt_ref[...]
    sums_ref[:, :features] = doc_sums(pick, a_ref[...])
    sums_ref[:, features : 2 * features] = doc_sums(pick, b_ref[...])
    sums_ref[:, 2 * features : 3 * features] = doc_sums(pick, c_ref[...])
    sums_ref[:, 3 * features :] = dot_nn(pick, gproj_ref[...])


def outs_kernel(pieces, *refs):
    parts = refs[:pieces]
    cot_ref, mid_ref, pick_ref, pickt_ref, mod_ref, out_ref, low_ref, sums_ref, hold_ref, gate_ref, a_ref = refs[pieces:]
    features = cot_ref.shape[1]
    gate_ref[...] = dot_nn(pick_ref[...], mod_ref[:, 5 * features : 6 * features])

    def step(rows):
        fc2_out = parts[0][rows, :].astype(F32)
        for p in parts[1:]:
            fc2_out = fc2_out + p[rows, :].astype(F32)
        hold_ref[rows, :] = (mid_ref[rows, :] + gate_ref[rows, :] * fc2_out).astype(BF)
        a_ref[rows, :] = cot_ref[rows, :].astype(F32) * fc2_out

    by_rows(cot_ref.shape[0], step)
    seg = out_ref.shape[0]
    out_ref[...] = hold_ref[:seg, :]
    low_ref[...] = hold_ref[seg:, :]
    sums_ref[...] = doc_sums(pickt_ref[...], a_ref[...])


def finish_kernel(starts, seg, *refs):
    pieces = len(starts)
    parts = [r.at[at : at + 2 * seg, :] for r, at in zip(refs, starts)]
    lat_ref, gmid_ref, pick_ref, pickt_ref, mod_ref, out_ref, low_ref, sums_ref, scale_ref, b_ref, c_ref = refs[
        pieces:
    ]
    features = lat_ref.shape[1]
    scale_ref[...] = dot_nn(pick_ref[...], mod_ref[:, features : 2 * features])

    def rows_step(rows):
        grad_in = parts[0][rows, :].astype(F32)
        for p in parts[1:]:
            grad_in = grad_in + p[rows, :].astype(F32)
        normed, inverse = normalize(lat_ref[rows, :].astype(F32))
        b_ref[rows, :] = grad_in
        c_ref[rows, :] = grad_in * normed
        return gmid_ref[rows, :] + normalize_back(grad_in * (1.0 + scale_ref[rows, :]), normed, inverse)

    def step(rows):
        c_rows = rows
        grad = rows_step(c_rows)
        out_ref[rows, :] = grad

    def step_low(rows):
        out = rows_step(pl.ds(pl.multiple_of(rows.start + seg, CHUNK), CHUNK))
        low_ref[rows, :] = out.astype(BF)

    by_rows(seg, step)
    by_rows(seg, step_low)
    pick = pickt_ref[...]
    sums_ref[:, :features] = doc_sums(pick, b_ref[...])
    sums_ref[:, features:] = doc_sums(pick, c_ref[...])


def attend(row_in, qkv_cols, qkv_b, docq, dock, hpd):
    group, block = len(row_in), row_in[0].shape[0]
    features = row_in[0].shape[1]
    length, width = group * block, hpd * HEAD
    n, size = len(qkv_cols), qkv_cols[0][0].shape[0]
    counts = [len(c) for c in qkv_cols]
    qkv_cols = [c for cs in qkv_cols for c in cs]
    fixed = lambda i: (0, 0)

    def kernel(*refs):
        xs = refs[:group]
        ws, refs = grouped(refs[group:], counts)
        b_ref, docq_ref, dock_ref = refs[:3]
        refs = refs[3:]
        qkv_ref, w_ref = refs[:2]
        outs = refs[2 : group + 2]
        outt_ref, peak_ref, vt_ref, out_ref, slab_ref = refs[group + 2 :]
        i = pl.program_id(0)

        @pl.when(i == 0)
        def _():
            for m in range(n):
                place_rows(ws[m], slab_ref.at[m])
            for k in range(n):
                w_ref[k * size : (k + 1) * size, :] = slab_ref[k ^ lax.axis_index("dp")]
            for m in range(group):
                part = dot_nn(xs[m][...], w_ref[...]) + b_ref[...]
                qkv_ref[m * block : (m + 1) * block, :] = part.astype(BF)

        attend_kernel(hpd, block, qkv_ref, docq_ref, dock_ref, out_ref, outt_ref, peak_ref, vt_ref)
        for m in range(group):

            @pl.when(i == m)
            def _():
                outs[m][...] = out_ref[...]

    got = launch(
        "attend",
        kernel,
        [*row_in, *qkv_cols, qkv_b, docq, dock],
        in_specs=[pl.BlockSpec((block, features), fixed) for _ in range(group)]
        + [pl.BlockSpec(c.shape, fixed) for c in qkv_cols]
        + [
            pl.BlockSpec((1, 3 * width), fixed),
            pl.BlockSpec((1, block), lambda i: (0, i)),
            pl.BlockSpec((length, 128), fixed),
        ],
        out_specs=[pl.BlockSpec((length, 3 * width), fixed), pl.BlockSpec((features, 3 * width), fixed)]
        + [pl.BlockSpec((block, width), fixed) for _ in range(group)]
        + [
            pl.BlockSpec((width, block), lambda i: (0, i)),
            pl.BlockSpec((8, block), lambda i: (0, i)),
        ],
        out_shape=[sds((length, 3 * width), BF), sds((features, 3 * width), BF)]
        + [sds((block, width), BF) for _ in range(group)]
        + [sds((width, length), F32), sds((8, length), F32)],
        scratch=[
            pltpu.VMEM((hpd, HEAD, length), BF),
            pltpu.VMEM((block, width), BF),
            pltpu.VMEM((n, size, 3 * width), BF),
        ],
        grid=(group,),
    )
    return got[0], got[2 : 2 + group], got[2 + group], got[3 + group], got[1]


def attend_back(qkv, grad_out, outt, peak, docq, dock, hpd):
    group, block = len(grad_out), grad_out[0].shape[0]
    length, width = group * block, hpd * HEAD
    fixed = lambda i: (0, 0)

    def kernel(qkv_ref, *refs):
        dos = refs[:group]
        outt_ref, peak_ref, docq_ref, dock_ref = refs[group : group + 4]
        grad_ref, kt_ref, dk_ref, dv_ref, do_ref = refs[group + 4 :]

        @pl.when(pl.program_id(0) == 0)
        def _():
            for m in range(group):
                do_ref[m * block : (m + 1) * block, :] = dos[m][...]

        attend_back_kernel(
            hpd, block, group, qkv_ref, do_ref, outt_ref, peak_ref, docq_ref, dock_ref, grad_ref, kt_ref, dk_ref, dv_ref
        )

    return launch(
        "attend_back",
        kernel,
        [qkv, *grad_out, outt, peak, docq, dock],
        in_specs=[pl.BlockSpec((length, 3 * width), fixed)]
        + [pl.BlockSpec((block, width), fixed) for _ in range(group)]
        + [
            pl.BlockSpec((width, block), lambda i: (0, i)),
            pl.BlockSpec((8, block), lambda i: (0, i)),
            pl.BlockSpec((1, block), lambda i: (0, i)),
            pl.BlockSpec((length, 128), fixed),
        ],
        out_specs=[pl.BlockSpec((length, 3 * width), fixed)],
        out_shape=[sds((length, 3 * width), BF)],
        scratch=[
            pltpu.VMEM((hpd, HEAD, length), BF),
            pltpu.VMEM((hpd, length, HEAD), F32),
            pltpu.VMEM((hpd, length, HEAD), F32),
            pltpu.VMEM((length, width), BF),
        ],
        grid=(group,),
    )[0]


def place_rows(pieces, ref):
    at = 0
    for p in pieces:
        ref[at : at + p.shape[0], :] = p[...]
        at += p.shape[0]


def mlp_kernel(xs, gs, per, refs):
    n = len(xs)
    w_own, w_other, b1_ref, w2_ref, b2_ref = refs[:5]
    act_ref, gf1_ref, sums_ref = refs[5:8]
    backs, parts = refs[8 : 8 + n], refs[8 + n : 8 + 2 * n]
    w1_ref, x_ref, g_ref, back_ref, part_ref, row_ref = refs[8 + 2 * n :]
    i = pl.program_id(0)
    hidden = w1_ref.shape[1]
    block = x_ref.shape[0] // per

    @pl.when(i == 0)
    def _():
        size = w_own.shape[1] // 2
        whole_rows(w_own, w_other, w1_ref, slice(0, size), slice(0, hidden))
        sums_ref[...] = jnp.zeros_like(sums_ref)
        row_ref[...] = jnp.zeros_like(row_ref)
        span = b2_ref.shape[0]

        def bias(d):
            row_ref[0:1, d * span : (d + 1) * span] = b2_ref[...].astype(F32).reshape(1, span)

        by_index(lax.axis_index("dp"), n, bias)

    for m in range(n):

        @pl.when(i == m // per)
        def _():
            at = pl.ds(m % per * block, block)
            place_rows(xs[m], x_ref.at[at, :])
            place_rows(gs[m], g_ref.at[at, :])

    u = dot_nn(x_ref[...], w1_ref[...]) + b1_ref[...].astype(F32).reshape(1, hidden)
    root = 0.7978845608028654
    squared = u * u
    t = jnp.tanh(root * u * (1.0 + 0.044715 * squared))
    act = (0.5 * u * (1.0 + t)).astype(BF)
    act_ref[...] = act
    slope = 0.5 * (1.0 + t) + 0.5 * u * (1.0 - t * t) * (root * (1.0 + 3 * 0.044715 * squared))
    gf1 = (dot_nt(g_ref[...], w2_ref[...]) * slope).astype(BF)
    gf1_ref[...] = gf1
    back_ref[...] = dot_nt(gf1, w1_ref[...]).astype(BF)
    part_ref[...] = (dot_nn(act, w2_ref[...]) + row_ref[0:1, :]).astype(BF)
    for m in range(n):

        @pl.when(i == m // per)
        def _():
            at = slice(m % per * block, (m % per + 1) * block)
            parts[m][...] = part_ref[at, :]
            backs[m][...] = back_ref[at, :]

    sums_ref[0:1, :hidden] += jnp.sum(gf1.astype(F32), axis=0, keepdims=True)


def grouped(refs, counts):
    out, at = [], 0
    for count in counts:
        out.append(refs[at : at + count])
        at += count
    return out, refs[at:]


def mlp(xs, gs, w_own, w_other, b1, w2, b2):
    n = len(xs)
    block, features = sum(p.shape[0] for p in xs[0]), xs[0][0].shape[1]
    hidden = w2.shape[0]
    per = min(4, n)
    fixed = lambda i: (0, 0)
    piece = pl.BlockSpec((block, features), fixed)
    third = pl.BlockSpec(w_own.shape, lambda i: (0, 0, 0))
    flat = [p for ps in list(xs) + list(gs) for p in ps]
    counts = [len(ps) for ps in list(xs) + list(gs)]

    def kernel(*refs):
        pieces, rest = grouped(refs, counts)
        mlp_kernel(pieces[:n], pieces[n:], per, rest)

    got = launch(
        "mlp",
        kernel,
        flat + [w_own, w_other, b1, w2, b2],
        in_specs=[pl.BlockSpec(p.shape, fixed) for p in flat]
        + [third, third, pl.BlockSpec((hidden,), lambda i: (0,)), pl.BlockSpec((hidden, features), fixed)]
        + [pl.BlockSpec(b2.shape, lambda i: (0,))],
        out_specs=[
            pl.BlockSpec((per * block, hidden), lambda i: (i, 0)),
            pl.BlockSpec((per * block, hidden), lambda i: (i, 0)),
            pl.BlockSpec((8, features), fixed),
        ]
        + [piece] * (2 * n),
        out_shape=[
            sds((n * block, hidden), BF),
            sds((n * block, hidden), BF),
            sds((8, features), F32),
        ]
        + [sds((block, features), BF)] * (2 * n),
        scratch=[
            pltpu.VMEM((features, hidden), BF),
            pltpu.VMEM((per * block, features), BF),
            pltpu.VMEM((per * block, features), BF),
            pltpu.VMEM((per * block, features), BF),
            pltpu.VMEM((per * block, features), BF),
            pltpu.VMEM((8, features), F32),
        ],
        grid=(n // per,),
    )
    return got[:3], got[3 : n + 3], got[n + 3 :]


def wgrad(lefts, rights, name):
    rows, cols = lefts[0].shape[1], rights[0].shape[1]
    block = 384 if rows % 384 == 0 else rows

    def kernel(*refs):
        a_refs, b_refs = refs[: len(lefts)], refs[len(lefts) : -1]

        left = jnp.concatenate([r[...] for r in a_refs], axis=0)
        right = jnp.concatenate([r[...] for r in b_refs], axis=0)
        refs[-1][...] = dot_tn(left, right).astype(BF)

    return launch(
        name,
        kernel,
        list(lefts) + list(rights),
        in_specs=[pl.BlockSpec((a.shape[0], block), lambda i: (0, i)) for a in lefts]
        + [pl.BlockSpec(b.shape, lambda i: (0, 0)) for b in rights],
        out_specs=[pl.BlockSpec((block, cols), lambda i: (i, 0))],
        out_shape=[sds((rows, cols), BF)],
        grid=(rows // block,),
    )[0]


def core_rows(ref, groups, k, mine):
    core = lax.axis_index("blk") % 2
    size = ref.shape[0] // (2 * groups)
    low = ref[2 * k * size : (2 * k + 1) * size, :]
    high = ref[(2 * k + 1) * size : (2 * k + 2) * size, :]
    return jnp.where(core == 0, low, high) if mine else jnp.where(core == 0, high, low)


def other_half(x, groups, name):
    rows, cols = x.shape
    size = rows // (2 * groups)

    def kernel(x_ref, out_ref):
        for k in range(groups):
            out_ref[k * size : (k + 1) * size, :] = core_rows(x_ref, groups, k, False)

    return whole_call(kernel, name, [sds((rows // 2, cols), BF)], [x])[0]


def halves(total, bit):
    size = total.shape[0] // 2
    mine = (lax.axis_index("blk") // bit) % 2
    low, high = total[:size], total[size:]
    return jnp.where(mine == 0, low, high), jnp.where(mine == 0, high, low)


def own_half(x, got, groups, bit, name):
    rows, cols = x.shape
    size = rows // (2 * groups)

    def kernel(x_ref, got_ref, keep_ref, send_ref, all_ref):
        for k in range(groups):
            at = slice(k * size, (k + 1) * size)
            mine = core_rows(x_ref, groups, k, True).astype(F32)
            all_ref[at, :] = (mine + got_ref[at, :].astype(F32)).astype(BF)
        keep_ref[...], send_ref[...] = halves(all_ref[...], bit)

    return whole_call(
        kernel, name, [sds((rows // 4, cols), BF)] * 2, [x, got], [pltpu.VMEM((rows // 2, cols), BF)]
    )


def own_blocks(x, got, n, name):
    rows, cols = x.shape
    size = rows // (2 * n)

    def kernel(x_ref, got_ref, *outs):
        def step(d):
            for m in range(n):
                k = m ^ d
                mine = core_rows(x_ref, n, k, True).astype(F32)
                outs[m][...] = (mine + got_ref[k * size : (k + 1) * size, :].astype(F32)).astype(BF)

        by_index(lax.axis_index("dp"), n, step)

    return whole_call(kernel, name, [sds((size, cols), BF)] * n, [x, got])


def give_back(own, other, name):
    seg, features = own.shape

    def kernel(own_ref, other_ref, out_ref):
        micro = lax.axis_index("blk") // (lax.axis_size("blk") // 2)
        out_ref[micro, 0] = own_ref[...]
        out_ref[1 - micro, 0] = other_ref[...].astype(out_ref.dtype)

    return whole_call(kernel, name, [sds((2, 1, seg, features), own.dtype)], [own, other])[0]


def add_up(refs):
    total = refs[0][...].astype(F32)
    for r in refs[1:]:
        total = total + r[...].astype(F32)
    return total


def fold_sum(parts, bit, name):
    def kernel(*refs):
        keep, send = halves(add_up(refs[:-2]), bit)
        refs[-2][...], refs[-1][...] = keep.astype(BF), send.astype(BF)

    rows, cols = parts[0].shape
    return whole_call(kernel, name, [sds((rows // 2, cols), BF)] * 2, list(parts))


def join_rows(own, got, bit, name):
    def kernel(own_ref, got_ref, out_ref):
        low = (lax.axis_index("blk") // bit) % 2 == 0
        size = own_ref.shape[0]
        out_ref[:size, :] = jnp.where(low, own_ref[...], got_ref[...])
        out_ref[size:, :] = jnp.where(low, got_ref[...], own_ref[...])

    return whole_call(kernel, name, [sds((2 * own.shape[0], own.shape[1]), BF)], [own, got])[0]


def join_blocks(own, got, bit, n, name):
    rows, cols = 2 * own.shape[0], own.shape[1]
    size = rows // n

    def kernel(own_ref, got_ref, *refs):
        outs, all_ref = refs[:-1], refs[-1]
        low = (lax.axis_index("blk") // bit) % 2 == 0
        half = own_ref.shape[0]
        all_ref[:half, :] = jnp.where(low, own_ref[...], got_ref[...])
        all_ref[half:, :] = jnp.where(low, got_ref[...], own_ref[...])

        def step(d):
            for m in range(n):
                outs[m][...] = all_ref[(m ^ d) * size : ((m ^ d) + 1) * size, :]

        by_index(lax.axis_index("dp"), n, step)

    return whole_call(kernel, name, [sds((size, cols), BF)] * n, [own, got], [pltpu.VMEM((rows, cols), BF)])


def sum_of(parts, name, dtype=BF):
    def kernel(*refs):
        refs[-1][...] = add_up(refs[:-1]).astype(dtype)

    return whole_call(kernel, name, [sds(parts[0].shape, dtype)], list(parts))[0]


def take_from(x, got, chips, name):
    def kernel(x_ref, got_ref, out_ref):
        chip = lax.axis_index("blk") // 2
        here = functools.reduce(jnp.logical_or, [chip == c for c in chips])
        out_ref[...] = jnp.where(here, got_ref[...].astype(F32), x_ref[...].astype(F32)).astype(BF)

    return whole_call(kernel, name, [sds(x.shape, BF)], [x, got])[0]


def sum_at(parts, count, name):
    def kernel(*refs):
        refs[-1][...] = add_up([r.at[at : at + count, :] for r, (_, at) in zip(refs, parts)]).astype(BF)

    shape = sds((count, parts[0][0].shape[1]), BF)
    return whole_call(kernel, name, [shape], [x for x, _ in parts])[0]


def qkv_wgrad_kernel(n, group, *refs):
    xs, grad_ref = refs[:group], refs[group]
    outs = refs[group + 1 : group + 1 + n]
    bias_ref, acc_ref = refs[group + 1 + n :]
    block, features = xs[0].shape
    size, width = features // n, grad_ref.shape[1] // 3
    mine = lax.axis_index("dp")
    step = 384 if features % 384 == 0 else features
    for at in range(0, features, step):
        total = dot_tn(xs[0][:, at : at + step], grad_ref[:block, :])
        for m in range(1, group):
            total = total + dot_tn(xs[m][:, at : at + step], grad_ref[m * block : (m + 1) * block, :])
        acc_ref[at : at + step, :] = total
    for m in range(n):
        rows = pl.ds(pl.multiple_of((m ^ mine) * size, size), size)
        outs[m][...] = acc_ref[rows, :].astype(BF)
    total = dot_nn(jnp.ones((8, block * group), BF), grad_ref[...])
    bias_ref[...] = jnp.zeros_like(bias_ref)

    def place(j):
        bias_ref[:, j * width : (j + 1) * width] = total[:, :width]
        bias_ref[:, features + j * width : features + (j + 1) * width] = total[:, 2 * width :]

    by_index(lax.axis_index("blk") % group, group, place)


def place_qkv_kernel(group, *refs):
    parts = refs[:group]
    out_ref, slab_ref = refs[group:]
    mine = lax.axis_index("blk") % group
    size = parts[0].shape[1] // 3
    for m in range(group):
        slab_ref[m] = parts[m][...]
    for j in range(group):
        got = slab_ref[j ^ mine].astype(F32)
        for p in range(3):
            at = p * group * size + j * size
            out_ref[:, at : at + size] = got[:, p * size : (p + 1) * size]


def both_cores(own, other):
    core = lax.axis_index("blk") % 2
    return jnp.where(core == 0, own, other), jnp.where(core == 0, other, own)


def place_fc1(own, other, name):
    n = len(own)
    size, cols = own[0].shape
    wide = n if cols % 128 else 1

    def kernel(*refs):
        out_ref = refs[-1]
        for t in range(wide):
            at = slice(t * cols, (t + 1) * cols)

            def step(k):
                low, high = both_cores(refs[k][...].astype(F32), refs[n + k][...].astype(F32))
                out_ref[:size, at] = low
                out_ref[size:, at] = high

            by_index((pl.program_id(0) * wide + t) ^ lax.axis_index("dp"), n, step)

    piece = pl.BlockSpec((size, cols), lambda j: (0, 0))
    return launch(
        name,
        kernel,
        list(own) + list(other),
        [piece] * (2 * n),
        [pl.BlockSpec((2 * size, wide * cols), lambda j: (0, j))],
        [sds((2 * size, n * cols), F32)],
        grid=(n // wide,),
    )[0]


def both_kernel(half, own_ref, got_ref, out_ref):
    first = lax.axis_index("blk") // half == 0
    own, got = own_ref[...].astype(F32), got_ref[...].astype(F32)
    out_ref[...] = jnp.concatenate([jnp.where(first, own, got), jnp.where(first, got, own)], axis=0).astype(BF)


def add_kernel(a_ref, b_ref, out_ref):
    out_ref[...] = (a_ref[...].astype(F32) + b_ref[...].astype(F32)).astype(out_ref.dtype)


def place_cores_kernel(own_ref, other_ref, out_ref):
    size = out_ref.shape[0] // 2
    low, high = both_cores(own_ref[...].astype(F32), other_ref[...].astype(F32))
    out_ref[:size, :] = low
    out_ref[size:, :] = high


def gather_sums_kernel(in_ref, mid_ref, out_ref, fc1_ref, fc2_ref, qv_ref, all_ref):
    features = out_ref.shape[1]
    all_ref[...] = jnp.zeros_like(all_ref)
    all_ref[:DOCS, : 2 * features] = in_ref[:DOCS, :]
    all_ref[:DOCS, 2 * features : 5 * features] = mid_ref[:DOCS, : 3 * features]
    all_ref[:DOCS, 5 * features :] = out_ref[:DOCS, :]
    row = slice(DOCS, DOCS + 1)
    all_ref[row, :features] = fc1_ref[0:1, :]
    all_ref[row, features : 2 * features] = fc2_ref[row, :]
    all_ref[row, 2 * features : 3 * features] = mid_ref[row, 3 * features :]
    all_ref[row, 3 * features : 5 * features] = qv_ref[0:1, :]


def ada_kernel(n, *refs):
    slots = refs[:n]
    cols_ref, w_ref = refs[n : n + 2]
    wgrad_ref, rows_ref = refs[n + 2 : n + 4]
    conds = refs[n + 4 :]
    got, fc1, rest = [], 0.0, 0.0
    for m in range(n):
        got.append(slots[m][:DOCS, :].astype(F32))
        got.append(slots[m][8 : 8 + DOCS, :].astype(F32))
        bias = slots[m][DOCS : DOCS + 1, :].astype(F32) + slots[m][8 + DOCS : 9 + DOCS, :].astype(F32)
        fc1 = bias if m == 0 else fc1
        rest = rest + bias
    got = jnp.concatenate(got, axis=0)
    rows_ref[...] = jnp.concatenate(
        [jnp.sum(got, axis=0, keepdims=True), rest, fc1, jnp.zeros((5, rest.shape[1]), F32)], axis=0
    )
    got = got.astype(BF)
    wgrad_ref[...] = dot_tn(cols_ref[...].astype(BF), got)
    back = dot_nt(got, w_ref[...])
    first = pl.program_id(0) == 0
    for m in range(n):
        part = back[8 * m : 8 * m + 8, :]
        conds[m][...] = part + jnp.where(first, 0.0, conds[m][...])


def ada(slots, cols, weight):
    n = len(slots)
    dshard, span = weight.shape
    block = span // 6
    return launch(
        "ada",
        functools.partial(ada_kernel, n),
        [*slots, cols, weight],
        in_specs=[pl.BlockSpec((16, block), lambda i: (0, i))] * n
        + [pl.BlockSpec(cols.shape, lambda i: (0, 0)), pl.BlockSpec((dshard, block), lambda i: (0, i))],
        out_specs=[pl.BlockSpec((dshard, block), lambda i: (0, i)), pl.BlockSpec((8, block), lambda i: (0, i))]
        + [pl.BlockSpec((8, dshard), lambda i: (0, 0))] * n,
        out_shape=[sds((dshard, span), F32), sds((8, span), F32)] + [sds((8, dshard), F32)] * n,
        grid=(6,),
    )


def biases_kernel(n, rows_ref, ada_ref, qv_ref, proj_ref, fc1_ref, fc2_ref):
    features = rows_ref.shape[1] // 6
    span, size = ada_ref.shape[0], fc2_ref.shape[0]

    def step(d):
        def part(i):
            at = i * features + d * size
            return rows_ref[1:2, at : at + size]

        ada_ref[...] = rows_ref[0:1, d * span : (d + 1) * span].reshape(span)
        fc2_ref[...] = part(1).reshape(size)
        proj_ref[...] = part(2).reshape(size)
        qv_ref[0:1, :] = part(3)
        qv_ref[1:2, :] = part(4)

    by_index(lax.axis_index("dp"), n, step)
    fc1_ref[...] = rows_ref[2:3, : fc1_ref.shape[0]].reshape(fc1_ref.shape[0])


def cond_kernel(n, *refs):
    parts, cond_ref, out_ref, slab_ref = refs[:n], refs[n], refs[n + 1], refs[n + 2]
    dp = lax.axis_index("dp")
    for m in range(n):
        slab_ref[m] = parts[m][...]
    grad = jnp.concatenate([slab_ref[k ^ dp] for k in range(n)], axis=1)
    for u in range(2):
        cond = cond_ref[u, 0].astype(F32)
        sig = 1.0 / (1.0 + jnp.exp(-cond))
        out_ref[u, 0] = grad[u * DOCS : (u + 1) * DOCS] * (sig * (1.0 + cond * (1.0 - sig)))


def local(
    latents,
    conditions,
    doc_lengths,
    cotangent,
    ada_weight,
    ada_bias,
    qkv_weight,
    qv_bias,
    proj_weight,
    proj_bias,
    fc1_weight,
    fc1_bias,
    fc2_weight,
    fc2_bias,
):
    n_dp, n_blk = lax.axis_size("dp"), lax.axis_size("blk")
    dp, blk = lax.axis_index("dp"), lax.axis_index("blk")
    half = n_blk // 2
    group = half
    core, micro = blk % 2, blk // half
    seg, features = latents.shape[2], latents.shape[3]
    hidden = fc1_weight.shape[1] // n_dp
    dshard = features // n_dp
    hpd = HEADS // group
    width = hpd * HEAD
    hhalf, dhalf = hidden // 2, dshard // 2
    tokens = 2 * seg
    LAST.clear()
    masks = [2 * i for i in range(group // 2)] + [2 * i + 1 for i in range(group // 2)]

    act_shape = sds((tokens, features), BF)
    half_shape = sds((seg, features), BF)
    full_shape = sds((tokens, features), F32)
    sums_shape = sds((16, features), F32)
    full_vmem = pltpu.VMEM((tokens, features), F32)
    v = types.SimpleNamespace()
    chip_bits = bits_of(2, n_blk)

    def step_open():
        v.pack, v.lat_own, v.cot_own, across, v.docq, v.dock, v.pick_mod, v.pick_sum = whole_call(
            functools.partial(open_kernel, half),
            "open",
            [sds((16, features), BF)]
            + [half_shape, half_shape, act_shape]
            + [
                sds((1, group * tokens), jnp.int32),
                sds((group * tokens, 128), jnp.int32),
                sds((tokens, 32), BF),
                sds((16, tokens), BF),
            ],
            [conditions, proj_bias, qv_bias, latents, cotangent, doc_lengths],
        )
        v.across = swap(across, "blk", half)
        v.pack = direct({m: v.pack for m in range(n_dp)}, "dp")

    def step_qkv_cols():
        (cols,) = whole_call(
            functools.partial(qkv_cols_kernel, group), "qkv_cols", [sds((dshard, 3 * width), BF)], [qkv_weight]
        )
        v.qkv_cols = spread_dp(cols)

    def step_mod_part():
        *parts, v.cond_cols, v.proj_b, v.qkv_bias = whole_call(
            functools.partial(mod_part_kernel, n_dp, group),
            "mod_part",
            [sds((DOCS, 6 * features), F32)] * n_dp
            + [sds((8 * n_dp, dshard), F32), sds((1, features), F32), sds((1, 3 * width), F32)],
            [v.pack[m] for m in range(n_dp)] + [ada_weight, ada_bias],
            [pltpu.VMEM((8, 6 * features), F32), pltpu.VMEM((n_dp, 8, features), F32)],
        )
        v.mod_parts = direct(dict(enumerate(parts)), "dp")

    def step_mod_all():
        parts = [v.mod_parts[m] for m in range(n_dp)]
        (v.mod,) = whole_call(mod_all_kernel, "mod_all", [sds((32, 6 * features), BF)], parts)

    def step_attn_in():
        attn_in, v.latent = whole_call(
            attn_in_kernel,
            "attn_in",
            [act_shape] * 2,
            [v.lat_own, v.across, v.pick_mod, v.mod],
            [full_vmem] * 2,
        )
        rows = {0: attn_in}
        for bit in bits_of(2, group):
            for m in list(rows):
                rows[m | bit] = swap(rows[m], "blk", bit)
        for m in list(rows):
            rows[m | 1] = swap(rows[m], "blk", 1)
        v.row_in = [rows[m] for m in masks]

    def step_grad_fc2():
        grad_fc2, v.cot, v.sums_fc2 = whole_call(
            grad_fc2_kernel,
            "grad_fc2",
            [act_shape, act_shape, sums_shape],
            [v.cot_own, v.across, v.pick_mod, v.pick_sum, v.mod],
        )
        v.all_grad = spread_dp(grad_fc2)

    def step_cuts():
        move = whole_call(
            functools.partial(cuts_kernel, n_dp),
            "cuts",
            [sds((2 * dhalf, features), BF)] * n_dp,
            [fc1_weight, proj_weight],
        )
        v.move = direct(dict(enumerate(move)), "dp")

    def step_attend():
        v.qkv, outs, v.outt, v.peak, v.qkv_w = attend(
            v.row_in, v.qkv_cols, v.qkv_bias, v.docq, v.dock, hpd
        )
        v.outs = direct(dict(zip(masks, outs)), "blk")

    def step_stack():
        (v.move_own,) = whole_call(
            functools.partial(stack_kernel, n_dp),
            "stack",
            [sds((n_dp, 2 * dhalf, features), BF)],
            [v.move[m] for m in range(n_dp)],
        )
        v.move_other = swap(v.move_own, "blk", 1)

    def step_mix():
        v.low, v.attn_proj, v.mid, mlp_in, v.proj_w = whole_call(
            functools.partial(mix_kernel, group),
            "mix",
            [act_shape, full_shape, full_shape, act_shape, sds((group, width, features), BF)],
            [v.outs[m] for m in range(group)]
            + [v.move_own, v.move_other, v.proj_b, v.latent, v.pick_mod, v.mod],
            [pltpu.VMEM((features, features), BF), pltpu.VMEM((group, tokens, width), BF)] + [full_vmem] * 3,
        )
        v.all_in = spread_dp(mlp_in)

    def step_mlp():
        (v.act, v.grad_fc1, v.sums_fc1), back, part = mlp(
            v.all_in, v.all_grad, v.move_own, v.move_other, fc1_bias, fc2_weight, fc2_bias
        )
        v.back = direct(dict(enumerate(back)), "dp")
        v.part = direct(dict(enumerate(part)), "dp")

    def flat(pieces):
        return [p for ps in pieces for p in ps]

    def step_fc2_wgrad():
        v.fc2_g = wgrad([v.act], flat(v.all_grad), "fc2_wgrad")

    def step_fc1_wgrad():
        v.fc1_g = wgrad(flat(v.all_in), [v.grad_fc1], "fc1_wgrad")

    def step_turn():
        v.gmid, v.grad_proj, v.sums_mid, *grad_attn = whole_call(
            functools.partial(turn_kernel, n_dp, group),
            "turn",
            [full_shape, act_shape, sds((16, 4 * features), F32)] + [sds((tokens, width), BF)] * group,
            [v.back[m] for m in range(n_dp)]
            + [v.cot, v.mid, v.attn_proj, v.proj_w, v.pick_mod, v.pick_sum, v.mod],
            [full_vmem] * 5,
        )
        v.grad_attn = direct(dict(enumerate(grad_attn)), "blk")

    def step_proj_wgrad():
        v.proj_g = wgrad([v.low], [v.grad_proj], "proj_wgrad")

    def halve(x, groups, name):
        return swap(other_half(x, groups, name), "blk", 1)

    def step_fc2_other():
        v.fc2_got = halve(v.fc2_g, 1, "fc2_other")

    def step_fc1_other():
        v.fc1_got = halve(v.fc1_g, n_dp, "fc1_other")

    def step_proj_other():
        v.proj_got = halve(v.proj_g, n_dp, "proj_other")

    def step_fc2_own():
        v.fc2 = CubeSum(*own_half(v.fc2_g, v.fc2_got, 1, chip_bits[0], "fc2_own"), chip_bits, "fc2_cube")

    def step_fc1_own():
        v.fc1 = CubeSum(*own_half(v.fc1_g, v.fc1_got, n_dp, chip_bits[0], "fc1_own"), chip_bits, "fc1_cube")

    def step_fc2_a():
        v.fc2.fold()

    def step_fc2_b():
        v.fc2.total()

    def step_fc2_j():
        v.fc2.join()

    def step_fc1_a():
        v.fc1.fold()

    def step_fc1_b():
        v.fc1.total()

    def step_fc1_j():
        v.fc1.join()

    def step_proj_a():
        v.proj.until(2)

    def step_proj_b():
        v.proj.until(1)

    def step_fc2_c():
        v.fc2_own = join_rows(v.fc2.x, v.fc2.got, chip_bits[0], "fc2_cube")
        v.fc2_other = swap(v.fc2_own, "blk", 1)

    def step_fc1_c():
        blocks = join_blocks(v.fc1.x, v.fc1.got, chip_bits[0], n_dp, "fc1_cube")
        blocks = direct(dict(enumerate(blocks)), "dp")
        v.fc1_own = [blocks[m] for m in range(n_dp)]
        v.fc1_other = [swap(x, "blk", 1) for x in v.fc1_own]

    def step_proj_blocks():
        v.proj_parts = direct(
            dict(enumerate(own_blocks(v.proj_g, v.proj_got, n_dp, "proj_blocks"))), "dp"
        )

    def step_proj_sum():
        v.proj = LineSum(sum_of([v.proj_parts[m] for m in range(n_dp)], "proj_sum"), "proj_line")

    def step_proj_c():
        v.proj.until(0)
        v.proj_other = swap(v.proj.x, "blk", 1)

    def step_attend_back():
        grad_qkv = attend_back(
            v.qkv, [v.grad_attn[m] for m in masks], v.outt, v.peak, v.docq, v.dock, hpd
        )
        v.grad_qkv = grad_qkv
        count = (group // 2) * tokens
        send = swap(dot_nt(grad_qkv[count:], v.qkv_w).astype(BF), "blk", 1)
        keep = dot_nt(grad_qkv[:count], v.qkv_w).astype(BF)
        v.blocks = {m: [(keep, i * tokens), (send, i * tokens)] for i, m in enumerate(masks[: group // 2])}

    def step_qkv_wgrad():
        *qkv_g, v.sums_qv = whole_call(
            functools.partial(qkv_wgrad_kernel, n_dp, group),
            "qkv_wgrad",
            [sds((dshard, 3 * width), BF)] * n_dp + [sds((8, 2 * features), F32)],
            v.row_in + [v.grad_qkv],
            [pltpu.VMEM((features, 3 * width), F32)],
        )
        v.qkv_g = direct(dict(enumerate(qkv_g)), "dp")

    def step_outs():
        v.block_own, other, v.sums_out = whole_call(
            functools.partial(outs_kernel, n_dp),
            "outs",
            [half_shape, half_shape, sums_shape],
            [v.part[m] for m in range(n_dp)] + [v.cot, v.mid, v.pick_mod, v.pick_sum, v.mod],
            [pltpu.VMEM((tokens, features), BF)] + [full_vmem] * 2,
        )
        v.block_other = swap(other, "blk", half)

    def step_attn_sum():
        blocks = v.blocks
        for bit in reversed(bits_of(2, group)):
            for m in [m for m in blocks if m & bit]:
                blocks[m ^ bit].append((swap(sum_at(blocks.pop(m), tokens, "attn_sum"), "blk", bit), 0))

    def step_finish():
        parts = v.blocks[0]
        v.latent_own, other, v.sums_in = whole_call(
            functools.partial(finish_kernel, [at for _, at in parts], seg),
            "finish",
            [sds((seg, features), F32), half_shape, sds((16, 2 * features), F32)],
            [x for x, _ in parts] + [v.latent, v.gmid, v.pick_mod, v.pick_sum, v.mod],
            [full_vmem] * 3,
        )
        v.latent_other = swap(other, "blk", half)

    def step_qkv_sum():
        v.qkv_x = sum_of([v.qkv_g[m] for m in range(n_dp)], "qkv_sum")
        v.qkv_got = swap(v.qkv_x, "blk", half)

    def step_qkv_sum2():
        parts = {0: sum_of([v.qkv_x, v.qkv_got], "qkv_sum")}
        for bit in bits_of(2, group):
            for m in list(parts):
                parts[m | bit] = swap(parts[m], "blk", bit)
        for m in list(parts):
            parts[m | 1] = swap(parts[m], "blk", 1)
        v.qkv_parts = parts

    def step_gather_sums():
        (v.sums,) = whole_call(
            gather_sums_kernel,
            "gather_sums",
            [sds((8, 6 * features), F32)],
            [v.sums_in, v.sums_mid, v.sums_out, v.sums_fc1, v.sums_fc2, v.sums_qv],
        )
        v.sums_got = swap(v.sums, "blk", 1)

    def step_sums_c():
        for bit in bits_of(2, group):
            (v.sums,) = whole_call(add_kernel, "sums", [sds(v.sums.shape, BF)], [v.sums, v.sums_got])
            v.sums_got = swap(v.sums, "blk", bit)

    def step_sums_g():
        (v.sums,) = whole_call(add_kernel, "sums", [sds(v.sums.shape, BF)], [v.sums, v.sums_got])
        v.sums_got = swap(v.sums, "blk", half)

    def step_sums_h():
        (both,) = whole_call(
            functools.partial(both_kernel, half), "both", [sds((16, 6 * features), BF)], [v.sums, v.sums_got]
        )
        v.slots = direct({m: both for m in range(n_dp)}, "dp")

    def step_ada():
        v.ada_wgrad, v.rows_sum, *parts = ada([v.slots[m] for m in range(n_dp)], v.cond_cols, ada_weight)
        v.cond_parts = direct(dict(enumerate(parts)), "dp")

    def step_biases():
        spans = [ada_bias.shape, (2, dshard), (dshard,), (hidden,), (dshard,)]
        v.ada_bgrad, v.qv_bgrad, v.proj_bgrad, v.fc1_bgrad, v.fc2_bgrad = whole_call(
            functools.partial(biases_kernel, n_dp), "biases", [sds(x, F32) for x in spans], [v.rows_sum]
        )

    def step_cond():
        (v.cond_grad,) = whole_call(
            functools.partial(cond_kernel, n_dp),
            "cond_grad",
            [sds((2, 1, DOCS, features), F32)],
            [v.cond_parts[m] for m in range(n_dp)] + [conditions],
            [pltpu.VMEM((n_dp, 8, dshard), F32)],
        )

    def step_place_qkv():
        (v.qkv_wgrad,) = whole_call(
            functools.partial(place_qkv_kernel, group),
            "place_qkv",
            [sds((dshard, 3 * features), F32)],
            [v.qkv_parts[m] for m in range(group)],
            [pltpu.VMEM((group, dshard, 3 * width), BF)],
        )

    def step_place_fc2():
        (v.fc2_wgrad,) = whole_call(
            place_cores_kernel, "place_fc2", [sds((hidden, features), F32)], [v.fc2_own, v.fc2_other]
        )

    def step_place_proj():
        (v.proj_wgrad,) = whole_call(
            place_cores_kernel, "place_proj", [sds((dshard, features), F32)], [v.proj.x, v.proj_other]
        )

    def step_place_fc1():
        v.fc1_wgrad = place_fc1(v.fc1_own, v.fc1_other, "place_fc1")

    def step_block_out():
        v.block_out = give_back(v.block_own, v.block_other, "block_out")

    def step_latent_grad():
        v.latent_grad = give_back(v.latent_own, v.latent_other, "latent_grad")

    for step in (
        step_open, step_qkv_cols, step_mod_part, step_cuts, step_mod_all, step_attn_in, step_attend, step_grad_fc2,
        step_stack, step_mix, step_mlp, step_fc2_wgrad, step_fc1_wgrad, step_turn, step_fc2_other, step_fc2_own,
        step_fc1_other, step_attend_back, step_attn_sum, step_fc2_a, step_fc1_own, step_qkv_wgrad, step_finish,
        step_proj_wgrad, step_outs, step_fc2_b, step_gather_sums, step_qkv_sum, step_sums_c, step_fc1_a,
        step_fc2_j, step_sums_g, step_proj_other, step_proj_blocks, step_fc1_b, step_proj_sum, step_sums_h,
        step_fc2_c, step_ada, step_qkv_sum2, step_proj_a, step_place_fc2, step_fc1_j, step_fc1_c, step_biases, step_cond,
        step_proj_b, step_place_qkv, step_latent_grad, step_proj_c, step_place_fc1, step_place_proj,
        step_block_out,
    ):
        step()

    return (
        v.block_out,
        v.latent_grad,
        v.cond_grad,
        v.ada_wgrad,
        v.ada_bgrad,
        v.qkv_wgrad,
        v.qv_bgrad,
        v.proj_wgrad,
        v.proj_bgrad,
        v.fc1_wgrad,
        v.fc1_bgrad,
        v.fc2_wgrad,
        v.fc2_bgrad,
    )


def solution(mesh):
    in_specs = (
        P(None, "dp", "blk", None),
        P(None, "dp", None, None),
        P(None, "dp", None),
        P(None, "dp", "blk", None),
        P("dp", None),
        P("dp"),
        P("dp", None),
        P(None, "dp"),
        P("dp", None),
        P("dp"),
        P("dp", None),
        P("dp"),
        P("dp", None),
        P("dp"),
    )
    out_specs = (
        P(None, "dp", "blk", None),
        P(None, "dp", "blk", None),
        P(None, "dp", None, None),
        P("dp", None),
        P("dp"),
        P("dp", None),
        P(None, "dp"),
        P("dp", None),
        P("dp"),
        P("dp", None),
        P("dp"),
        P("dp", None),
        P("dp"),
    )
    return jax.shard_map(local, mesh=mesh, in_specs=in_specs, out_specs=out_specs, check_vma=False)
```

time: 663 us -> 411 us (0.62)
  other arithmetic: 102 us -> 0 us
  local copies, waits for them, and re-layouts: 109 us -> 25.2 us
  matrix products: 50 us -> 3.11 us
  Pallas kernels: 58.8 us -> 101 us
  waiting for transfers between devices: 225 us -> 185 us
  starting transfers between devices: 105 us -> 91.4 us
    ppermute x9 -> x3, waiting for transfers between devices: 55.5 us -> 0.01 us  [along(): lax.ppermute(x, 'blk', [(2 * a + c, 2 * b + c) for a, b in pairs for c in...]
    pallas_call x4 -> x53, Pallas kernels: 58.8 us -> 101 us  [launch(): pl.pallas_call(body, **{} if grid is None else {'grid': grid}, in_specs=l...]
    dot_general x9 -> x0, matrix products: 42.1 us -> none  [the longest x5 26.5 us: dot_tn(): lax.dot_general(a, b, (((0,), (0,)), ((), ())), preferred_element_type=F32)]
    convert_element_type x30 -> x0, other arithmetic: 34.3 us -> none  [the longest x11 12.6 us: add(): return (a.astype(F32) + b.astype(F32)).astype(BF)]
    reduce_sum x17 -> x0, other arithmetic: 24.9 us -> none  [the longest x7 13 us: local(): fc2_bsum = jnp.sum(all_grad.astype(F32), axis=0, keepdims=True)]
    slice x36 -> x6, local copies, waits for them, and re-layouts: 19.3 us -> 0.14 us  [spread_dp(): blocks[3] = [swap(one[:cut], 'dp', 2), swap(two[cut:], 'dp', 1)]]
    convert_element_type x9 -> x0, local copies, waits for them, and re-layouts: 16.4 us -> none  [the longest x4 6.02 us: local(): dot_nt(grad_proj, proj_x[m * width:(m + 1) * width]).astype(BF)]
    ppermute x88 -> x81, waiting for transfers between devices: 170 us -> 185 us  [swap(): return lax.ppermute(x, axis, [(i, i ^ mask) for i in range(count)])]
  transfers between devices with their start and end apart: 97 -> 84, of which waited for: 36 -> 43; matrix products, arithmetic and copies ran while one was open for 34% -> 0% of each run, Pallas kernels for 6% -> 15%
where the time goes in v2:
time: 411 us; the launch traced here: 407 us
  waiting for transfers between devices  185 us (45%)
  Pallas kernels  101 us (25%)
  starting transfers between devices  91.4 us (22%)
  local copies, waits for them, and re-layouts  25.2 us (6%)
    ppermute x81, waiting for transfers between devices, swap(): return lax.ppermute(x, axis, [(i, i ^ mask) for i in range(count)])  185 us
    pallas_call x53, Pallas kernels, launch(): pl.pallas_call(body, **{} if grid is None else {'grid': grid}, in_specs=l...  101 us
    ppermute x81, starting transfers between devices, swap(): return lax.ppermute(x, axis, [(i, i ^ mask) for i in range(count)])  84.8 us
    unnamed x86, local copies, waits for them, and re-layouts  25.1 us
  transfers between devices with their start and end apart: 84, of which 43 were waited for; matrix products, arithmetic and copies ran while one was open for 0% of the time, Pallas kernels for 15%

profile of v2, /device:TPU:0, one launch (start us, length us, event | category | flops | bytes accessed | tf_op | source)
XLA Modules:
  0.0 407.2 jit_solution(5694517315728297058)
XLA Ops:
  6.4 4.1 %collective-permute-start = (bf16[256,1152]{1,0:T(8,128)(2,1)S(1)}, bf16[256,1152]{1,0:T(8,128)(2,1)S(1)}, u32[]{:S(2)}, u32[]{:S(2)}) collective-permute-start(bf16[256,1152]{1,0:T(8,128)(2,1)S(1)} %get-tuple-element.107), channel_id=1, source_target_pairs={{0,4},{1,5},{2,6},{3,7},{4,0},{5,1},{6,2},{7,3},{8,12},{9,13},{10,... | collective-permute-start | bytes 1769480 | tf_op jit(solution)/shard_map/ppermute | solution.py:52
  10.5 2.4 collective-permute-start.3
  17.4 2.1 copy-done.2
  24.0 2.4 collective-permute-done.4.refs_1_
  28.7 1.9 collective-permute-done.5.refs_2_
  30.6 7.3 %collective-permute-done.6.refs_3_ = f32[4,6912]{1,0:T(4,128)S(1)} collective-permute-done((f32[4,6912]{1,0:T(4,128)S(1)}, f32[4,6912]{1,0:T(4,128)S(1)}, u32[]{:S(2)}, u32[]{:S(2)}) %collective-permute-start.6) | collective-permute-done | bytes 110624 | tf_op jit(solution)/shard_map/ppermute | solution.py:52
  45.4 5.0 %collective-permute-done.13.refs_8_ = bf16[144,864]{1,0:T(8,128)(2,1)S(1)} collective-permute-done((bf16[144,864]{1,0:T(8,128)(2,1)S(1)}, bf16[144,864]{1,0:T(8,128)(2,1)S(1)}, u32[]{:S(2)}, u32[]{:S(2)}) %collective-permute-start.13) | collective-permute-done | bytes 248864 | tf_op jit(solution)/shard_map/ppermute | solution.py:52
  50.4 1.8 collective-permute-start.19
  55.0 16.4 %attend.1 = (bf16[1024,864]{1,0:T(8,128)(2,1)S(1)}, bf16[1152,864]{1,0:T(8,128)(2,1)S(1)}, bf16[256,288]{1,0:T(8,128)(2,1)S(1)}, bf16[256,288]{1,0:T(8,128)(2,1)...) custom-call(bf16[256,1152]{1,0:T(8,128)(2,1)S(1)} %get-tuple-element, ...), custom_call_target="tpu_custom_call" | custom-call | flops 1000 | bytes 1000 | tf_op jit(solution)/shard_map/attend/pallas_call | solution.py:243
  80.1 1.8 collective-permute-done.14.refs_1_
  83.0 1.9 collective-permute-done.15.refs_2_
  84.9 2.5 collective-permute-done.16.refs_3_
  87.4 2.6 mix.1
  95.8 2.3 collective-permute-done.25.refs_6_.refs_2_
  99.7 7.4 %collective-permute-done.22.refs_2_ = bf16[256,1152]{1,0:T(8,128)(2,1)S(1)} collective-permute-done((bf16[256,1152]{1,0:T(8,128)(2,1)S(1)}, bf16[256,1152]{1,0:T(8,128)(2,1)S(1)}, u32[]{:S(2)}, u32[]{:S(2)}) %collective-permute-start.22) | collective-permute-done | bytes 589856 | tf_op jit(solution)/shard_map/ppermute | solution.py:52
  108.3 2.4 collective-permute-done.21.refs_1_
  112.3 4.7 %collective-permute-done.28.refs_9_.refs_5_ = bf16[128,1152]{1,0:T(8,128)(2,1)S(1)} collective-permute-done((bf16[128,1152]{1,0:T(8,128)(2,1)S(1)}, bf16[128,1152]{1,0:T(8,128)(2,1)S(1)}, u32[]{:S(2)}, u32[]{:S(2)}) %collective-permute-start.28) | collective-permute-done | bytes 294944 | tf_op jit(solution)/shard_map/ppermute | solution.py:52
  117.0 5.5 %collective-permute-done.24.refs_4_ = bf16[128,1152]{1,0:T(8,128)(2,1)S(1)} collective-permute-done((bf16[128,1152]{1,0:T(8,128)(2,1)S(1)}, bf16[128,1152]{1,0:T(8,128)(2,1)S(1)}, u32[]{:S(2)}, u32[]{:S(2)}) %collective-permute-start.24) | collective-permute-done | bytes 294944 | tf_op jit(solution)/shard_map/ppermute | solution.py:52
  123.7 17.6 %mlp.1 = (bf16[1024,1152]{1,0:T(8,128)(2,1)S(1)}, bf16[1024,1152]{1,0:T(8,128)(2,1)S(1)}, f32[8,1152]{1,0:T(8,128)S(1)}, bf16[256,1152]{1,0:T(8,128)(2,1)S(1)}, ...) custom-call(bf16[256,1152]{1,0:T(8,128)(2,1)S(1)} %copy-done.12, ...), custom_call_target="tpu_custom_call" | custom-call | flops 1000 | bytes 1000 | tf_op jit(solution)/shard_map/mlp/pallas_call | solution.py:243
  144.8 4.2 %fc2_wgrad.1.refs_6_.refs_0_ = bf16[1152,1152]{1,0:T(8,128)(2,1)S(1)} custom-call(bf16[1024,1152]{1,0:T(8,128)(2,1)S(1)} %get-tuple-element.148.refs_0_, bf16[256,1152]{1,0:T(8,128)(2,1)S(1)} %copy-done.10, bf16[256,1152]{1,0:T(8,128)(2,1)S(1)} %collective-permute-done.25.refs_6_.refs_2_, bf16[256,1152]{1,0:T(8,128)(2,1)S(1)} %collective-permute-done.26.refs_7_.refs_3_, ...), custom_call_target="tpu_custom_call" | custom-call | flops 1000 | bytes 1000 | tf_op jit(solution)/shard_map/fc2_wgrad/pallas_call | solution.py:243
  149.1 4.0 fc1_wgrad.1.refs_11_.refs_0_
  153.1 4.5 %collective-permute-done.32.refs_1_ = bf16[256,1152]{1,0:T(8,128)(2,1)S(1)} collective-permute-done((bf16[256,1152]{1,0:T(8,128)(2,1)S(1)}, bf16[256,1152]{1,0:T(8,128)(2,1)S(1)}, u32[]{:S(2)}, u32[]{:S(2)}) %collective-permute-start.32) | collective-permute-done | bytes 589856 | tf_op jit(solution)/shard_map/ppermute | solution.py:52
  157.6 10.3 %collective-permute-done.33.refs_2_ = bf16[256,1152]{1,0:T(8,128)(2,1)S(1)} collective-permute-done((bf16[256,1152]{1,0:T(8,128)(2,1)S(1)}, bf16[256,1152]{1,0:T(8,128)(2,1)S(1)}, u32[]{:S(2)}, u32[]{:S(2)}) %collective-permute-start.33) | collective-permute-done | bytes 589856 | tf_op jit(solution)/shard_map/ppermute | solution.py:52
  169.5 4.1 turn.1
  174.4 1.7 collective-permute-start.37
  178.0 3.6 collective-permute-done.35.refs_2_
  181.6 3.3 collective-permute-done.37.refs_4_
  185.0 15.2 %attend_back.1.refs_2_.refs_4_ = bf16[1024,864]{1,0:T(8,128)(2,1)S(1)} custom-call(bf16[1024,864]{1,0:T(8,128)(2,1)S(1)} %copy-done.23, bf16[256,288]{1,0:T(8,128)(2,1)S(1)} %get-tuple-element.152.refs_1_, bf16[256,288]{1,0:T(8,128)(2,1)S(1)} %collective-permute-done.35.refs_2_, bf16[256,288]{1,0:T(8,128)(2,1)S(1)} %collective-permute-done.36.refs_3_, ...), custom_call_target="tpu_custom_call" | custom-call | flops 1000 | bytes 1000 | tf_op jit(solution)/shard_map/attend_back/pallas_call | solution.py:243
  207.9 11.5 %collective-permute-done.42.refs_1_ = bf16[288,1152]{1,0:T(8,128)(2,1)S(1)} collective-permute-done((bf16[288,1152]{1,0:T(8,128)(2,1)S(1)}, bf16[288,1152]{1,0:T(8,128)(2,1)S(1)}, u32[]{:S(2)}, u32[]{:S(2)}) %collective-permute-start.42) | collective-permute-done | bytes 663584 | tf_op jit(solution)/shard_map/ppermute | solution.py:52
  220.8 3.3 qkv_wgrad.1
  225.1 3.4 collective-permute-start.44
  229.5 2.4 collective-permute-start.51
  233.8 9.0 %collective-permute-done.40.refs_2_ = bf16[256,1152]{1,0:T(8,128)(2,1)S(1)} collective-permute-done((bf16[256,1152]{1,0:T(8,128)(2,1)S(1)}, bf16[256,1152]{1,0:T(8,128)(2,1)S(1)}, u32[]{:S(2)}, u32[]{:S(2)}) %collective-permute-start.40) | collective-permute-done | bytes 589856 | tf_op jit(solution)/shard_map/ppermute | solution.py:52
  242.8 1.7 collective-permute-start.48
  244.5 2.2 finish.1
  249.8 5.2 %collective-permute-done.47.refs_2_ = bf16[288,864]{1,0:T(8,128)(2,1)S(1)} collective-permute-done((bf16[288,864]{1,0:T(8,128)(2,1)S(1)}, bf16[288,864]{1,0:T(8,128)(2,1)S(1)}, u32[]{:S(2)}, u32[]{:S(2)}) %collective-permute-start.47) | collective-permute-done | bytes 497696 | tf_op jit(solution)/shard_map/ppermute | solution.py:52
  256.8 7.0 %collective-permute-done.51.refs_1_ = bf16[288,1152]{1,0:T(8,128)(2,1)S(1)} collective-permute-done((bf16[288,1152]{1,0:T(8,128)(2,1)S(1)}, bf16[288,1152]{1,0:T(8,128)(2,1)S(1)}, u32[]{:S(2)}, u32[]{:S(2)}) %collective-permute-start.51) | collective-permute-done | bytes 663584 | tf_op jit(solution)/shard_map/ppermute | solution.py:52
  265.2 2.4 collective-permute-start.63
  273.1 16.4 %collective-permute-done.56.refs_1_ = bf16[144,1152]{1,0:T(8,128)(2,1)S(1)} collective-permute-done((bf16[144,1152]{1,0:T(8,128)(2,1)S(1)}, bf16[144,1152]{1,0:T(8,128)(2,1)S(1)}, u32[]{:S(2)}, u32[]{:S(2)}) %collective-permute-start.56) | collective-permute-done | bytes 331808 | tf_op jit(solution)/shard_map/ppermute | solution.py:52
  289.5 3.4 collective-permute-start.59
  293.2 4.9 %collective-permute-done.59.refs_1_ = bf16[8,6912]{1,0:T(8,128)(2,1)S(1)} collective-permute-done((bf16[8,6912]{1,0:T(8,128)(2,1)S(1)}, bf16[8,6912]{1,0:T(8,128)(2,1)S(1)}, u32[]{:S(2)}, u32[]{:S(2)}) %collective-permute-start.59) | collective-permute-done | bytes 110624 | tf_op jit(solution)/shard_map/ppermute | solution.py:52
  298.9 1.7 collective-permute-start.62
  302.4 5.7 %collective-permute-done.62.refs_3_ = bf16[16,6912]{1,0:T(8,128)(2,1)S(1)} collective-permute-done((bf16[16,6912]{1,0:T(8,128)(2,1)S(1)}, bf16[16,6912]{1,0:T(8,128)(2,1)S(1)}, u32[]{:S(2)}, u32[]{:S(2)}) %collective-permute-start.62) | collective-permute-done | bytes 221216 | tf_op jit(solution)/shard_map/ppermute | solution.py:52
  308.1 4.6 %collective-permute-start.57 = (bf16[144,1152]{1,0:T(8,128)(2,1)S(1)}, bf16[144,1152]{1,0:T(8,128)(2,1)S(1)}, u32[]{:S(2)}, u32[]{:S(2)}) collective-permute-start(bf16[144,1152]{1,0:T(8,128)(2,1)S(1)} %proj_sum.1.refs_2_.refs_0_), channel_id=1, source_target_pairs={{0,2},{1,3},{6,4},{7,5},{8,10},{9,11},{14,12},{15,13},{16,18},{17,... | collective-permute-start | bytes 995336 | tf_op jit(solution)/shard_map/ppermute | solution.py:91
  312.8 1.8 collective-permute-start.68
  314.6 5.4 %ada.1 = (f32[288,6912]{1,0:T(8,128)}, f32[8,6912]{1,0:T(8,128)S(1)}, f32[8,288]{1,0:T(8,128)S(1)}, f32[8,288]{1,0:T(8,128)S(1)}, f32[8,288]{1,0:T(8,128)S(1)}, /*index=5*/f32[8,288]{1,0:T(8,128)S(1)}) custom-call(bf16[16,6912]{1,0:T(8,128)(2,1)S(1)} %both.1.refs_2_.refs_0_, bf16[16,6912]{1,0:T(8,128)(2,1)S(1)} %collective-permute-done.60.refs_1_, ...), custom_call_target="tpu_custom_call" | custom-call | flops 1000 | bytes 1000 | tf_op jit(solution)/shard_map/ada/pallas_call | solution.py:243
  320.0 11.7 %collective-permute-done.58.refs_1_ = bf16[288,864]{1,0:T(8,128)(2,1)S(1)} collective-permute-done((bf16[288,864]{1,0:T(8,128)(2,1)S(1)}, bf16[288,864]{1,0:T(8,128)(2,1)S(1)}, u32[]{:S(2)}, u32[]{:S(2)}) %collective-permute-start.58) | collective-permute-done | bytes 497696 | tf_op jit(solution)/shard_map/ppermute | solution.py:52
  332.1 3.1 place_fc2.1.refs_2_
  335.1 3.8 collective-permute-done.68.refs_1_
  338.9 2.5 copy-done
  341.7 8.3 %collective-permute-done.74.refs_2_ = bf16[288,864]{1,0:T(8,128)(2,1)S(1)} collective-permute-done((bf16[288,864]{1,0:T(8,128)(2,1)S(1)}, bf16[288,864]{1,0:T(8,128)(2,1)S(1)}, u32[]{:S(2)}, u32[]{:S(2)}) %collective-permute-start.74) | collective-permute-done | bytes 497696 | tf_op jit(solution)/shard_map/ppermute | solution.py:52
  351.4 2.9 collective-permute-done.65.refs_1_
  355.2 2.9 collective-permute-done.66.refs_2_
  358.1 2.2 collective-permute-start.72
  360.3 3.8 collective-permute-done.70.refs_1_
  364.2 1.7 collective-permute-start.67
  366.9 1.9 collective-permute-done.67.refs_3_
  373.7 1.7 collective-permute-start.79
  376.8 2.7 place_qkv.1.refs_2_
  379.5 2.1 copy-done.4
  383.2 3.4 collective-permute-done.78.refs_2_
  389.0 2.9 place_fc1.1.refs_2_
  391.9 2.5 copy-done.1
  395.6 9.1 %collective-permute-done.43.refs_1_ = bf16[128,1152]{1,0:T(8,128)(2,1)S(1)} collective-permute-done((bf16[128,1152]{1,0:T(8,128)(2,1)S(1)}, bf16[128,1152]{1,0:T(8,128)(2,1)S(1)}, u32[]{:S(2)}, u32[]{:S(2)}) %collective-permute-start.43) | collective-permute-done | bytes 294944 | tf_op jit(solution)/shard_map/ppermute | solution.py:52
  (251 shorter events, 100.9 us)
Async XLA Ops:
  6.4 31.6 %collective-permute-start = (bf16[256,1152]{1,0:T(8,128)(2,1)S(1)}, bf16[256,1152]{1,0:T(8,128)(2,1)S(1)}, u32[]{:S(2)}, u32[]{:S(2)}) collective-permute-start(bf16[256,1152]{1,0:T(8,128)(2,1)S(1)} %get-tuple-element.107), channel_id=1, source_target_pairs={{0,4},{1,5},{2,6},{3,7},{4,0},{5,1},{6,2},{7,3},{8,12},{9,13},{10,... | collective-permute-start | bytes 1769480 | tf_op jit(solution)/shard_map/ppermute | solution.py:52
  15.8 25.3 %collective-permute-start.11 = (bf16[288,864]{1,0:T(8,128)(2,1)S(1)}, bf16[288,864]{1,0:T(8,128)(2,1)S(1)}, u32[]{:S(2)}, u32[]{:S(2)}) collective-permute-start(bf16[288,864]{1,0:T(8,128)(2,1)S(1)} %qkv_cols.1.refs_6_.refs_4_), channel_id=1, source_target_pairs={{0,16},{8,24},{16,0},{24,8},{1,17},{9,25},{17,1},{25,9},{2,18},{10... | collective-permute-start | bytes 1493000 | tf_op jit(solution)/shard_map/ppermute | solution.py:52
  21.9 20.2 %collective-permute-start.10 = (bf16[288,864]{1,0:T(8,128)(2,1)S(1)}, bf16[288,864]{1,0:T(8,128)(2,1)S(1)}, u32[]{:S(2)}, u32[]{:S(2)}) collective-permute-start(bf16[288,864]{1,0:T(8,128)(2,1)S(1)} %qkv_cols.1.refs_6_.refs_4_), channel_id=1, source_target_pairs={{0,8},{8,0},{16,24},{24,16},{1,9},{9,1},{17,25},{25,17},{2,10},{10... | collective-permute-start | bytes 1493000 | tf_op jit(solution)/shard_map/ppermute | solution.py:52
  22.4 8.2 %collective-permute-start.5 = (f32[4,6912]{1,0:T(4,128)S(1)}, f32[4,6912]{1,0:T(4,128)S(1)}, u32[]{:S(2)}, u32[]{:S(2)}) collective-permute-start(f32[4,6912]{1,0:T(4,128)S(1)} %get-tuple-element.113), channel_id=1, source_target_pairs={{0,16},{8,24},{16,0},{24,8},{1,17},{9,25},{17,1},{25,9},{2,18},{10... | collective-permute-start | bytes 331784 | tf_op jit(solution)/shard_map/ppermute | solution.py:52
  26.4 11.6 %collective-permute-start.6 = (f32[4,6912]{1,0:T(4,128)S(1)}, f32[4,6912]{1,0:T(4,128)S(1)}, u32[]{:S(2)}, u32[]{:S(2)}) collective-permute-start(f32[4,6912]{1,0:T(4,128)S(1)} %get-tuple-element.114), channel_id=1, source_target_pairs={{0,24},{8,16},{16,8},{24,0},{1,25},{9,17},{17,9},{25,1},{2,26},{10... | collective-permute-start | bytes 331784 | tf_op jit(solution)/shard_map/ppermute | solution.py:52
  39.5 13.0 %collective-permute-start.7 = (bf16[256,1152]{1,0:T(8,128)(2,1)S(1)}, bf16[256,1152]{1,0:T(8,128)(2,1)S(1)}, u32[]{:S(2)}, u32[]{:S(2)}) collective-permute-start(bf16[256,1152]{1,0:T(8,128)(2,1)S(1)} %get-tuple-element.117.refs_0_.refs_12_), channel_id=1, source_target_pairs={{0,2},{1,3},{2,0},{3,1},{4,6},{5,7},{6,4},{7,5},{8,10},{9,11},{10,... | collective-permute-start | bytes 1769480 | tf_op jit(solution)/shard_map/ppermute | solution.py:52
  41.1 9.2 %collective-permute-start.13 = (bf16[144,864]{1,0:T(8,128)(2,1)S(1)}, bf16[144,864]{1,0:T(8,128)(2,1)S(1)}, u32[]{:S(2)}, u32[]{:S(2)}) collective-permute-start(bf16[144,864]{1,0:T(8,128)(2,1)S(1)} %slice.33), channel_id=1, source_target_pairs={{0,8},{8,0},{16,24},{24,16},{1,9},{9,1},{17,25},{25,17},{2,10},{10... | collective-permute-start | bytes 746504 | tf_op jit(solution)/shard_map/ppermute | solution.py:52
  42.1 10.0 %collective-permute-start.12 = (bf16[144,864]{1,0:T(8,128)(2,1)S(1)}, bf16[144,864]{1,0:T(8,128)(2,1)S(1)}, u32[]{:S(2)}, u32[]{:S(2)}) collective-permute-start(bf16[144,864]{1,0:T(8,128)(2,1)S(1)} %slice.32), channel_id=1, source_target_pairs={{0,16},{8,24},{16,0},{24,8},{1,17},{9,25},{17,1},{25,9},{2,18},{10... | collective-permute-start | bytes 746504 | tf_op jit(solution)/shard_map/ppermute | solution.py:52
  43.6 31.6 %collective-permute-start.17 = (bf16[288,1152]{1,0:T(8,128)(2,1)S(1)}, bf16[288,1152]{1,0:T(8,128)(2,1)S(1)}, u32[]{:S(2)}, u32[]{:S(2)}) collective-permute-start(bf16[288,1152]{1,0:T(8,128)(2,1)S(1)} %get-tuple-element.123), channel_id=1, source_target_pairs={{0,8},{8,0},{16,24},{24,16},{1,9},{9,1},{17,25},{25,17},{2,10},{10... | collective-permute-start | bytes 1990664 | tf_op jit(solution)/shard_map/ppermute | solution.py:52
  44.2 32.2 %collective-permute-start.18 = (bf16[288,1152]{1,0:T(8,128)(2,1)S(1)}, bf16[288,1152]{1,0:T(8,128)(2,1)S(1)}, u32[]{:S(2)}, u32[]{:S(2)}) collective-permute-start(bf16[288,1152]{1,0:T(8,128)(2,1)S(1)} %get-tuple-element.124), channel_id=1, source_target_pairs={{0,16},{8,24},{16,0},{24,8},{1,17},{9,25},{17,1},{25,9},{2,18},{10... | collective-permute-start | bytes 1990664 | tf_op jit(solution)/shard_map/ppermute | solution.py:52
  50.4 26.0 %collective-permute-start.19 = (bf16[288,1152]{1,0:T(8,128)(2,1)S(1)}, bf16[288,1152]{1,0:T(8,128)(2,1)S(1)}, u32[]{:S(2)}, u32[]{:S(2)}) collective-permute-start(bf16[288,1152]{1,0:T(8,128)(2,1)S(1)} %get-tuple-element.125), channel_id=1, source_target_pairs={{0,24},{8,16},{16,8},{24,0},{1,25},{9,17},{17,9},{25,1},{2,26},{10... | collective-permute-start | bytes 1990664 | tf_op jit(solution)/shard_map/ppermute | solution.py:52
  76.6 10.8 %collective-permute-start.20 = (bf16[4,288,1152]{2,1,0:T(8,128)(2,1)S(1)}, bf16[4,288,1152]{2,1,0:T(8,128)(2,1)S(1)}, u32[]{:S(2)}, u32[]{:S(2)}) collective-permute-start(bf16[4,288,1152]{2,1,0:T(8,128)(2,1)S(1)} %stack.1.refs_4_.refs_10_), channel_id=1, source_target_pairs={{0,1},{1,0},{2,3},{3,2},{4,5},{5,4},{6,7},{7,6},{8,9},{9,8},{10,11... | collective-permute-start | bytes 7962632 | tf_op jit(solution)/shard_map/ppermute | solution.py:52
  77.5 9.9 %collective-permute-start.16 = (bf16[256,288]{1,0:T(8,128)(2,1)S(1)}, bf16[256,288]{1,0:T(8,128)(2,1)S(1)}, u32[]{:S(2)}, u32[]{:S(2)}) collective-permute-start(bf16[256,288]{1,0:T(8,128)(2,1)S(1)} %get-tuple-element.122), channel_id=1, source_target_pairs={{0,3},{1,2},{2,1},{3,0},{4,7},{5,6},{6,5},{7,4},{8,11},{9,10},{10,... | collective-permute-start | bytes 442376 | tf_op jit(solution)/shard_map/ppermute | solution.py:52
  78.6 15.9 %collective-permute-start.26 = (bf16[256,1152]{1,0:T(8,128)(2,1)S(1)}, bf16[256,1152]{1,0:T(8,128)(2,1)S(1)}, u32[]{:S(2)}, u32[]{:S(2)}) collective-permute-start(bf16[256,1152]{1,0:T(8,128)(2,1)S(1)} %get-tuple-element.133.refs_5_.refs_1_), channel_id=1, source_target_pairs={{0,16},{8,24},{16,0},{24,8},{1,17},{9,25},{17,1},{25,9},{2,18},{10... | collective-permute-start | bytes 1769480 | tf_op jit(solution)/shard_map/ppermute | solution.py:52
  81.9 16.2 %collective-permute-start.25 = (bf16[256,1152]{1,0:T(8,128)(2,1)S(1)}, bf16[256,1152]{1,0:T(8,128)(2,1)S(1)}, u32[]{:S(2)}, u32[]{:S(2)}) collective-permute-start(bf16[256,1152]{1,0:T(8,128)(2,1)S(1)} %get-tuple-element.133.refs_5_.refs_1_), channel_id=1, source_target_pairs={{0,8},{8,0},{16,24},{24,16},{1,9},{9,1},{17,25},{25,17},{2,10},{10... | collective-permute-start | bytes 1769480 | tf_op jit(solution)/shard_map/ppermute | solution.py:52
  90.9 16.2 %collective-permute-start.22 = (bf16[256,1152]{1,0:T(8,128)(2,1)S(1)}, bf16[256,1152]{1,0:T(8,128)(2,1)S(1)}, u32[]{:S(2)}, u32[]{:S(2)}) collective-permute-start(bf16[256,1152]{1,0:T(8,128)(2,1)S(1)} %get-tuple-element.132.refs_0_), channel_id=1, source_target_pairs={{0,16},{8,24},{16,0},{24,8},{1,17},{9,25},{17,1},{25,9},{2,18},{10... | collective-permute-start | bytes 1769480 | tf_op jit(solution)/shard_map/ppermute | solution.py:52
  92.5 18.2 %collective-permute-start.21 = (bf16[256,1152]{1,0:T(8,128)(2,1)S(1)}, bf16[256,1152]{1,0:T(8,128)(2,1)S(1)}, u32[]{:S(2)}, u32[]{:S(2)}) collective-permute-start(bf16[256,1152]{1,0:T(8,128)(2,1)S(1)} %get-tuple-element.132.refs_0_), channel_id=1, source_target_pairs={{0,8},{8,0},{16,24},{24,16},{1,9},{9,1},{17,25},{25,17},{2,10},{10... | collective-permute-start | bytes 1769480 | tf_op jit(solution)/shard_map/ppermute | solution.py:52
  94.6 22.5 %collective-permute-start.28 = (bf16[128,1152]{1,0:T(8,128)(2,1)S(1)}, bf16[128,1152]{1,0:T(8,128)(2,1)S(1)}, u32[]{:S(2)}, u32[]{:S(2)}) collective-permute-start(bf16[128,1152]{1,0:T(8,128)(2,1)S(1)} %slice.37), channel_id=1, source_target_pairs={{0,8},{8,0},{16,24},{24,16},{1,9},{9,1},{17,25},{25,17},{2,10},{10... | collective-permute-start | bytes 884744 | tf_op jit(solution)/shard_map/ppermute | solution.py:52
  98.1 18.9 %collective-permute-start.27 = (bf16[128,1152]{1,0:T(8,128)(2,1)S(1)}, bf16[128,1152]{1,0:T(8,128)(2,1)S(1)}, u32[]{:S(2)}, u32[]{:S(2)}) collective-permute-start(bf16[128,1152]{1,0:T(8,128)(2,1)S(1)} %slice.36), channel_id=1, source_target_pairs={{0,16},{8,24},{16,0},{24,8},{1,17},{9,25},{17,1},{25,9},{2,18},{10... | collective-permute-start | bytes 884744 | tf_op jit(solution)/shard_map/ppermute | solution.py:52
  107.1 15.4 %collective-permute-start.24 = (bf16[128,1152]{1,0:T(8,128)(2,1)S(1)}, bf16[128,1152]{1,0:T(8,128)(2,1)S(1)}, u32[]{:S(2)}, u32[]{:S(2)}) collective-permute-start(bf16[128,1152]{1,0:T(8,128)(2,1)S(1)} %slice.35), channel_id=1, source_target_pairs={{0,8},{8,0},{16,24},{24,16},{1,9},{9,1},{17,25},{25,17},{2,10},{10... | collective-permute-start | bytes 884744 | tf_op jit(solution)/shard_map/ppermute | solution.py:52
  110.7 11.8 %collective-permute-start.23 = (bf16[128,1152]{1,0:T(8,128)(2,1)S(1)}, bf16[128,1152]{1,0:T(8,128)(2,1)S(1)}, u32[]{:S(2)}, u32[]{:S(2)}) collective-permute-start(bf16[128,1152]{1,0:T(8,128)(2,1)S(1)} %slice.34), channel_id=1, source_target_pairs={{0,16},{8,24},{16,0},{24,8},{1,17},{9,25},{17,1},{25,9},{2,18},{10... | collective-permute-start | bytes 884744 | tf_op jit(solution)/shard_map/ppermute | solution.py:52
  141.3 16.3 %collective-permute-start.32 = (bf16[256,1152]{1,0:T(8,128)(2,1)S(1)}, bf16[256,1152]{1,0:T(8,128)(2,1)S(1)}, u32[]{:S(2)}, u32[]{:S(2)}) collective-permute-start(bf16[256,1152]{1,0:T(8,128)(2,1)S(1)} %get-tuple-element.142), channel_id=1, source_target_pairs={{0,8},{8,0},{16,24},{24,16},{1,9},{9,1},{17,25},{25,17},{2,10},{10... | collective-permute-start | bytes 1769480 | tf_op jit(solution)/shard_map/ppermute | solution.py:52
  142.5 25.4 %collective-permute-start.33 = (bf16[256,1152]{1,0:T(8,128)(2,1)S(1)}, bf16[256,1152]{1,0:T(8,128)(2,1)S(1)}, u32[]{:S(2)}, u32[]{:S(2)}) collective-permute-start(bf16[256,1152]{1,0:T(8,128)(2,1)S(1)} %get-tuple-element.143), channel_id=1, source_target_pairs={{0,16},{8,24},{16,0},{24,8},{1,17},{9,25},{17,1},{25,9},{2,18},{10... | collective-permute-start | bytes 1769480 | tf_op jit(solution)/shard_map/ppermute | solution.py:52
  143.5 26.1 %collective-permute-start.34 = (bf16[256,1152]{1,0:T(8,128)(2,1)S(1)}, bf16[256,1152]{1,0:T(8,128)(2,1)S(1)}, u32[]{:S(2)}, u32[]{:S(2)}) collective-permute-start(bf16[256,1152]{1,0:T(8,128)(2,1)S(1)} %get-tuple-element.144), channel_id=1, source_target_pairs={{0,24},{8,16},{16,8},{24,0},{1,25},{9,17},{17,9},{25,1},{2,26},{10... | collective-permute-start | bytes 1769480 | tf_op jit(solution)/shard_map/ppermute | solution.py:52
  173.9 7.8 %collective-permute-start.35 = (bf16[256,288]{1,0:T(8,128)(2,1)S(1)}, bf16[256,288]{1,0:T(8,128)(2,1)S(1)}, u32[]{:S(2)}, u32[]{:S(2)}) collective-permute-start(bf16[256,288]{1,0:T(8,128)(2,1)S(1)} %get-tuple-element.153), channel_id=1, source_target_pairs={{0,2},{1,3},{2,0},{3,1},{4,6},{5,7},{6,4},{7,5},{8,10},{9,11},{10,... | collective-permute-start | bytes 442376 | tf_op jit(solution)/shard_map/ppermute | solution.py:52
  174.4 10.5 %collective-permute-start.37 = (bf16[256,288]{1,0:T(8,128)(2,1)S(1)}, bf16[256,288]{1,0:T(8,128)(2,1)S(1)}, u32[]{:S(2)}, u32[]{:S(2)}) collective-permute-start(bf16[256,288]{1,0:T(8,128)(2,1)S(1)} %get-tuple-element.155), channel_id=1, source_target_pairs={{0,3},{1,2},{2,1},{3,0},{4,7},{5,6},{6,5},{7,4},{8,11},{9,10},{10,... | collective-permute-start | bytes 442376 | tf_op jit(solution)/shard_map/ppermute | solution.py:52
  202.1 17.9 %collective-permute-start.41 = (bf16[576,1152]{1,0:T(8,128)(2,1)S(1)}, bf16[576,1152]{1,0:T(8,128)(2,1)S(1)}, u32[]{:S(2)}, u32[]{:S(2)}) collective-permute-start(bf16[576,1152]{1,0:T(8,128)(2,1)S(1)} %fc1_other.1.refs_9_), channel_id=1, source_target_pairs={{0,1},{1,0},{2,3},{3,2},{4,5},{5,4},{6,7},{7,6},{8,9},{9,8},{10,11... | collective-permute-start | bytes 3981320 | tf_op jit(solution)/shard_map/ppermute | solution.py:52
  202.3 17.1 %collective-permute-start.42 = (bf16[288,1152]{1,0:T(8,128)(2,1)S(1)}, bf16[288,1152]{1,0:T(8,128)(2,1)S(1)}, u32[]{:S(2)}, u32[]{:S(2)}) collective-permute-start(bf16[288,1152]{1,0:T(8,128)(2,1)S(1)} %get-tuple-element.161), channel_id=1, source_target_pairs={{0,2},{1,3},{2,0},{3,1},{4,6},{5,7},{6,4},{7,5},{8,10},{9,11},{10,... | collective-permute-start | bytes 1990664 | tf_op jit(solution)/shard_map/ppermute | solution.py:52
  202.6 22.5 %collective-permute-start.29 = (bf16[256,1152]{1,0:T(8,128)(2,1)S(1)}, bf16[256,1152]{1,0:T(8,128)(2,1)S(1)}, u32[]{:S(2)}, u32[]{:S(2)}) collective-permute-start(bf16[256,1152]{1,0:T(8,128)(2,1)S(1)} %get-tuple-element.136), channel_id=1, source_target_pairs={{0,8},{8,0},{16,24},{24,16},{1,9},{9,1},{17,25},{25,17},{2,10},{10... | collective-permute-start | bytes 1769480 | tf_op jit(solution)/shard_map/ppermute | solution.py:52
  203.6 25.8 %collective-permute-start.30 = (bf16[256,1152]{1,0:T(8,128)(2,1)S(1)}, bf16[256,1152]{1,0:T(8,128)(2,1)S(1)}, u32[]{:S(2)}, u32[]{:S(2)}) collective-permute-start(bf16[256,1152]{1,0:T(8,128)(2,1)S(1)} %get-tuple-element.137), channel_id=1, source_target_pairs={{0,16},{8,24},{16,0},{24,8},{1,17},{9,25},{17,1},{25,9},{2,18},{10... | collective-permute-start | bytes 1769480 | tf_op jit(solution)/shard_map/ppermute | solution.py:52
  206.5 25.7 %collective-permute-start.31 = (bf16[256,1152]{1,0:T(8,128)(2,1)S(1)}, bf16[256,1152]{1,0:T(8,128)(2,1)S(1)}, u32[]{:S(2)}, u32[]{:S(2)}) collective-permute-start(bf16[256,1152]{1,0:T(8,128)(2,1)S(1)} %get-tuple-element.138), channel_id=1, source_target_pairs={{0,24},{8,16},{16,8},{24,0},{1,25},{9,17},{17,9},{25,1},{2,26},{10... | collective-permute-start | bytes 1769480 | tf_op jit(solution)/shard_map/ppermute | solution.py:52
  219.4 23.4 %collective-permute-start.40 = (bf16[256,1152]{1,0:T(8,128)(2,1)S(1)}, bf16[256,1152]{1,0:T(8,128)(2,1)S(1)}, u32[]{:S(2)}, u32[]{:S(2)}) collective-permute-start(bf16[256,1152]{1,0:T(8,128)(2,1)S(1)} %attn_sum.1.refs_2_), channel_id=1, source_target_pairs={{0,2},{1,3},{2,0},{3,1},{4,6},{5,7},{6,4},{7,5},{8,10},{9,11},{10,... | collective-permute-start | bytes 1769480 | tf_op jit(solution)/shard_map/ppermute | solution.py:52
  224.1 25.6 %collective-permute-start.46 = (bf16[288,864]{1,0:T(8,128)(2,1)S(1)}, bf16[288,864]{1,0:T(8,128)(2,1)S(1)}, u32[]{:S(2)}, u32[]{:S(2)}) collective-permute-start(bf16[288,864]{1,0:T(8,128)(2,1)S(1)} %get-tuple-element.171), channel_id=1, source_target_pairs={{0,8},{8,0},{16,24},{24,16},{1,9},{9,1},{17,25},{25,17},{2,10},{10... | collective-permute-start | bytes 1493000 | tf_op jit(solution)/shard_map/ppermute | solution.py:52
  225.1 24.4 %collective-permute-start.44 = (bf16[144,1152]{1,0:T(8,128)(2,1)S(1)}, bf16[144,1152]{1,0:T(8,128)(2,1)S(1)}, u32[]{:S(2)}, u32[]{:S(2)}) collective-permute-start(bf16[144,1152]{1,0:T(8,128)(2,1)S(1)} %get-tuple-element.169), channel_id=1, source_target_pairs={{0,4},{1,5},{2,6},{3,7},{4,0},{5,1},{6,2},{7,3},{8,12},{9,13},{10,... | collective-permute-start | bytes 995336 | tf_op jit(solution)/shard_map/ppermute | solution.py:52
  229.5 34.3 %collective-permute-start.51 = (bf16[288,1152]{1,0:T(8,128)(2,1)S(1)}, bf16[288,1152]{1,0:T(8,128)(2,1)S(1)}, u32[]{:S(2)}, u32[]{:S(2)}) collective-permute-start(bf16[288,1152]{1,0:T(8,128)(2,1)S(1)} %get-tuple-element.174), channel_id=1, source_target_pairs={{0,2},{1,3},{2,0},{3,1},{4,6},{5,7},{6,4},{7,5},{8,10},{9,11},{10,... | collective-permute-start | bytes 1990664 | tf_op jit(solution)/shard_map/ppermute | solution.py:52
  232.2 22.9 %collective-permute-start.47 = (bf16[288,864]{1,0:T(8,128)(2,1)S(1)}, bf16[288,864]{1,0:T(8,128)(2,1)S(1)}, u32[]{:S(2)}, u32[]{:S(2)}) collective-permute-start(bf16[288,864]{1,0:T(8,128)(2,1)S(1)} %get-tuple-element.172), channel_id=1, source_target_pairs={{0,16},{8,24},{16,0},{24,8},{1,17},{9,25},{17,1},{25,9},{2,18},{10... | collective-permute-start | bytes 1493000 | tf_op jit(solution)/shard_map/ppermute | solution.py:52
  242.8 12.3 %collective-permute-start.48 = (bf16[288,864]{1,0:T(8,128)(2,1)S(1)}, bf16[288,864]{1,0:T(8,128)(2,1)S(1)}, u32[]{:S(2)}, u32[]{:S(2)}) collective-permute-start(bf16[288,864]{1,0:T(8,128)(2,1)S(1)} %get-tuple-element.173), channel_id=1, source_target_pairs={{0,24},{8,16},{16,8},{24,0},{1,25},{9,17},{17,9},{25,1},{2,26},{10... | collective-permute-start | bytes 1493000 | tf_op jit(solution)/shard_map/ppermute | solution.py:52
  249.7 14.3 %collective-permute-start.50 = (bf16[144,1152]{1,0:T(8,128)(2,1)S(1)}, bf16[144,1152]{1,0:T(8,128)(2,1)S(1)}, u32[]{:S(2)}, u32[]{:S(2)}) collective-permute-start(bf16[144,1152]{1,0:T(8,128)(2,1)S(1)} %fc2_cube.5.refs_6_.refs_0_), channel_id=1, source_target_pairs={{0,4},{1,5},{2,6},{3,7},{4,0},{5,1},{6,2},{7,3},{8,12},{9,13},{10,... | collective-permute-start | bytes 995336 | tf_op jit(solution)/shard_map/ppermute | solution.py:52
  255.4 9.5 %collective-permute-start.49 = (bf16[8,6912]{1,0:T(8,128)(2,1)S(1)}, bf16[8,6912]{1,0:T(8,128)(2,1)S(1)}, u32[]{:S(2)}, u32[]{:S(2)}) collective-permute-start(bf16[8,6912]{1,0:T(8,128)(2,1)S(1)} %sums.2.refs_2_.refs_0_), channel_id=1, source_target_pairs={{0,2},{1,3},{2,0},{3,1},{4,6},{5,7},{6,4},{7,5},{8,10},{9,11},{10,... | collective-permute-start | bytes 331784 | tf_op jit(solution)/shard_map/ppermute | solution.py:52
  265.2 33.0 %collective-permute-start.63 = (bf16[288,1152]{1,0:T(8,128)(2,1)S(1)}, bf16[288,1152]{1,0:T(8,128)(2,1)S(1)}, u32[]{:S(2)}, u32[]{:S(2)}) collective-permute-start(bf16[288,1152]{1,0:T(8,128)(2,1)S(1)} %fc2_cube.6.refs_2_.refs_0_), channel_id=1, source_target_pairs={{0,2},{1,3},{2,0},{3,1},{4,6},{5,7},{6,4},{7,5},{8,10},{9,11},{10,... | collective-permute-start | bytes 1990664 | tf_op jit(solution)/shard_map/ppermute | solution.py:52
  267.6 21.9 %collective-permute-start.56 = (bf16[144,1152]{1,0:T(8,128)(2,1)S(1)}, bf16[144,1152]{1,0:T(8,128)(2,1)S(1)}, u32[]{:S(2)}, u32[]{:S(2)}) collective-permute-start(bf16[144,1152]{1,0:T(8,128)(2,1)S(1)} %get-tuple-element.180), channel_id=1, source_target_pairs={{0,4},{1,5},{2,6},{3,7},{4,0},{5,1},{6,2},{7,3},{8,12},{9,13},{10,... | collective-permute-start | bytes 995336 | tf_op jit(solution)/shard_map/ppermute | solution.py:52
  269.5 23.4 %collective-permute-start.53 = (bf16[144,1152]{1,0:T(8,128)(2,1)S(1)}, bf16[144,1152]{1,0:T(8,128)(2,1)S(1)}, u32[]{:S(2)}, u32[]{:S(2)}) collective-permute-start(bf16[144,1152]{1,0:T(8,128)(2,1)S(1)} %get-tuple-element.177), channel_id=1, source_target_pairs={{0,8},{8,0},{16,24},{24,16},{1,9},{9,1},{17,25},{25,17},{2,10},{10... | collective-permute-start | bytes 995336 | tf_op jit(solution)/shard_map/ppermute | solution.py:52
  270.6 22.4 %collective-permute-start.54 = (bf16[144,1152]{1,0:T(8,128)(2,1)S(1)}, bf16[144,1152]{1,0:T(8,128)(2,1)S(1)}, u32[]{:S(2)}, u32[]{:S(2)}) collective-permute-start(bf16[144,1152]{1,0:T(8,128)(2,1)S(1)} %get-tuple-element.178), channel_id=1, source_target_pairs={{0,16},{8,24},{16,0},{24,8},{1,17},{9,25},{17,1},{25,9},{2,18},{10... | collective-permute-start | bytes 995336 | tf_op jit(solution)/shard_map/ppermute | solution.py:52
  271.8 21.1 %collective-permute-start.55 = (bf16[144,1152]{1,0:T(8,128)(2,1)S(1)}, bf16[144,1152]{1,0:T(8,128)(2,1)S(1)}, u32[]{:S(2)}, u32[]{:S(2)}) collective-permute-start(bf16[144,1152]{1,0:T(8,128)(2,1)S(1)} %get-tuple-element.179), channel_id=1, source_target_pairs={{0,24},{8,16},{16,8},{24,0},{1,25},{9,17},{17,9},{25,1},{2,26},{10... | collective-permute-start | bytes 995336 | tf_op jit(solution)/shard_map/ppermute | solution.py:52
  289.5 8.6 %collective-permute-start.59 = (bf16[8,6912]{1,0:T(8,128)(2,1)S(1)}, bf16[8,6912]{1,0:T(8,128)(2,1)S(1)}, u32[]{:S(2)}, u32[]{:S(2)}) collective-permute-start(bf16[8,6912]{1,0:T(8,128)(2,1)S(1)} %sums.3.refs_1_.refs_0_), channel_id=1, source_target_pairs={{0,4},{1,5},{2,6},{3,7},{4,0},{5,1},{6,2},{7,3},{8,12},{9,13},{10,... | collective-permute-start | bytes 331784 | tf_op jit(solution)/shard_map/ppermute | solution.py:52
  298.4 33.7 %collective-permute-start.69 = (bf16[576,1152]{1,0:T(8,128)(2,1)S(1)}, bf16[576,1152]{1,0:T(8,128)(2,1)S(1)}, u32[]{:S(2)}, u32[]{:S(2)}) collective-permute-start(bf16[576,1152]{1,0:T(8,128)(2,1)S(1)} %fc2_cube.7.refs_6_.refs_0_), channel_id=1, source_target_pairs={{0,1},{1,0},{2,3},{3,2},{4,5},{5,4},{6,7},{7,6},{8,9},{9,8},{10,11... | collective-permute-start | bytes 3981320 | tf_op jit(solution)/shard_map/ppermute | solution.py:52
  298.5 33.3 %collective-permute-start.58 = (bf16[288,864]{1,0:T(8,128)(2,1)S(1)}, bf16[288,864]{1,0:T(8,128)(2,1)S(1)}, u32[]{:S(2)}, u32[]{:S(2)}) collective-permute-start(bf16[288,864]{1,0:T(8,128)(2,1)S(1)} %qkv_sum.2.refs_2_.refs_0_), channel_id=1, source_target_pairs={{0,4},{1,5},{2,6},{3,7},{4,0},{5,1},{6,2},{7,3},{8,12},{9,13},{10,... | collective-permute-start | bytes 1493000 | tf_op jit(solution)/shard_map/ppermute | solution.py:52
  298.9 9.2 %collective-permute-start.62 = (bf16[16,6912]{1,0:T(8,128)(2,1)S(1)}, bf16[16,6912]{1,0:T(8,128)(2,1)S(1)}, u32[]{:S(2)}, u32[]{:S(2)}) collective-permute-start(bf16[16,6912]{1,0:T(8,128)(2,1)S(1)} %both.1.refs_2_.refs_0_), channel_id=1, source_target_pairs={{0,24},{8,16},{16,8},{24,0},{1,25},{9,17},{17,9},{25,1},{2,26},{10... | collective-permute-start | bytes 663560 | tf_op jit(solution)/shard_map/ppermute | solution.py:52
  300.7 12.1 %collective-permute-start.61 = (bf16[16,6912]{1,0:T(8,128)(2,1)S(1)}, bf16[16,6912]{1,0:T(8,128)(2,1)S(1)}, u32[]{:S(2)}, u32[]{:S(2)}) collective-permute-start(bf16[16,6912]{1,0:T(8,128)(2,1)S(1)} %both.1.refs_2_.refs_0_), channel_id=1, source_target_pairs={{0,16},{8,24},{16,0},{24,8},{1,17},{9,25},{17,1},{25,9},{2,18},{10... | collective-permute-start | bytes 663560 | tf_op jit(solution)/shard_map/ppermute | solution.py:52
  301.1 13.4 %collective-permute-start.60 = (bf16[16,6912]{1,0:T(8,128)(2,1)S(1)}, bf16[16,6912]{1,0:T(8,128)(2,1)S(1)}, u32[]{:S(2)}, u32[]{:S(2)}) collective-permute-start(bf16[16,6912]{1,0:T(8,128)(2,1)S(1)} %both.1.refs_2_.refs_0_), channel_id=1, source_target_pairs={{0,8},{8,0},{16,24},{24,16},{1,9},{9,1},{17,25},{25,17},{2,10},{10... | collective-permute-start | bytes 663560 | tf_op jit(solution)/shard_map/ppermute | solution.py:52
  308.1 23.8 %collective-permute-start.57 = (bf16[144,1152]{1,0:T(8,128)(2,1)S(1)}, bf16[144,1152]{1,0:T(8,128)(2,1)S(1)}, u32[]{:S(2)}, u32[]{:S(2)}) collective-permute-start(bf16[144,1152]{1,0:T(8,128)(2,1)S(1)} %proj_sum.1.refs_2_.refs_0_), channel_id=1, source_target_pairs={{0,2},{1,3},{6,4},{7,5},{8,10},{9,11},{14,12},{15,13},{16,18},{17,... | collective-permute-start | bytes 995336 | tf_op jit(solution)/shard_map/ppermute | solution.py:91
  312.8 26.1 %collective-permute-start.68 = (bf16[144,1152]{1,0:T(8,128)(2,1)S(1)}, bf16[144,1152]{1,0:T(8,128)(2,1)S(1)}, u32[]{:S(2)}, u32[]{:S(2)}) collective-permute-start(bf16[144,1152]{1,0:T(8,128)(2,1)S(1)} %fc1_cube.5.refs_4_.refs_0_), channel_id=1, source_target_pairs={{0,4},{1,5},{2,6},{3,7},{4,0},{5,1},{6,2},{7,3},{8,12},{9,13},{10,... | collective-permute-start | bytes 995336 | tf_op jit(solution)/shard_map/ppermute | solution.py:52
  331.9 18.1 %collective-permute-start.74 = (bf16[288,864]{1,0:T(8,128)(2,1)S(1)}, bf16[288,864]{1,0:T(8,128)(2,1)S(1)}, u32[]{:S(2)}, u32[]{:S(2)}) collective-permute-start(bf16[288,864]{1,0:T(8,128)(2,1)S(1)} %qkv_sum.3.refs_2_.refs_0_), channel_id=1, source_target_pairs={{0,2},{1,3},{2,0},{3,1},{4,6},{5,7},{6,4},{7,5},{8,10},{9,11},{10,... | collective-permute-start | bytes 1493000 | tf_op jit(solution)/shard_map/ppermute | solution.py:52
  341.5 22.6 %collective-permute-start.70 = (bf16[288,1152]{1,0:T(8,128)(2,1)S(1)}, bf16[288,1152]{1,0:T(8,128)(2,1)S(1)}, u32[]{:S(2)}, u32[]{:S(2)}) collective-permute-start(bf16[288,1152]{1,0:T(8,128)(2,1)S(1)} %fc1_cube.6.refs_0_.refs_2_), channel_id=1, source_target_pairs={{0,2},{1,3},{2,0},{3,1},{4,6},{5,7},{6,4},{7,5},{8,10},{9,11},{10,... | collective-permute-start | bytes 1990664 | tf_op jit(solution)/shard_map/ppermute | solution.py:52
  341.6 33.8 %collective-permute-start.73 = (bf16[288,864]{1,0:T(8,128)(2,1)S(1)}, bf16[288,864]{1,0:T(8,128)(2,1)S(1)}, u32[]{:S(2)}, u32[]{:S(2)}) collective-permute-start(bf16[288,864]{1,0:T(8,128)(2,1)S(1)} %qkv_sum.3.refs_2_.refs_0_), channel_id=1, source_target_pairs={{0,1},{1,0},{2,3},{3,2},{4,5},{5,4},{6,7},{7,6},{8,9},{9,8},{10,11... | collective-permute-start | bytes 1493000 | tf_op jit(solution)/shard_map/ppermute | solution.py:52
  349.9 26.8 %collective-permute-start.75 = (bf16[288,864]{1,0:T(8,128)(2,1)S(1)}, bf16[288,864]{1,0:T(8,128)(2,1)S(1)}, u32[]{:S(2)}, u32[]{:S(2)}) collective-permute-start(bf16[288,864]{1,0:T(8,128)(2,1)S(1)} %collective-permute-done.74.refs_2_), channel_id=1, source_target_pairs={{0,1},{1,0},{2,3},{3,2},{4,5},{5,4},{6,7},{7,6},{8,9},{9,8},{10,11... | collective-permute-start | bytes 1493000 | tf_op jit(solution)/shard_map/ppermute | solution.py:52
  349.9 21.0 %collective-permute-start.64 = (bf16[144,1152]{1,0:T(8,128)(2,1)S(1)}, bf16[144,1152]{1,0:T(8,128)(2,1)S(1)}, u32[]{:S(2)}, u32[]{:S(2)}) collective-permute-start(bf16[144,1152]{1,0:T(8,128)(2,1)S(1)} %proj_line.3.refs_2_.refs_0_), channel_id=1, source_target_pairs={{2,4},{3,5},{4,2},{5,3},{10,12},{11,13},{12,10},{13,11},{18,20},{1... | collective-permute-start | bytes 995336 | tf_op jit(solution)/shard_map/ppermute | solution.py:91
  358.1 15.6 %collective-permute-start.72 = (bf16[128,1152]{1,0:T(8,128)(2,1)S(1)}, bf16[128,1152]{1,0:T(8,128)(2,1)S(1)}, u32[]{:S(2)}, u32[]{:S(2)}) collective-permute-start(bf16[128,1152]{1,0:T(8,128)(2,1)S(1)} %get-tuple-element.190), channel_id=1, source_target_pairs={{0,4},{1,5},{2,6},{3,7},{4,0},{5,1},{6,2},{7,3},{8,12},{9,13},{10,... | collective-permute-start | bytes 884744 | tf_op jit(solution)/shard_map/ppermute | solution.py:52
  368.8 14.0 %collective-permute-start.77 = (bf16[144,1152]{1,0:T(8,128)(2,1)S(1)}, bf16[144,1152]{1,0:T(8,128)(2,1)S(1)}, u32[]{:S(2)}, u32[]{:S(2)}) collective-permute-start(bf16[144,1152]{1,0:T(8,128)(2,1)S(1)} %get-tuple-element.191), channel_id=1, source_target_pairs={{0,8},{8,0},{16,24},{24,16},{1,9},{9,1},{17,25},{25,17},{2,10},{10... | collective-permute-start | bytes 995336 | tf_op jit(solution)/shard_map/ppermute | solution.py:52
  370.9 15.7 %collective-permute-start.78 = (bf16[144,1152]{1,0:T(8,128)(2,1)S(1)}, bf16[144,1152]{1,0:T(8,128)(2,1)S(1)}, u32[]{:S(2)}, u32[]{:S(2)}) collective-permute-start(bf16[144,1152]{1,0:T(8,128)(2,1)S(1)} %get-tuple-element.192), channel_id=1, source_target_pairs={{0,16},{8,24},{16,0},{24,8},{1,17},{9,25},{17,1},{25,9},{2,18},{10... | collective-permute-start | bytes 995336 | tf_op jit(solution)/shard_map/ppermute | solution.py:52
  373.7 13.0 %collective-permute-start.79 = (bf16[144,1152]{1,0:T(8,128)(2,1)S(1)}, bf16[144,1152]{1,0:T(8,128)(2,1)S(1)}, u32[]{:S(2)}, u32[]{:S(2)}) collective-permute-start(bf16[144,1152]{1,0:T(8,128)(2,1)S(1)} %get-tuple-element.193), channel_id=1, source_target_pairs={{0,24},{8,16},{16,8},{24,0},{1,25},{9,17},{17,9},{25,1},{2,26},{10... | collective-permute-start | bytes 995336 | tf_op jit(solution)/shard_map/ppermute | solution.py:52
  375.4 11.7 %collective-permute-start.71 = (bf16[144,1152]{1,0:T(8,128)(2,1)S(1)}, bf16[144,1152]{1,0:T(8,128)(2,1)S(1)}, u32[]{:S(2)}, u32[]{:S(2)}) collective-permute-start(bf16[144,1152]{1,0:T(8,128)(2,1)S(1)} %proj_line.4.refs_4_.refs_0_), channel_id=1, source_target_pairs={{2,0},{3,1},{4,6},{5,7},{10,8},{11,9},{12,14},{13,15},{18,16},{19,... | collective-permute-start | bytes 995336 | tf_op jit(solution)/shard_map/ppermute | solution.py:91
  376.7 11.9 %collective-permute-start.80 = (bf16[144,1152]{1,0:T(8,128)(2,1)S(1)}, bf16[144,1152]{1,0:T(8,128)(2,1)S(1)}, u32[]{:S(2)}, u32[]{:S(2)}) collective-permute-start(bf16[144,1152]{1,0:T(8,128)(2,1)S(1)} %get-tuple-element.187.refs_1_.refs_0_), channel_id=1, source_target_pairs={{0,1},{1,0},{2,3},{3,2},{4,5},{5,4},{6,7},{7,6},{8,9},{9,8},{10,11... | collective-permute-start | bytes 995336 | tf_op jit(solution)/shard_map/ppermute | solution.py:52
  388.6 16.2 %collective-permute-start.43 = (bf16[128,1152]{1,0:T(8,128)(2,1)S(1)}, bf16[128,1152]{1,0:T(8,128)(2,1)S(1)}, u32[]{:S(2)}, u32[]{:S(2)}) collective-permute-start(bf16[128,1152]{1,0:T(8,128)(2,1)S(1)} %get-tuple-element.167), channel_id=1, source_target_pairs={{0,4},{1,5},{2,6},{3,7},{4,0},{5,1},{6,2},{7,3},{8,12},{9,13},{10,... | collective-permute-start | bytes 884744 | tf_op jit(solution)/shard_map/ppermute | solution.py:52
  (63 other events, 585.4 us)

commit v3 on v2

--- a/solution.py
+++ b/solution.py
@@ -285,12 +285,18 @@
             step(i)
 
 
-def open_kernel(half, cond_ref, bias_ref, qv_ref, lat_ref, cot_ref, lengths_ref, *refs):
-    pack_ref, lat_own, cot_own, send_ref, docq_ref, dock_ref, mod_ref, sum_ref = refs
+def part_ways_kernel(half, x_ref, own_ref, send_ref):
+    micro = lax.axis_index("blk") // half
+    own_ref[...] = x_ref[micro, 0]
+    send_ref[...] = x_ref[1 - micro, 0]
+
+
+def open_kernel(half, seg, cond_ref, bias_ref, qv_ref, lengths_ref, *refs):
+    pack_ref, docq_ref, dock_ref, mod_ref, sum_ref = refs
     blk = lax.axis_index("blk")
     micro = blk // half
     group = half
-    seg, features = lat_own.shape
+    features = pack_ref.shape[1]
     tokens = 2 * seg
     dshard = qv_ref.shape[1]
     cond = jnp.concatenate([cond_ref[0, 0], cond_ref[1, 0]], axis=0).astype(F32)
@@ -300,10 +306,6 @@
     )
     small = jnp.pad(small, ((0, 7), (0, features - 3 * dshard)))
     pack_ref[...] = jnp.concatenate([silu, small], axis=0).astype(BF)
-    lat_own[...] = lat_ref[micro, 0]
-    cot_own[...] = cot_ref[micro, 0]
-    send_ref[:seg, :] = lat_ref[1 - micro, 0]
-    send_ref[seg:, :] = cot_ref[1 - micro, 0]
     ends, last = [], 0
     for d in range(DOCS):
         last = last + lengths_ref[micro, 0, d]
@@ -430,7 +432,7 @@
 def attn_in_kernel(own_ref, got_ref, pick_ref, mod_ref, out_ref, lat_ref, shift_ref, scale_ref):
     seg, features = own_ref.shape
     lat_ref[:seg, :] = own_ref[...]
-    lat_ref[seg:, :] = got_ref[:seg, :]
+    lat_ref[seg:, :] = got_ref[...]
     shift_ref[...] = dot_nn(pick_ref[...], mod_ref[:, :features])
     scale_ref[...] = dot_nn(pick_ref[...], mod_ref[:, features : 2 * features])
 
@@ -444,7 +446,7 @@
 def grad_fc2_kernel(own_ref, got_ref, pick_ref, pickt_ref, mod_ref, out_ref, cot_ref, sums_ref):
     seg, features = own_ref.shape
     cot_ref[:seg, :] = own_ref[...]
-    cot_ref[seg:, :] = got_ref[seg:, :]
+    cot_ref[seg:, :] = got_ref[...]
     gate = dot_nn(pick_ref[...], mod_ref[:, 5 * features : 6 * features])
     out_ref[...] = (gate * cot_ref[...].astype(F32)).astype(BF)
     sums_ref[...] = dot_nn(pickt_ref[...], out_ref[...])
@@ -1170,21 +1172,31 @@
     chip_bits = bits_of(2, n_blk)
 
     def step_open():
-        v.pack, v.lat_own, v.cot_own, across, v.docq, v.dock, v.pick_mod, v.pick_sum = whole_call(
-            functools.partial(open_kernel, half),
+        args = [conditions, proj_bias, qv_bias, doc_lengths]
+        v.pack, v.docq, v.dock, v.pick_mod, v.pick_sum = launch(
             "open",
-            [sds((16, features), BF)]
-            + [half_shape, half_shape, act_shape]
-            + [
+            functools.partial(open_kernel, half, seg),
+            args,
+            [pl.BlockSpec(x.shape, lambda i, n=x.ndim: (0,) * n) for x in args[:3]] + [SM],
+            [VM] * 5,
+            [
+                sds((16, features), BF),
                 sds((1, group * tokens), jnp.int32),
                 sds((group * tokens, 128), jnp.int32),
                 sds((tokens, 32), BF),
                 sds((16, tokens), BF),
             ],
-            [conditions, proj_bias, qv_bias, latents, cotangent, doc_lengths],
-        )
-        v.across = swap(across, "blk", half)
+            grid=(1,),
+        )
         v.pack = direct({m: v.pack for m in range(n_dp)}, "dp")
+
+    def step_lat():
+        v.lat_own, send = whole_call(functools.partial(part_ways_kernel, half), "lat", [half_shape] * 2, [latents])
+        v.lat_got = swap(send, "blk", half)
+
+    def step_cot():
+        v.cot_own, send = whole_call(functools.partial(part_ways_kernel, half), "cot", [half_shape] * 2, [cotangent])
+        v.cot_got = swap(send, "blk", half)
 
     def step_qkv_cols():
         (cols,) = whole_call(
@@ -1212,7 +1224,7 @@
             attn_in_kernel,
             "attn_in",
             [act_shape] * 2,
-            [v.lat_own, v.across, v.pick_mod, v.mod],
+            [v.lat_own, v.lat_got, v.pick_mod, v.mod],
             [full_vmem] * 2,
         )
         rows = {0: attn_in}
@@ -1228,7 +1240,7 @@
             grad_fc2_kernel,
             "grad_fc2",
             [act_shape, act_shape, sums_shape],
-            [v.cot_own, v.across, v.pick_mod, v.pick_sum, v.mod],
+            [v.cot_own, v.cot_got, v.pick_mod, v.pick_sum, v.mod],
         )
         v.all_grad = spread_dp(grad_fc2)
 
@@ -1493,14 +1505,14 @@
         v.latent_grad = give_back(v.latent_own, v.latent_other, "latent_grad")
 
     for step in (
-        step_open, step_qkv_cols, step_mod_part, step_cuts, step_mod_all, step_attn_in, step_attend, step_grad_fc2,
-        step_stack, step_mix, step_mlp, step_fc2_wgrad, step_fc1_wgrad, step_turn, step_fc2_other, step_fc2_own,
-        step_fc1_other, step_attend_back, step_attn_sum, step_fc2_a, step_fc1_own, step_qkv_wgrad, step_finish,
-        step_proj_wgrad, step_outs, step_fc2_b, step_gather_sums, step_qkv_sum, step_sums_c, step_fc1_a,
-        step_fc2_j, step_sums_g, step_proj_other, step_proj_blocks, step_fc1_b, step_proj_sum, step_sums_h,
-        step_fc2_c, step_ada, step_qkv_sum2, step_proj_a, step_place_fc2, step_fc1_j, step_fc1_c, step_biases, step_cond,
-        step_proj_b, step_place_qkv, step_latent_grad, step_proj_c, step_place_fc1, step_place_proj,
-        step_block_out,
+        step_cuts, step_lat, step_open, step_qkv_cols, step_mod_part, step_mod_all, step_attn_in, step_cot,
+        step_attend, step_grad_fc2, step_stack, step_mix, step_mlp, step_fc2_wgrad, step_fc1_wgrad, step_turn,
+        step_fc2_other, step_fc1_other, step_fc2_own, step_attend_back, step_attn_sum, step_fc1_own,
+        step_qkv_wgrad, step_fc2_a, step_proj_wgrad, step_outs, step_finish, step_gather_sums, step_fc2_b,
+        step_sums_c, step_qkv_sum, step_fc1_a, step_fc2_j, step_sums_g, step_proj_other, step_proj_blocks,
+        step_sums_h, step_fc1_b, step_proj_sum, step_fc2_c, step_ada, step_proj_a, step_biases, step_qkv_sum2,
+        step_place_fc2, step_cond, step_fc1_j, step_proj_b, step_fc1_c, step_latent_grad, step_place_qkv,
+        step_proj_c, step_block_out, step_place_proj, step_place_fc1,
     ):
         step()
 

time: 411 us -> 401 us (0.976)
  starting transfers between devices: 91.4 us -> 81.1 us
    ppermute x81 -> x82, starting transfers between devices: 84.8 us -> 77.9 us  [swap(): return lax.ppermute(x, axis, [(i, i ^ mask) for i in range(count)])]
    ppermute x81 -> x82, waiting for transfers between devices: 185 us -> 189 us  [swap(): return lax.ppermute(x, axis, [(i, i ^ mask) for i in range(count)])]
    unnamed x86 -> x102, local copies, waits for them, and re-layouts: 25.1 us -> 21.4 us
    pallas_call x53 -> x55, Pallas kernels: 101 us -> 101 us  [launch(): pl.pallas_call(body, **{} if grid is None else {'grid': grid}, in_specs=l...]
  transfers between devices with their start and end apart: 84 -> 85, of which waited for: 43 -> 36; matrix products, arithmetic and copies ran while one was open for 0% -> 1% of each run, Pallas kernels for 15% -> 19%
where the time goes in v3:
time: 401 us; the launch traced here: 398 us
  waiting for transfers between devices  189 us (47%)
  Pallas kernels  101 us (25%)
  starting transfers between devices  81.1 us (20%)
  local copies, waits for them, and re-layouts  21.5 us (5%)
    ppermute x82, waiting for transfers between devices, swap(): return lax.ppermute(x, axis, [(i, i ^ mask) for i in range(count)])  189 us
    pallas_call x55, Pallas kernels, launch(): pl.pallas_call(body, **{} if grid is None else {'grid': grid}, in_specs=l...  101 us
    ppermute x82, starting transfers between devices, swap(): return lax.ppermute(x, axis, [(i, i ^ mask) for i in range(count)])  77.9 us
    unnamed x102, local copies, waits for them, and re-layouts  21.4 us
  transfers between devices with their start and end apart: 85, of which 36 were waited for; matrix products, arithmetic and copies ran while one was open for 1% of the time, Pallas kernels for 19%

profile of v3, /device:TPU:0, one launch (start us, length us, event | category | flops | bytes accessed | tf_op | source)
XLA Modules:
  0.0 397.9 jit_solution(4638541420080713272)
XLA Ops:
  0.7 1.7 copy-done.8
  4.6 4.1 %collective-permute-start = (bf16[128,1152]{1,0:T(8,128)(2,1)S(1)}, bf16[128,1152]{1,0:T(8,128)(2,1)S(1)}, u32[]{:S(2)}, u32[]{:S(2)}) collective-permute-start(bf16[128,1152]{1,0:T(8,128)(2,1)S(1)} %get-tuple-element.109), channel_id=1, source_target_pairs={{0,4},{1,5},{2,6},{3,7},{4,0},{5,1},{6,2},{7,3},{8,12},{9,13},{10,... | collective-permute-start | bytes 884744 | tf_op jit(solution)/shard_map/ppermute | solution.py:52
  9.6 2.5 collective-permute-start.3
  13.4 1.6 collective-permute-start.11
  18.5 1.6 collective-permute-start.5
  20.1 9.7 %collective-permute-done.4.refs_1_ = f32[4,6912]{1,0:T(4,128)S(1)} collective-permute-done((f32[4,6912]{1,0:T(4,128)S(1)}, f32[4,6912]{1,0:T(4,128)S(1)}, u32[]{:S(2)}, u32[]{:S(2)}) %collective-permute-start.4) | collective-permute-done | bytes 110624 | tf_op jit(solution)/shard_map/ppermute | solution.py:52
  29.8 1.7 collective-permute-start.6
  31.5 4.0 collective-permute-done.6.refs_3_
  37.0 1.7 collective-permute-start.7
  42.2 3.6 collective-permute-done.13.refs_8_
  45.8 1.8 collective-permute-start.18
  47.6 2.0 collective-permute-start.19
  49.7 1.8 collective-permute-done.9.refs_3_
  51.6 16.4 %attend.1 = (bf16[1024,864]{1,0:T(8,128)(2,1)S(1)}, bf16[1152,864]{1,0:T(8,128)(2,1)S(1)}, bf16[256,288]{1,0:T(8,128)(2,1)S(1)}, bf16[256,288]{1,0:T(8,128)(2,1)...) custom-call(bf16[256,1152]{1,0:T(8,128)(2,1)S(1)} %get-tuple-element, ...), custom_call_target="tpu_custom_call" | custom-call | flops 1000 | bytes 1000 | tf_op jit(solution)/shard_map/attend/pallas_call | solution.py:243
  72.9 1.9 collective-permute-done.18.refs_2_
  78.2 2.0 collective-permute-done.14.refs_1_
  81.2 2.1 collective-permute-done.15.refs_2_
  83.3 2.5 collective-permute-done.16.refs_3_
  85.8 2.6 mix.1
  97.0 11.2 %collective-permute-done.23.refs_2_ = bf16[256,1152]{1,0:T(8,128)(2,1)S(1)} collective-permute-done((bf16[256,1152]{1,0:T(8,128)(2,1)S(1)}, bf16[256,1152]{1,0:T(8,128)(2,1)S(1)}, u32[]{:S(2)}, u32[]{:S(2)}) %collective-permute-start.23) | collective-permute-done | bytes 589856 | tf_op jit(solution)/shard_map/ppermute | solution.py:52
  110.6 5.2 %collective-permute-done.29.refs_9_.refs_5_ = bf16[128,1152]{1,0:T(8,128)(2,1)S(1)} collective-permute-done((bf16[128,1152]{1,0:T(8,128)(2,1)S(1)}, bf16[128,1152]{1,0:T(8,128)(2,1)S(1)}, u32[]{:S(2)}, u32[]{:S(2)}) %collective-permute-start.29) | collective-permute-done | bytes 294944 | tf_op jit(solution)/shard_map/ppermute | solution.py:52
  115.8 6.1 %collective-permute-done.25.refs_4_ = bf16[128,1152]{1,0:T(8,128)(2,1)S(1)} collective-permute-done((bf16[128,1152]{1,0:T(8,128)(2,1)S(1)}, bf16[128,1152]{1,0:T(8,128)(2,1)S(1)}, u32[]{:S(2)}, u32[]{:S(2)}) %collective-permute-start.25) | collective-permute-done | bytes 294944 | tf_op jit(solution)/shard_map/ppermute | solution.py:52
  121.9 17.6 %mlp.1 = (bf16[1024,1152]{1,0:T(8,128)(2,1)S(1)}, bf16[1024,1152]{1,0:T(8,128)(2,1)S(1)}, f32[8,1152]{1,0:T(8,128)S(1)}, bf16[256,1152]{1,0:T(8,128)(2,1)S(1)}, ...) custom-call(bf16[256,1152]{1,0:T(8,128)(2,1)S(1)} %get-tuple-element, ...), custom_call_target="tpu_custom_call" | custom-call | flops 1000 | bytes 1000 | tf_op jit(solution)/shard_map/mlp/pallas_call | solution.py:243
  141.4 1.7 collective-permute-start.35
  143.1 4.2 %fc2_wgrad.1.refs_6_.refs_0_ = bf16[1152,1152]{1,0:T(8,128)(2,1)S(1)} custom-call(bf16[1024,1152]{1,0:T(8,128)(2,1)S(1)} %get-tuple-element.150.refs_0_, bf16[256,1152]{1,0:T(8,128)(2,1)S(1)} %get-tuple-element.135.refs_5_.refs_1_, bf16[256,1152]{1,0:T(8,128)(2,1)S(1)} %collective-permute-done.26.refs_6_.refs_2_, ...), custom_call_target="tpu_custom_call" | custom-call | flops 1000 | bytes 1000 | tf_op jit(solution)/shard_map/fc2_wgrad/pallas_call | solution.py:243
  147.4 4.0 %fc1_wgrad.1.refs_11_.refs_0_ = bf16[1152,1152]{1,0:T(8,128)(2,1)S(1)} custom-call(bf16[256,1152]{1,0:T(8,128)(2,1)S(1)} %copy-done.18, bf16[256,1152]{1,0:T(8,128)(2,1)S(1)} %collective-permute-done.22.refs_1_, bf16[256,1152]{1,0:T(8,128)(2,1)S(1)} %collective-permute-done.23.refs_2_, bf16[128,1152]{1,0:T(8,128)(2,1)S(1)} %collective-permute-done.24.refs_3_, ...), custom_call_target="tpu_custom_call" | custom-call | flops 1000 | bytes 1000 | tf_op jit(solution)/shard_map/fc1_wgrad/pallas_call | solution.py:243
  151.4 4.4 %collective-permute-done.33.refs_1_ = bf16[256,1152]{1,0:T(8,128)(2,1)S(1)} collective-permute-done((bf16[256,1152]{1,0:T(8,128)(2,1)S(1)}, bf16[256,1152]{1,0:T(8,128)(2,1)S(1)}, u32[]{:S(2)}, u32[]{:S(2)}) %collective-permute-start.33) | collective-permute-done | bytes 589856 | tf_op jit(solution)/shard_map/ppermute | solution.py:52
  155.8 12.2 %collective-permute-done.34.refs_2_ = bf16[256,1152]{1,0:T(8,128)(2,1)S(1)} collective-permute-done((bf16[256,1152]{1,0:T(8,128)(2,1)S(1)}, bf16[256,1152]{1,0:T(8,128)(2,1)S(1)}, u32[]{:S(2)}, u32[]{:S(2)}) %collective-permute-start.34) | collective-permute-done | bytes 589856 | tf_op jit(solution)/shard_map/ppermute | solution.py:52
  168.1 4.1 %turn.1 = (f32[256,1152]{1,0:T(8,128)S(1)}, bf16[256,1152]{1,0:T(8,128)(2,1)S(1)}, f32[16,4608]{1,0:T(8,128)S(1)}, bf16[256,288]{1,0:T(8,128)(2,1)S(1)}, bf16[25...) custom-call(bf16[256,1152]{1,0:T(8,128)(2,1)S(1)} %get-tuple-element.143.refs_0_, ...), custom_call_target="tpu_custom_call" | custom-call | flops 1000 | bytes 1000 | tf_op jit(solution)/shard_map/turn/pallas_call | solution.py:243
  172.9 1.7 collective-permute-start.40
  176.3 3.8 collective-permute-done.38.refs_2_
  180.1 3.3 collective-permute-done.40.refs_4_
  183.5 15.2 %attend_back.1.refs_2_.refs_4_ = bf16[1024,864]{1,0:T(8,128)(2,1)S(1)} custom-call(bf16[1024,864]{1,0:T(8,128)(2,1)S(1)} %copy-done.28, bf16[256,288]{1,0:T(8,128)(2,1)S(1)} %get-tuple-element.157.refs_1_, bf16[256,288]{1,0:T(8,128)(2,1)S(1)} %collective-permute-done.38.refs_2_, bf16[256,288]{1,0:T(8,128)(2,1)S(1)} %collective-permute-done.39.refs_3_, ...), custom_call_target="tpu_custom_call" | custom-call | flops 1000 | bytes 1000 | tf_op jit(solution)/shard_map/attend_back/pallas_call | solution.py:243
  204.4 1.6 collective-permute-start.32
  206.2 1.8 collective-permute-start.44
  208.9 3.3 qkv_wgrad.1
  212.2 8.2 %collective-permute-done.37.refs_1_ = bf16[288,1152]{1,0:T(8,128)(2,1)S(1)} collective-permute-done((bf16[288,1152]{1,0:T(8,128)(2,1)S(1)}, bf16[288,1152]{1,0:T(8,128)(2,1)S(1)}, u32[]{:S(2)}, u32[]{:S(2)}) %collective-permute-start.37) | collective-permute-done | bytes 663584 | tf_op jit(solution)/shard_map/ppermute | solution.py:52
  221.3 8.0 %collective-permute-done.31.refs_2_ = bf16[256,1152]{1,0:T(8,128)(2,1)S(1)} collective-permute-done((bf16[256,1152]{1,0:T(8,128)(2,1)S(1)}, bf16[256,1152]{1,0:T(8,128)(2,1)S(1)}, u32[]{:S(2)}, u32[]{:S(2)}) %collective-permute-start.31) | collective-permute-done | bytes 589856 | tf_op jit(solution)/shard_map/ppermute | solution.py:52
  233.0 7.1 %collective-permute-done.44.refs_2_ = bf16[256,1152]{1,0:T(8,128)(2,1)S(1)} collective-permute-done((bf16[256,1152]{1,0:T(8,128)(2,1)S(1)}, bf16[256,1152]{1,0:T(8,128)(2,1)S(1)}, u32[]{:S(2)}, u32[]{:S(2)}) %collective-permute-start.44) | collective-permute-done | bytes 589856 | tf_op jit(solution)/shard_map/ppermute | solution.py:52
  240.1 2.2 finish.1
  245.9 21.7 %collective-permute-done.51.refs_2_ = bf16[288,864]{1,0:T(8,128)(2,1)S(1)} collective-permute-done((bf16[288,864]{1,0:T(8,128)(2,1)S(1)}, bf16[288,864]{1,0:T(8,128)(2,1)S(1)}, u32[]{:S(2)}, u32[]{:S(2)}) %collective-permute-start.51) | collective-permute-done | bytes 497696 | tf_op jit(solution)/shard_map/ppermute | solution.py:52
  269.3 2.3 collective-permute-start.57
  274.4 11.9 %collective-permute-done.58.refs_1_ = bf16[8,6912]{1,0:T(8,128)(2,1)S(1)} collective-permute-done((bf16[8,6912]{1,0:T(8,128)(2,1)S(1)}, bf16[8,6912]{1,0:T(8,128)(2,1)S(1)}, u32[]{:S(2)}, u32[]{:S(2)}) %collective-permute-start.58) | collective-permute-done | bytes 110624 | tf_op jit(solution)/shard_map/ppermute | solution.py:52
  286.3 1.6 collective-permute-start.56
  288.0 5.2 %collective-permute-done.57.refs_1_ = bf16[144,1152]{1,0:T(8,128)(2,1)S(1)} collective-permute-done((bf16[144,1152]{1,0:T(8,128)(2,1)S(1)}, bf16[144,1152]{1,0:T(8,128)(2,1)S(1)}, u32[]{:S(2)}, u32[]{:S(2)}) %collective-permute-start.57) | collective-permute-done | bytes 331808 | tf_op jit(solution)/shard_map/ppermute | solution.py:52
  293.2 3.2 collective-permute-done.56.refs_3_
  296.9 3.4 collective-permute-start.70
  300.4 1.6 collective-permute-start.62
  304.1 4.7 %collective-permute-done.62.refs_3_ = bf16[16,6912]{1,0:T(8,128)(2,1)S(1)} collective-permute-done((bf16[16,6912]{1,0:T(8,128)(2,1)S(1)}, bf16[16,6912]{1,0:T(8,128)(2,1)S(1)}, u32[]{:S(2)}, u32[]{:S(2)}) %collective-permute-start.62) | collective-permute-done | bytes 221216 | tf_op jit(solution)/shard_map/ppermute | solution.py:52
  309.8 3.7 collective-permute-done.61.refs_2_
  313.8 1.7 collective-permute-done.60.refs_1_
  315.5 5.4 %ada.1 = (f32[288,6912]{1,0:T(8,128)}, f32[8,6912]{1,0:T(8,128)S(1)}, f32[8,288]{1,0:T(8,128)S(1)}, f32[8,288]{1,0:T(8,128)S(1)}, f32[8,288]{1,0:T(8,128)S(1)}, /*index=5*/f32[8,288]{1,0:T(8,128)S(1)}) custom-call(bf16[16,6912]{1,0:T(8,128)(2,1)S(1)} %both.1.refs_2_.refs_0_, bf16[16,6912]{1,0:T(8,128)(2,1)S(1)} %collective-permute-done.60.refs_1_, ...), custom_call_target="tpu_custom_call" | custom-call | flops 1000 | bytes 1000 | tf_op jit(solution)/shard_map/ada/pallas_call | solution.py:243
  321.6 9.1 %collective-permute-done.70.refs_1_ = bf16[288,864]{1,0:T(8,128)(2,1)S(1)} collective-permute-done((bf16[288,864]{1,0:T(8,128)(2,1)S(1)}, bf16[288,864]{1,0:T(8,128)(2,1)S(1)}, u32[]{:S(2)}, u32[]{:S(2)}) %collective-permute-start.70) | collective-permute-done | bytes 497696 | tf_op jit(solution)/shard_map/ppermute | solution.py:52
  335.2 3.1 place_fc2.1.refs_5_
  338.6 2.5 copy-done
  342.7 2.0 collective-permute-start.76
  344.7 4.3 %collective-permute-done.73.refs_2_ = bf16[288,864]{1,0:T(8,128)(2,1)S(1)} collective-permute-done((bf16[288,864]{1,0:T(8,128)(2,1)S(1)}, bf16[288,864]{1,0:T(8,128)(2,1)S(1)}, u32[]{:S(2)}, u32[]{:S(2)}) %collective-permute-start.73) | collective-permute-done | bytes 497696 | tf_op jit(solution)/shard_map/ppermute | solution.py:52
  349.6 2.3 collective-permute-start.75
  353.3 9.8 %collective-permute-done.76.refs_1_ = bf16[288,1152]{1,0:T(8,128)(2,1)S(1)} collective-permute-done((bf16[288,1152]{1,0:T(8,128)(2,1)S(1)}, bf16[288,1152]{1,0:T(8,128)(2,1)S(1)}, u32[]{:S(2)}, u32[]{:S(2)}) %collective-permute-start.76) | collective-permute-done | bytes 663584 | tf_op jit(solution)/shard_map/ppermute | solution.py:52
  364.5 8.3 %collective-permute-done.75.refs_1_ = bf16[128,1152]{1,0:T(8,128)(2,1)S(1)} collective-permute-done((bf16[128,1152]{1,0:T(8,128)(2,1)S(1)}, bf16[128,1152]{1,0:T(8,128)(2,1)S(1)}, u32[]{:S(2)}, u32[]{:S(2)}) %collective-permute-start.75) | collective-permute-done | bytes 294944 | tf_op jit(solution)/shard_map/ppermute | solution.py:52
  377.6 2.7 place_qkv.1.refs_2_
  380.3 2.1 copy-done.2
  382.6 6.7 %collective-permute-done.43.refs_1_ = bf16[128,1152]{1,0:T(8,128)(2,1)S(1)} collective-permute-done((bf16[128,1152]{1,0:T(8,128)(2,1)S(1)}, bf16[128,1152]{1,0:T(8,128)(2,1)S(1)}, u32[]{:S(2)}, u32[]{:S(2)}) %collective-permute-start.43) | collective-permute-done | bytes 294944 | tf_op jit(solution)/shard_map/ppermute | solution.py:52
  394.8 2.9 place_fc1.1
  (271 shorter events, 81.4 us)
Async XLA Ops:
  4.6 31.0 %collective-permute-start = (bf16[128,1152]{1,0:T(8,128)(2,1)S(1)}, bf16[128,1152]{1,0:T(8,128)(2,1)S(1)}, u32[]{:S(2)}, u32[]{:S(2)}) collective-permute-start(bf16[128,1152]{1,0:T(8,128)(2,1)S(1)} %get-tuple-element.109), channel_id=1, source_target_pairs={{0,4},{1,5},{2,6},{3,7},{4,0},{5,1},{6,2},{7,3},{8,12},{9,13},{10,... | collective-permute-start | bytes 884744 | tf_op jit(solution)/shard_map/ppermute | solution.py:52
  13.4 25.4 %collective-permute-start.11 = (bf16[288,864]{1,0:T(8,128)(2,1)S(1)}, bf16[288,864]{1,0:T(8,128)(2,1)S(1)}, u32[]{:S(2)}, u32[]{:S(2)}) collective-permute-start(bf16[288,864]{1,0:T(8,128)(2,1)S(1)} %qkv_cols.1.refs_6_.refs_4_), channel_id=1, source_target_pairs={{0,16},{8,24},{16,0},{24,8},{1,17},{9,25},{17,1},{25,9},{2,18},{10... | collective-permute-start | bytes 1493000 | tf_op jit(solution)/shard_map/ppermute | solution.py:52
  14.9 25.0 %collective-permute-start.10 = (bf16[288,864]{1,0:T(8,128)(2,1)S(1)}, bf16[288,864]{1,0:T(8,128)(2,1)S(1)}, u32[]{:S(2)}, u32[]{:S(2)}) collective-permute-start(bf16[288,864]{1,0:T(8,128)(2,1)S(1)} %qkv_cols.1.refs_6_.refs_4_), channel_id=1, source_target_pairs={{0,8},{8,0},{16,24},{24,16},{1,9},{9,1},{17,25},{25,17},{2,10},{10... | collective-permute-start | bytes 1493000 | tf_op jit(solution)/shard_map/ppermute | solution.py:52
  18.2 11.6 %collective-permute-start.4 = (f32[4,6912]{1,0:T(4,128)S(1)}, f32[4,6912]{1,0:T(4,128)S(1)}, u32[]{:S(2)}, u32[]{:S(2)}) collective-permute-start(f32[4,6912]{1,0:T(4,128)S(1)} %get-tuple-element.114), channel_id=1, source_target_pairs={{0,8},{8,0},{16,24},{24,16},{1,9},{9,1},{17,25},{25,17},{2,10},{10... | collective-permute-start | bytes 331784 | tf_op jit(solution)/shard_map/ppermute | solution.py:52
  18.5 13.0 %collective-permute-start.5 = (f32[4,6912]{1,0:T(4,128)S(1)}, f32[4,6912]{1,0:T(4,128)S(1)}, u32[]{:S(2)}, u32[]{:S(2)}) collective-permute-start(f32[4,6912]{1,0:T(4,128)S(1)} %get-tuple-element.115), channel_id=1, source_target_pairs={{0,16},{8,24},{16,0},{24,8},{1,17},{9,25},{17,1},{25,9},{2,18},{10... | collective-permute-start | bytes 331784 | tf_op jit(solution)/shard_map/ppermute | solution.py:52
  37.0 12.6 %collective-permute-start.7 = (bf16[256,1152]{1,0:T(8,128)(2,1)S(1)}, bf16[256,1152]{1,0:T(8,128)(2,1)S(1)}, u32[]{:S(2)}, u32[]{:S(2)}) collective-permute-start(bf16[256,1152]{1,0:T(8,128)(2,1)S(1)} %get-tuple-element.118.refs_1_.refs_0_), channel_id=1, source_target_pairs={{0,2},{1,3},{2,0},{3,1},{4,6},{5,7},{6,4},{7,5},{8,10},{9,11},{10,... | collective-permute-start | bytes 1769480 | tf_op jit(solution)/shard_map/ppermute | solution.py:52
  39.9 7.7 %collective-permute-start.12 = (bf16[144,864]{1,0:T(8,128)(2,1)S(1)}, bf16[144,864]{1,0:T(8,128)(2,1)S(1)}, u32[]{:S(2)}, u32[]{:S(2)}) collective-permute-start(bf16[144,864]{1,0:T(8,128)(2,1)S(1)} %slice.32), channel_id=1, source_target_pairs={{0,16},{8,24},{16,0},{24,8},{1,17},{9,25},{17,1},{25,9},{2,18},{10... | collective-permute-start | bytes 746504 | tf_op jit(solution)/shard_map/ppermute | solution.py:52
  41.3 8.4 %collective-permute-start.8 = (bf16[256,1152]{1,0:T(8,128)(2,1)S(1)}, bf16[256,1152]{1,0:T(8,128)(2,1)S(1)}, u32[]{:S(2)}, u32[]{:S(2)}) collective-permute-start(bf16[256,1152]{1,0:T(8,128)(2,1)S(1)} %get-tuple-element.118.refs_1_.refs_0_), channel_id=1, source_target_pairs={{0,1},{1,0},{2,3},{3,2},{4,5},{5,4},{6,7},{7,6},{8,9},{9,8},{10,11... | collective-permute-start | bytes 1769480 | tf_op jit(solution)/shard_map/ppermute | solution.py:52
  41.3 31.6 %collective-permute-start.17 = (bf16[288,1152]{1,0:T(8,128)(2,1)S(1)}, bf16[288,1152]{1,0:T(8,128)(2,1)S(1)}, u32[]{:S(2)}, u32[]{:S(2)}) collective-permute-start(bf16[288,1152]{1,0:T(8,128)(2,1)S(1)} %get-tuple-element.125), channel_id=1, source_target_pairs={{0,8},{8,0},{16,24},{24,16},{1,9},{9,1},{17,25},{25,17},{2,10},{10... | collective-permute-start | bytes 1990664 | tf_op jit(solution)/shard_map/ppermute | solution.py:52
  45.8 28.9 %collective-permute-start.18 = (bf16[288,1152]{1,0:T(8,128)(2,1)S(1)}, bf16[288,1152]{1,0:T(8,128)(2,1)S(1)}, u32[]{:S(2)}, u32[]{:S(2)}) collective-permute-start(bf16[288,1152]{1,0:T(8,128)(2,1)S(1)} %get-tuple-element.126), channel_id=1, source_target_pairs={{0,16},{8,24},{16,0},{24,8},{1,17},{9,25},{17,1},{25,9},{2,18},{10... | collective-permute-start | bytes 1990664 | tf_op jit(solution)/shard_map/ppermute | solution.py:52
  47.6 27.2 %collective-permute-start.19 = (bf16[288,1152]{1,0:T(8,128)(2,1)S(1)}, bf16[288,1152]{1,0:T(8,128)(2,1)S(1)}, u32[]{:S(2)}, u32[]{:S(2)}) collective-permute-start(bf16[288,1152]{1,0:T(8,128)(2,1)S(1)} %get-tuple-element.127), channel_id=1, source_target_pairs={{0,24},{8,16},{16,8},{24,0},{1,25},{9,17},{17,9},{25,1},{2,26},{10... | collective-permute-start | bytes 1990664 | tf_op jit(solution)/shard_map/ppermute | solution.py:52
  49.7 22.0 %collective-permute-start.20 = (bf16[128,1152]{1,0:T(8,128)(2,1)S(1)}, bf16[128,1152]{1,0:T(8,128)(2,1)S(1)}, u32[]{:S(2)}, u32[]{:S(2)}) collective-permute-start(bf16[128,1152]{1,0:T(8,128)(2,1)S(1)} %get-tuple-element.128), channel_id=1, source_target_pairs={{0,4},{1,5},{2,6},{3,7},{4,0},{5,1},{6,2},{7,3},{8,12},{9,13},{10,... | collective-permute-start | bytes 884744 | tf_op jit(solution)/shard_map/ppermute | solution.py:52
  75.0 10.8 %collective-permute-start.21 = (bf16[4,288,1152]{2,1,0:T(8,128)(2,1)S(1)}, bf16[4,288,1152]{2,1,0:T(8,128)(2,1)S(1)}, u32[]{:S(2)}, u32[]{:S(2)}) collective-permute-start(bf16[4,288,1152]{2,1,0:T(8,128)(2,1)S(1)} %stack.1.refs_4_.refs_10_), channel_id=1, source_target_pairs={{0,1},{1,0},{2,3},{3,2},{4,5},{5,4},{6,7},{7,6},{8,9},{9,8},{10,11... | collective-permute-start | bytes 7962632 | tf_op jit(solution)/shard_map/ppermute | solution.py:52
  75.5 7.8 %collective-permute-start.15 = (bf16[256,288]{1,0:T(8,128)(2,1)S(1)}, bf16[256,288]{1,0:T(8,128)(2,1)S(1)}, u32[]{:S(2)}, u32[]{:S(2)}) collective-permute-start(bf16[256,288]{1,0:T(8,128)(2,1)S(1)} %get-tuple-element.123), channel_id=1, source_target_pairs={{0,2},{1,3},{2,0},{3,1},{4,6},{5,7},{6,4},{7,5},{8,10},{9,11},{10,... | collective-permute-start | bytes 442376 | tf_op jit(solution)/shard_map/ppermute | solution.py:52
  75.9 9.8 %collective-permute-start.16 = (bf16[256,288]{1,0:T(8,128)(2,1)S(1)}, bf16[256,288]{1,0:T(8,128)(2,1)S(1)}, u32[]{:S(2)}, u32[]{:S(2)}) collective-permute-start(bf16[256,288]{1,0:T(8,128)(2,1)S(1)} %get-tuple-element.124), channel_id=1, source_target_pairs={{0,3},{1,2},{2,1},{3,0},{4,7},{5,6},{6,5},{7,4},{8,11},{9,10},{10,... | collective-permute-start | bytes 442376 | tf_op jit(solution)/shard_map/ppermute | solution.py:52
  77.0 17.2 %collective-permute-start.27 = (bf16[256,1152]{1,0:T(8,128)(2,1)S(1)}, bf16[256,1152]{1,0:T(8,128)(2,1)S(1)}, u32[]{:S(2)}, u32[]{:S(2)}) collective-permute-start(bf16[256,1152]{1,0:T(8,128)(2,1)S(1)} %get-tuple-element.135.refs_5_.refs_1_), channel_id=1, source_target_pairs={{0,16},{8,24},{16,0},{24,8},{1,17},{9,25},{17,1},{25,9},{2,18},{10... | collective-permute-start | bytes 1769480 | tf_op jit(solution)/shard_map/ppermute | solution.py:52
  80.3 15.4 %collective-permute-start.26 = (bf16[256,1152]{1,0:T(8,128)(2,1)S(1)}, bf16[256,1152]{1,0:T(8,128)(2,1)S(1)}, u32[]{:S(2)}, u32[]{:S(2)}) collective-permute-start(bf16[256,1152]{1,0:T(8,128)(2,1)S(1)} %get-tuple-element.135.refs_5_.refs_1_), channel_id=1, source_target_pairs={{0,8},{8,0},{16,24},{24,16},{1,9},{9,1},{17,25},{25,17},{2,10},{10... | collective-permute-start | bytes 1769480 | tf_op jit(solution)/shard_map/ppermute | solution.py:52
  91.9 16.2 %collective-permute-start.23 = (bf16[256,1152]{1,0:T(8,128)(2,1)S(1)}, bf16[256,1152]{1,0:T(8,128)(2,1)S(1)}, u32[]{:S(2)}, u32[]{:S(2)}) collective-permute-start(bf16[256,1152]{1,0:T(8,128)(2,1)S(1)} %get-tuple-element.134.refs_0_), channel_id=1, source_target_pairs={{0,16},{8,24},{16,0},{24,8},{1,17},{9,25},{17,1},{25,9},{2,18},{10... | collective-permute-start | bytes 1769480 | tf_op jit(solution)/shard_map/ppermute | solution.py:52
  93.3 16.2 %collective-permute-start.22 = (bf16[256,1152]{1,0:T(8,128)(2,1)S(1)}, bf16[256,1152]{1,0:T(8,128)(2,1)S(1)}, u32[]{:S(2)}, u32[]{:S(2)}) collective-permute-start(bf16[256,1152]{1,0:T(8,128)(2,1)S(1)} %get-tuple-element.134.refs_0_), channel_id=1, source_target_pairs={{0,8},{8,0},{16,24},{24,16},{1,9},{9,1},{17,25},{25,17},{2,10},{10... | collective-permute-start | bytes 1769480 | tf_op jit(solution)/shard_map/ppermute | solution.py:52
  94.2 21.6 %collective-permute-start.29 = (bf16[128,1152]{1,0:T(8,128)(2,1)S(1)}, bf16[128,1152]{1,0:T(8,128)(2,1)S(1)}, u32[]{:S(2)}, u32[]{:S(2)}) collective-permute-start(bf16[128,1152]{1,0:T(8,128)(2,1)S(1)} %slice.37), channel_id=1, source_target_pairs={{0,8},{8,0},{16,24},{24,16},{1,9},{9,1},{17,25},{25,17},{2,10},{10... | collective-permute-start | bytes 884744 | tf_op jit(solution)/shard_map/ppermute | solution.py:52
  95.7 20.1 %collective-permute-start.28 = (bf16[128,1152]{1,0:T(8,128)(2,1)S(1)}, bf16[128,1152]{1,0:T(8,128)(2,1)S(1)}, u32[]{:S(2)}, u32[]{:S(2)}) collective-permute-start(bf16[128,1152]{1,0:T(8,128)(2,1)S(1)} %slice.36), channel_id=1, source_target_pairs={{0,16},{8,24},{16,0},{24,8},{1,17},{9,25},{17,1},{25,9},{2,18},{10... | collective-permute-start | bytes 884744 | tf_op jit(solution)/shard_map/ppermute | solution.py:52
  108.2 13.6 %collective-permute-start.25 = (bf16[128,1152]{1,0:T(8,128)(2,1)S(1)}, bf16[128,1152]{1,0:T(8,128)(2,1)S(1)}, u32[]{:S(2)}, u32[]{:S(2)}) collective-permute-start(bf16[128,1152]{1,0:T(8,128)(2,1)S(1)} %slice.35), channel_id=1, source_target_pairs={{0,8},{8,0},{16,24},{24,16},{1,9},{9,1},{17,25},{25,17},{2,10},{10... | collective-permute-start | bytes 884744 | tf_op jit(solution)/shard_map/ppermute | solution.py:52
  109.5 12.4 %collective-permute-start.24 = (bf16[128,1152]{1,0:T(8,128)(2,1)S(1)}, bf16[128,1152]{1,0:T(8,128)(2,1)S(1)}, u32[]{:S(2)}, u32[]{:S(2)}) collective-permute-start(bf16[128,1152]{1,0:T(8,128)(2,1)S(1)} %slice.34), channel_id=1, source_target_pairs={{0,16},{8,24},{16,0},{24,8},{1,17},{9,25},{17,1},{25,9},{2,18},{10... | collective-permute-start | bytes 884744 | tf_op jit(solution)/shard_map/ppermute | solution.py:52
  139.6 16.3 %collective-permute-start.33 = (bf16[256,1152]{1,0:T(8,128)(2,1)S(1)}, bf16[256,1152]{1,0:T(8,128)(2,1)S(1)}, u32[]{:S(2)}, u32[]{:S(2)}) collective-permute-start(bf16[256,1152]{1,0:T(8,128)(2,1)S(1)} %get-tuple-element.144), channel_id=1, source_target_pairs={{0,8},{8,0},{16,24},{24,16},{1,9},{9,1},{17,25},{25,17},{2,10},{10... | collective-permute-start | bytes 1769480 | tf_op jit(solution)/shard_map/ppermute | solution.py:52
  140.6 27.4 %collective-permute-start.34 = (bf16[256,1152]{1,0:T(8,128)(2,1)S(1)}, bf16[256,1152]{1,0:T(8,128)(2,1)S(1)}, u32[]{:S(2)}, u32[]{:S(2)}) collective-permute-start(bf16[256,1152]{1,0:T(8,128)(2,1)S(1)} %get-tuple-element.145), channel_id=1, source_target_pairs={{0,16},{8,24},{16,0},{24,8},{1,17},{9,25},{17,1},{25,9},{2,18},{10... | collective-permute-start | bytes 1769480 | tf_op jit(solution)/shard_map/ppermute | solution.py:52
  141.4 26.7 %collective-permute-start.35 = (bf16[256,1152]{1,0:T(8,128)(2,1)S(1)}, bf16[256,1152]{1,0:T(8,128)(2,1)S(1)}, u32[]{:S(2)}, u32[]{:S(2)}) collective-permute-start(bf16[256,1152]{1,0:T(8,128)(2,1)S(1)} %get-tuple-element.146), channel_id=1, source_target_pairs={{0,24},{8,16},{16,8},{24,0},{1,25},{9,17},{17,9},{25,1},{2,26},{10... | collective-permute-start | bytes 1769480 | tf_op jit(solution)/shard_map/ppermute | solution.py:52
  172.4 7.8 %collective-permute-start.38 = (bf16[256,288]{1,0:T(8,128)(2,1)S(1)}, bf16[256,288]{1,0:T(8,128)(2,1)S(1)}, u32[]{:S(2)}, u32[]{:S(2)}) collective-permute-start(bf16[256,288]{1,0:T(8,128)(2,1)S(1)} %get-tuple-element.158), channel_id=1, source_target_pairs={{0,2},{1,3},{2,0},{3,1},{4,6},{5,7},{6,4},{7,5},{8,10},{9,11},{10,... | collective-permute-start | bytes 442376 | tf_op jit(solution)/shard_map/ppermute | solution.py:52
  172.9 10.6 %collective-permute-start.40 = (bf16[256,288]{1,0:T(8,128)(2,1)S(1)}, bf16[256,288]{1,0:T(8,128)(2,1)S(1)}, u32[]{:S(2)}, u32[]{:S(2)}) collective-permute-start(bf16[256,288]{1,0:T(8,128)(2,1)S(1)} %get-tuple-element.160), channel_id=1, source_target_pairs={{0,3},{1,2},{2,1},{3,0},{4,7},{5,6},{6,5},{7,4},{8,11},{9,10},{10,... | collective-permute-start | bytes 442376 | tf_op jit(solution)/shard_map/ppermute | solution.py:52
  174.8 31.4 %collective-permute-start.41 = (bf16[576,1152]{1,0:T(8,128)(2,1)S(1)}, bf16[576,1152]{1,0:T(8,128)(2,1)S(1)}, u32[]{:S(2)}, u32[]{:S(2)}) collective-permute-start(bf16[576,1152]{1,0:T(8,128)(2,1)S(1)} %fc1_other.1.refs_2_), channel_id=1, source_target_pairs={{0,1},{1,0},{2,3},{3,2},{4,5},{5,4},{6,7},{7,6},{8,9},{9,8},{10,11... | collective-permute-start | bytes 3981320 | tf_op jit(solution)/shard_map/ppermute | solution.py:52
  200.6 20.3 %collective-permute-start.30 = (bf16[256,1152]{1,0:T(8,128)(2,1)S(1)}, bf16[256,1152]{1,0:T(8,128)(2,1)S(1)}, u32[]{:S(2)}, u32[]{:S(2)}) collective-permute-start(bf16[256,1152]{1,0:T(8,128)(2,1)S(1)} %copy-done.50), channel_id=1, source_target_pairs={{0,8},{8,0},{16,24},{24,16},{1,9},{9,1},{17,25},{25,17},{2,10},{10... | collective-permute-start | bytes 1769480 | tf_op jit(solution)/shard_map/ppermute | solution.py:52
  201.7 27.6 %collective-permute-start.31 = (bf16[256,1152]{1,0:T(8,128)(2,1)S(1)}, bf16[256,1152]{1,0:T(8,128)(2,1)S(1)}, u32[]{:S(2)}, u32[]{:S(2)}) collective-permute-start(bf16[256,1152]{1,0:T(8,128)(2,1)S(1)} %copy-done.48), channel_id=1, source_target_pairs={{0,16},{8,24},{16,0},{24,8},{1,17},{9,25},{17,1},{25,9},{2,18},{10... | collective-permute-start | bytes 1769480 | tf_op jit(solution)/shard_map/ppermute | solution.py:52
  202.5 17.8 %collective-permute-start.37 = (bf16[288,1152]{1,0:T(8,128)(2,1)S(1)}, bf16[288,1152]{1,0:T(8,128)(2,1)S(1)}, u32[]{:S(2)}, u32[]{:S(2)}) collective-permute-start(bf16[288,1152]{1,0:T(8,128)(2,1)S(1)} %get-tuple-element.155), channel_id=1, source_target_pairs={{0,2},{1,3},{2,0},{3,1},{4,6},{5,7},{6,4},{7,5},{8,10},{9,11},{10,... | collective-permute-start | bytes 1990664 | tf_op jit(solution)/shard_map/ppermute | solution.py:52
  204.4 27.3 %collective-permute-start.32 = (bf16[256,1152]{1,0:T(8,128)(2,1)S(1)}, bf16[256,1152]{1,0:T(8,128)(2,1)S(1)}, u32[]{:S(2)}, u32[]{:S(2)}) collective-permute-start(bf16[256,1152]{1,0:T(8,128)(2,1)S(1)} %get-tuple-element.140), channel_id=1, source_target_pairs={{0,24},{8,16},{16,8},{24,0},{1,25},{9,17},{17,9},{25,1},{2,26},{10... | collective-permute-start | bytes 1769480 | tf_op jit(solution)/shard_map/ppermute | solution.py:52
  206.2 33.9 %collective-permute-start.44 = (bf16[256,1152]{1,0:T(8,128)(2,1)S(1)}, bf16[256,1152]{1,0:T(8,128)(2,1)S(1)}, u32[]{:S(2)}, u32[]{:S(2)}) collective-permute-start(bf16[256,1152]{1,0:T(8,128)(2,1)S(1)} %attn_sum.1.refs_2_), channel_id=1, source_target_pairs={{0,2},{1,3},{2,0},{3,1},{4,6},{5,7},{6,4},{7,5},{8,10},{9,11},{10,... | collective-permute-start | bytes 1769480 | tf_op jit(solution)/shard_map/ppermute | solution.py:52
  220.6 23.1 %collective-permute-start.46 = (bf16[144,1152]{1,0:T(8,128)(2,1)S(1)}, bf16[144,1152]{1,0:T(8,128)(2,1)S(1)}, u32[]{:S(2)}, u32[]{:S(2)}) collective-permute-start(bf16[144,1152]{1,0:T(8,128)(2,1)S(1)} %get-tuple-element.171), channel_id=1, source_target_pairs={{0,4},{1,5},{2,6},{3,7},{4,0},{5,1},{6,2},{7,3},{8,12},{9,13},{10,... | collective-permute-start | bytes 995336 | tf_op jit(solution)/shard_map/ppermute | solution.py:52
  221.0 46.9 %collective-permute-start.49 = (bf16[288,1152]{1,0:T(8,128)(2,1)S(1)}, bf16[288,1152]{1,0:T(8,128)(2,1)S(1)}, u32[]{:S(2)}, u32[]{:S(2)}) collective-permute-start(bf16[288,1152]{1,0:T(8,128)(2,1)S(1)} %get-tuple-element.172), channel_id=1, source_target_pairs={{0,2},{1,3},{2,0},{3,1},{4,6},{5,7},{6,4},{7,5},{8,10},{9,11},{10,... | collective-permute-start | bytes 1990664 | tf_op jit(solution)/shard_map/ppermute | solution.py:52
  229.3 15.7 %collective-permute-start.50 = (bf16[288,864]{1,0:T(8,128)(2,1)S(1)}, bf16[288,864]{1,0:T(8,128)(2,1)S(1)}, u32[]{:S(2)}, u32[]{:S(2)}) collective-permute-start(bf16[288,864]{1,0:T(8,128)(2,1)S(1)} %get-tuple-element.174), channel_id=1, source_target_pairs={{0,8},{8,0},{16,24},{24,16},{1,9},{9,1},{17,25},{25,17},{2,10},{10... | collective-permute-start | bytes 1493000 | tf_op jit(solution)/shard_map/ppermute | solution.py:52
  242.4 25.2 %collective-permute-start.51 = (bf16[288,864]{1,0:T(8,128)(2,1)S(1)}, bf16[288,864]{1,0:T(8,128)(2,1)S(1)}, u32[]{:S(2)}, u32[]{:S(2)}) collective-permute-start(bf16[288,864]{1,0:T(8,128)(2,1)S(1)} %get-tuple-element.175), channel_id=1, source_target_pairs={{0,16},{8,24},{16,0},{24,8},{1,17},{9,25},{17,1},{25,9},{2,18},{10... | collective-permute-start | bytes 1493000 | tf_op jit(solution)/shard_map/ppermute | solution.py:52
  243.7 24.0 %collective-permute-start.52 = (bf16[288,864]{1,0:T(8,128)(2,1)S(1)}, bf16[288,864]{1,0:T(8,128)(2,1)S(1)}, u32[]{:S(2)}, u32[]{:S(2)}) collective-permute-start(bf16[288,864]{1,0:T(8,128)(2,1)S(1)} %get-tuple-element.176), channel_id=1, source_target_pairs={{0,24},{8,16},{16,8},{24,0},{1,25},{9,17},{17,9},{25,1},{2,26},{10... | collective-permute-start | bytes 1493000 | tf_op jit(solution)/shard_map/ppermute | solution.py:52
  245.0 23.2 %collective-permute-start.48 = (bf16[144,1152]{1,0:T(8,128)(2,1)S(1)}, bf16[144,1152]{1,0:T(8,128)(2,1)S(1)}, u32[]{:S(2)}, u32[]{:S(2)}) collective-permute-start(bf16[144,1152]{1,0:T(8,128)(2,1)S(1)} %fc2_cube.5.refs_2_.refs_0_), channel_id=1, source_target_pairs={{0,4},{1,5},{2,6},{3,7},{4,0},{5,1},{6,2},{7,3},{8,12},{9,13},{10,... | collective-permute-start | bytes 995336 | tf_op jit(solution)/shard_map/ppermute | solution.py:52
  245.1 23.2 %collective-permute-start.47 = (bf16[8,6912]{1,0:T(8,128)(2,1)S(1)}, bf16[8,6912]{1,0:T(8,128)(2,1)S(1)}, u32[]{:S(2)}, u32[]{:S(2)}) collective-permute-start(bf16[8,6912]{1,0:T(8,128)(2,1)S(1)} %sums.2.refs_4_.refs_0_), channel_id=1, source_target_pairs={{0,2},{1,3},{2,0},{3,1},{4,6},{5,7},{6,4},{7,5},{8,10},{9,11},{10,... | collective-permute-start | bytes 331784 | tf_op jit(solution)/shard_map/ppermute | solution.py:52
  268.5 28.1 %collective-permute-start.63 = (bf16[288,1152]{1,0:T(8,128)(2,1)S(1)}, bf16[288,1152]{1,0:T(8,128)(2,1)S(1)}, u32[]{:S(2)}, u32[]{:S(2)}) collective-permute-start(bf16[288,1152]{1,0:T(8,128)(2,1)S(1)} %fc2_cube.6.refs_2_.refs_0_), channel_id=1, source_target_pairs={{0,2},{1,3},{2,0},{3,1},{4,6},{5,7},{6,4},{7,5},{8,10},{9,11},{10,... | collective-permute-start | bytes 1990664 | tf_op jit(solution)/shard_map/ppermute | solution.py:52
  268.6 17.7 %collective-permute-start.58 = (bf16[8,6912]{1,0:T(8,128)(2,1)S(1)}, bf16[8,6912]{1,0:T(8,128)(2,1)S(1)}, u32[]{:S(2)}, u32[]{:S(2)}) collective-permute-start(bf16[8,6912]{1,0:T(8,128)(2,1)S(1)} %sums.3.refs_1_.refs_0_), channel_id=1, source_target_pairs={{0,4},{1,5},{2,6},{3,7},{4,0},{5,1},{6,2},{7,3},{8,12},{9,13},{10,... | collective-permute-start | bytes 331784 | tf_op jit(solution)/shard_map/ppermute | solution.py:52
  269.3 23.9 %collective-permute-start.57 = (bf16[144,1152]{1,0:T(8,128)(2,1)S(1)}, bf16[144,1152]{1,0:T(8,128)(2,1)S(1)}, u32[]{:S(2)}, u32[]{:S(2)}) collective-permute-start(bf16[144,1152]{1,0:T(8,128)(2,1)S(1)} %get-tuple-element.182), channel_id=1, source_target_pairs={{0,4},{1,5},{2,6},{3,7},{4,0},{5,1},{6,2},{7,3},{8,12},{9,13},{10,... | collective-permute-start | bytes 995336 | tf_op jit(solution)/shard_map/ppermute | solution.py:52
  272.2 21.1 %collective-permute-start.54 = (bf16[144,1152]{1,0:T(8,128)(2,1)S(1)}, bf16[144,1152]{1,0:T(8,128)(2,1)S(1)}, u32[]{:S(2)}, u32[]{:S(2)}) collective-permute-start(bf16[144,1152]{1,0:T(8,128)(2,1)S(1)} %get-tuple-element.179), channel_id=1, source_target_pairs={{0,8},{8,0},{16,24},{24,16},{1,9},{9,1},{17,25},{25,17},{2,10},{10... | collective-permute-start | bytes 995336 | tf_op jit(solution)/shard_map/ppermute | solution.py:52
  273.1 20.1 %collective-permute-start.55 = (bf16[144,1152]{1,0:T(8,128)(2,1)S(1)}, bf16[144,1152]{1,0:T(8,128)(2,1)S(1)}, u32[]{:S(2)}, u32[]{:S(2)}) collective-permute-start(bf16[144,1152]{1,0:T(8,128)(2,1)S(1)} %get-tuple-element.180), channel_id=1, source_target_pairs={{0,16},{8,24},{16,0},{24,8},{1,17},{9,25},{17,1},{25,9},{2,18},{10... | collective-permute-start | bytes 995336 | tf_op jit(solution)/shard_map/ppermute | solution.py:52
  286.3 10.2 %collective-permute-start.56 = (bf16[144,1152]{1,0:T(8,128)(2,1)S(1)}, bf16[144,1152]{1,0:T(8,128)(2,1)S(1)}, u32[]{:S(2)}, u32[]{:S(2)}) collective-permute-start(bf16[144,1152]{1,0:T(8,128)(2,1)S(1)} %get-tuple-element.181), channel_id=1, source_target_pairs={{0,24},{8,16},{16,8},{24,0},{1,25},{9,17},{17,9},{25,1},{2,26},{10... | collective-permute-start | bytes 995336 | tf_op jit(solution)/shard_map/ppermute | solution.py:52
  296.8 37.1 %collective-permute-start.69 = (bf16[576,1152]{1,0:T(8,128)(2,1)S(1)}, bf16[576,1152]{1,0:T(8,128)(2,1)S(1)}, u32[]{:S(2)}, u32[]{:S(2)}) collective-permute-start(bf16[576,1152]{1,0:T(8,128)(2,1)S(1)} %fc2_cube.7.refs_6_.refs_0_), channel_id=1, source_target_pairs={{0,1},{1,0},{2,3},{3,2},{4,5},{5,4},{6,7},{7,6},{8,9},{9,8},{10,11... | collective-permute-start | bytes 3981320 | tf_op jit(solution)/shard_map/ppermute | solution.py:52
  296.9 33.8 %collective-permute-start.70 = (bf16[288,864]{1,0:T(8,128)(2,1)S(1)}, bf16[288,864]{1,0:T(8,128)(2,1)S(1)}, u32[]{:S(2)}, u32[]{:S(2)}) collective-permute-start(bf16[288,864]{1,0:T(8,128)(2,1)S(1)} %qkv_sum.2.refs_2_.refs_0_), channel_id=1, source_target_pairs={{0,4},{1,5},{2,6},{3,7},{4,0},{5,1},{6,2},{7,3},{8,12},{9,13},{10,... | collective-permute-start | bytes 1493000 | tf_op jit(solution)/shard_map/ppermute | solution.py:52
  300.4 8.5 %collective-permute-start.62 = (bf16[16,6912]{1,0:T(8,128)(2,1)S(1)}, bf16[16,6912]{1,0:T(8,128)(2,1)S(1)}, u32[]{:S(2)}, u32[]{:S(2)}) collective-permute-start(bf16[16,6912]{1,0:T(8,128)(2,1)S(1)} %both.1.refs_2_.refs_0_), channel_id=1, source_target_pairs={{0,24},{8,16},{16,8},{24,0},{1,25},{9,17},{17,9},{25,1},{2,26},{10... | collective-permute-start | bytes 663560 | tf_op jit(solution)/shard_map/ppermute | solution.py:52
  302.0 18.9 %collective-permute-start.59 = (bf16[144,1152]{1,0:T(8,128)(2,1)S(1)}, bf16[144,1152]{1,0:T(8,128)(2,1)S(1)}, u32[]{:S(2)}, u32[]{:S(2)}) collective-permute-start(bf16[144,1152]{1,0:T(8,128)(2,1)S(1)} %proj_sum.1.refs_2_.refs_0_), channel_id=1, source_target_pairs={{0,2},{1,3},{6,4},{7,5},{8,10},{9,11},{14,12},{15,13},{16,18},{17,... | collective-permute-start | bytes 995336 | tf_op jit(solution)/shard_map/ppermute | solution.py:91
  303.3 10.2 %collective-permute-start.61 = (bf16[16,6912]{1,0:T(8,128)(2,1)S(1)}, bf16[16,6912]{1,0:T(8,128)(2,1)S(1)}, u32[]{:S(2)}, u32[]{:S(2)}) collective-permute-start(bf16[16,6912]{1,0:T(8,128)(2,1)S(1)} %both.1.refs_2_.refs_0_), channel_id=1, source_target_pairs={{0,16},{8,24},{16,0},{24,8},{1,17},{9,25},{17,1},{25,9},{2,18},{10... | collective-permute-start | bytes 663560 | tf_op jit(solution)/shard_map/ppermute | solution.py:52
  313.5 28.3 %collective-permute-start.65 = (bf16[144,1152]{1,0:T(8,128)(2,1)S(1)}, bf16[144,1152]{1,0:T(8,128)(2,1)S(1)}, u32[]{:S(2)}, u32[]{:S(2)}) collective-permute-start(bf16[144,1152]{1,0:T(8,128)(2,1)S(1)} %fc1_cube.5.refs_4_.refs_0_), channel_id=1, source_target_pairs={{0,4},{1,5},{2,6},{3,7},{4,0},{5,1},{6,2},{7,3},{8,12},{9,13},{10,... | collective-permute-start | bytes 995336 | tf_op jit(solution)/shard_map/ppermute | solution.py:52
  331.5 17.4 %collective-permute-start.73 = (bf16[288,864]{1,0:T(8,128)(2,1)S(1)}, bf16[288,864]{1,0:T(8,128)(2,1)S(1)}, u32[]{:S(2)}, u32[]{:S(2)}) collective-permute-start(bf16[288,864]{1,0:T(8,128)(2,1)S(1)} %qkv_sum.3.refs_2_.refs_0_), channel_id=1, source_target_pairs={{0,2},{1,3},{2,0},{3,1},{4,6},{5,7},{6,4},{7,5},{8,10},{9,11},{10,... | collective-permute-start | bytes 1493000 | tf_op jit(solution)/shard_map/ppermute | solution.py:52
  342.7 20.4 %collective-permute-start.76 = (bf16[288,1152]{1,0:T(8,128)(2,1)S(1)}, bf16[288,1152]{1,0:T(8,128)(2,1)S(1)}, u32[]{:S(2)}, u32[]{:S(2)}) collective-permute-start(bf16[288,1152]{1,0:T(8,128)(2,1)S(1)} %fc1_cube.6.refs_2_.refs_0_), channel_id=1, source_target_pairs={{0,2},{1,3},{2,0},{3,1},{4,6},{5,7},{6,4},{7,5},{8,10},{9,11},{10,... | collective-permute-start | bytes 1990664 | tf_op jit(solution)/shard_map/ppermute | solution.py:52
  344.7 29.4 %collective-permute-start.72 = (bf16[288,864]{1,0:T(8,128)(2,1)S(1)}, bf16[288,864]{1,0:T(8,128)(2,1)S(1)}, u32[]{:S(2)}, u32[]{:S(2)}) collective-permute-start(bf16[288,864]{1,0:T(8,128)(2,1)S(1)} %qkv_sum.3.refs_2_.refs_0_), channel_id=1, source_target_pairs={{0,1},{1,0},{2,3},{3,2},{4,5},{5,4},{6,7},{7,6},{8,9},{9,8},{10,11... | collective-permute-start | bytes 1493000 | tf_op jit(solution)/shard_map/ppermute | solution.py:52
  349.0 26.3 %collective-permute-start.74 = (bf16[288,864]{1,0:T(8,128)(2,1)S(1)}, bf16[288,864]{1,0:T(8,128)(2,1)S(1)}, u32[]{:S(2)}, u32[]{:S(2)}) collective-permute-start(bf16[288,864]{1,0:T(8,128)(2,1)S(1)} %collective-permute-done.73.refs_2_), channel_id=1, source_target_pairs={{0,1},{1,0},{2,3},{3,2},{4,5},{5,4},{6,7},{7,6},{8,9},{9,8},{10,11... | collective-permute-start | bytes 1493000 | tf_op jit(solution)/shard_map/ppermute | solution.py:52
  349.6 23.1 %collective-permute-start.75 = (bf16[128,1152]{1,0:T(8,128)(2,1)S(1)}, bf16[128,1152]{1,0:T(8,128)(2,1)S(1)}, u32[]{:S(2)}, u32[]{:S(2)}) collective-permute-start(bf16[128,1152]{1,0:T(8,128)(2,1)S(1)} %get-tuple-element.191), channel_id=1, source_target_pairs={{0,4},{1,5},{2,6},{3,7},{4,0},{5,1},{6,2},{7,3},{8,12},{9,13},{10,... | collective-permute-start | bytes 884744 | tf_op jit(solution)/shard_map/ppermute | solution.py:52
  352.0 28.3 %collective-permute-start.71 = (bf16[144,1152]{1,0:T(8,128)(2,1)S(1)}, bf16[144,1152]{1,0:T(8,128)(2,1)S(1)}, u32[]{:S(2)}, u32[]{:S(2)}) collective-permute-start(bf16[144,1152]{1,0:T(8,128)(2,1)S(1)} %proj_line.4.refs_2_.refs_0_), channel_id=1, source_target_pairs={{2,0},{3,1},{4,6},{5,7},{10,8},{11,9},{12,14},{13,15},{18,16},{19,... | collective-permute-start | bytes 995336 | tf_op jit(solution)/shard_map/ppermute | solution.py:91
  363.4 25.9 %collective-permute-start.78 = (bf16[144,1152]{1,0:T(8,128)(2,1)S(1)}, bf16[144,1152]{1,0:T(8,128)(2,1)S(1)}, u32[]{:S(2)}, u32[]{:S(2)}) collective-permute-start(bf16[144,1152]{1,0:T(8,128)(2,1)S(1)} %get-tuple-element.196), channel_id=1, source_target_pairs={{0,8},{8,0},{16,24},{24,16},{1,9},{9,1},{17,25},{25,17},{2,10},{10... | collective-permute-start | bytes 995336 | tf_op jit(solution)/shard_map/ppermute | solution.py:52
  372.8 17.0 %collective-permute-start.79 = (bf16[144,1152]{1,0:T(8,128)(2,1)S(1)}, bf16[144,1152]{1,0:T(8,128)(2,1)S(1)}, u32[]{:S(2)}, u32[]{:S(2)}) collective-permute-start(bf16[144,1152]{1,0:T(8,128)(2,1)S(1)} %get-tuple-element.197), channel_id=1, source_target_pairs={{0,16},{8,24},{16,0},{24,8},{1,17},{9,25},{17,1},{25,9},{2,18},{10... | collective-permute-start | bytes 995336 | tf_op jit(solution)/shard_map/ppermute | solution.py:52
  374.1 15.7 %collective-permute-start.80 = (bf16[144,1152]{1,0:T(8,128)(2,1)S(1)}, bf16[144,1152]{1,0:T(8,128)(2,1)S(1)}, u32[]{:S(2)}, u32[]{:S(2)}) collective-permute-start(bf16[144,1152]{1,0:T(8,128)(2,1)S(1)} %get-tuple-element.198), channel_id=1, source_target_pairs={{0,24},{8,16},{16,8},{24,0},{1,25},{9,17},{17,9},{25,1},{2,26},{10... | collective-permute-start | bytes 995336 | tf_op jit(solution)/shard_map/ppermute | solution.py:52
  375.3 14.0 %collective-permute-start.43 = (bf16[128,1152]{1,0:T(8,128)(2,1)S(1)}, bf16[128,1152]{1,0:T(8,128)(2,1)S(1)}, u32[]{:S(2)}, u32[]{:S(2)}) collective-permute-start(bf16[128,1152]{1,0:T(8,128)(2,1)S(1)} %get-tuple-element.167), channel_id=1, source_target_pairs={{0,4},{1,5},{2,6},{3,7},{4,0},{5,1},{6,2},{7,3},{8,12},{9,13},{10,... | collective-permute-start | bytes 884744 | tf_op jit(solution)/shard_map/ppermute | solution.py:52
  380.3 13.1 %collective-permute-start.81 = (bf16[144,1152]{1,0:T(8,128)(2,1)S(1)}, bf16[144,1152]{1,0:T(8,128)(2,1)S(1)}, u32[]{:S(2)}, u32[]{:S(2)}) collective-permute-start(bf16[144,1152]{1,0:T(8,128)(2,1)S(1)} %get-tuple-element.192.refs_2_.refs_0_), channel_id=1, source_target_pairs={{0,1},{1,0},{2,3},{3,2},{4,5},{5,4},{6,7},{7,6},{8,9},{9,8},{10,11... | collective-permute-start | bytes 995336 | tf_op jit(solution)/shard_map/ppermute | solution.py:52
  (72 other events, 669.8 us)

commit v4 on v3

--- a/solution.py
+++ b/solution.py
@@ -1510,9 +1510,9 @@
         step_fc2_other, step_fc1_other, step_fc2_own, step_attend_back, step_attn_sum, step_fc1_own,
         step_qkv_wgrad, step_fc2_a, step_proj_wgrad, step_outs, step_finish, step_gather_sums, step_fc2_b,
         step_sums_c, step_qkv_sum, step_fc1_a, step_fc2_j, step_sums_g, step_proj_other, step_proj_blocks,
-        step_sums_h, step_fc1_b, step_proj_sum, step_fc2_c, step_ada, step_proj_a, step_biases, step_qkv_sum2,
-        step_place_fc2, step_cond, step_fc1_j, step_proj_b, step_fc1_c, step_latent_grad, step_place_qkv,
-        step_proj_c, step_block_out, step_place_proj, step_place_fc1,
+        step_sums_h, step_fc1_b, step_proj_sum, step_fc2_c, step_ada, step_proj_a, step_qkv_sum2, step_place_fc2,
+        step_cond, step_fc1_j, step_proj_b, step_biases, step_place_qkv, step_fc1_c, step_block_out, step_proj_c,
+        step_latent_grad, step_place_proj, step_place_fc1,
     ):
         step()
 

time: 401 us -> 398 us (level)
  waiting for transfers between devices: 189 us -> 184 us
    ppermute x82, waiting for transfers between devices: 189 us -> 184 us  [swap(): return lax.ppermute(x, axis, [(i, i ^ mask) for i in range(count)])]
  transfers between devices with their start and end apart: 85 -> 85, of which waited for: 36 -> 35; matrix products, arithmetic and copies ran while one was open for 1% -> 1% of each run, Pallas kernels for 19% -> 19%
where the time goes in v4:
time: 398 us; the launch traced here: 394 us
  waiting for transfers between devices  184 us (46%)
  Pallas kernels  101 us (25%)
  starting transfers between devices  82.7 us (21%)
  local copies, waits for them, and re-layouts  21.5 us (5%)
    ppermute x82, waiting for transfers between devices, swap(): return lax.ppermute(x, axis, [(i, i ^ mask) for i in range(count)])  184 us
    pallas_call x55, Pallas kernels, launch(): pl.pallas_call(body, **{} if grid is None else {'grid': grid}, in_specs=l...  101 us
    ppermute x82, starting transfers between devices, swap(): return lax.ppermute(x, axis, [(i, i ^ mask) for i in range(count)])  79.4 us
    unnamed x102, local copies, waits for them, and re-layouts  21.4 us
  transfers between devices with their start and end apart: 85, of which 35 were waited for; matrix products, arithmetic and copies ran while one was open for 1% of the time, Pallas kernels for 19%

profile of v4, /device:TPU:0, one launch (start us, length us, event | category | flops | bytes accessed | tf_op | source)
XLA Modules:
  0.0 394.4 jit_solution(17868572284957102189)
XLA Ops:
  0.7 1.7 copy-done.8
  4.6 4.1 %collective-permute-start = (bf16[128,1152]{1,0:T(8,128)(2,1)S(1)}, bf16[128,1152]{1,0:T(8,128)(2,1)S(1)}, u32[]{:S(2)}, u32[]{:S(2)}) collective-permute-start(bf16[128,1152]{1,0:T(8,128)(2,1)S(1)} %get-tuple-element.109), channel_id=1, source_target_pairs={{0,4},{1,5},{2,6},{3,7},{4,0},{5,1},{6,2},{7,3},{8,12},{9,13},{10,... | collective-permute-start | bytes 884744 | tf_op jit(solution)/shard_map/ppermute | solution.py:52
  9.6 2.5 collective-permute-start.3
  13.4 1.6 collective-permute-start.11
  18.5 1.6 collective-permute-start.5
  20.1 9.7 %collective-permute-done.4.refs_1_ = f32[4,6912]{1,0:T(4,128)S(1)} collective-permute-done((f32[4,6912]{1,0:T(4,128)S(1)}, f32[4,6912]{1,0:T(4,128)S(1)}, u32[]{:S(2)}, u32[]{:S(2)}) %collective-permute-start.4) | collective-permute-done | bytes 110624 | tf_op jit(solution)/shard_map/ppermute | solution.py:52
  29.8 1.7 collective-permute-start.6
  31.5 4.0 %collective-permute-done.6.refs_3_ = f32[4,6912]{1,0:T(4,128)S(1)} collective-permute-done((f32[4,6912]{1,0:T(4,128)S(1)}, f32[4,6912]{1,0:T(4,128)S(1)}, u32[]{:S(2)}, u32[]{:S(2)}) %collective-permute-start.6) | collective-permute-done | bytes 110624 | tf_op jit(solution)/shard_map/ppermute | solution.py:52
  37.0 1.7 collective-permute-start.7
  42.2 3.6 collective-permute-done.13.refs_8_
  45.8 1.8 collective-permute-start.18
  47.6 2.0 collective-permute-start.19
  49.7 1.8 collective-permute-done.9.refs_3_
  51.6 16.4 %attend.1 = (bf16[1024,864]{1,0:T(8,128)(2,1)S(1)}, bf16[1152,864]{1,0:T(8,128)(2,1)S(1)}, bf16[256,288]{1,0:T(8,128)(2,1)S(1)}, bf16[256,288]{1,0:T(8,128)(2,1)...) custom-call(bf16[256,1152]{1,0:T(8,128)(2,1)S(1)} %get-tuple-element, ...), custom_call_target="tpu_custom_call" | custom-call | flops 1000 | bytes 1000 | tf_op jit(solution)/shard_map/attend/pallas_call | solution.py:243
  72.9 1.9 collective-permute-done.18.refs_2_
  78.2 2.0 collective-permute-done.14.refs_1_
  81.2 2.1 collective-permute-done.15.refs_2_
  83.3 2.5 collective-permute-done.16.refs_3_
  85.8 2.6 mix.1
  97.0 11.2 %collective-permute-done.23.refs_2_ = bf16[256,1152]{1,0:T(8,128)(2,1)S(1)} collective-permute-done((bf16[256,1152]{1,0:T(8,128)(2,1)S(1)}, bf16[256,1152]{1,0:T(8,128)(2,1)S(1)}, u32[]{:S(2)}, u32[]{:S(2)}) %collective-permute-start.23) | collective-permute-done | bytes 589856 | tf_op jit(solution)/shard_map/ppermute | solution.py:52
  110.6 5.2 %collective-permute-done.29.refs_9_.refs_5_ = bf16[128,1152]{1,0:T(8,128)(2,1)S(1)} collective-permute-done((bf16[128,1152]{1,0:T(8,128)(2,1)S(1)}, bf16[128,1152]{1,0:T(8,128)(2,1)S(1)}, u32[]{:S(2)}, u32[]{:S(2)}) %collective-permute-start.29) | collective-permute-done | bytes 294944 | tf_op jit(solution)/shard_map/ppermute | solution.py:52
  115.8 6.1 %collective-permute-done.25.refs_4_ = bf16[128,1152]{1,0:T(8,128)(2,1)S(1)} collective-permute-done((bf16[128,1152]{1,0:T(8,128)(2,1)S(1)}, bf16[128,1152]{1,0:T(8,128)(2,1)S(1)}, u32[]{:S(2)}, u32[]{:S(2)}) %collective-permute-start.25) | collective-permute-done | bytes 294944 | tf_op jit(solution)/shard_map/ppermute | solution.py:52
  121.9 17.6 %mlp.1 = (bf16[1024,1152]{1,0:T(8,128)(2,1)S(1)}, bf16[1024,1152]{1,0:T(8,128)(2,1)S(1)}, f32[8,1152]{1,0:T(8,128)S(1)}, bf16[256,1152]{1,0:T(8,128)(2,1)S(1)}, ...) custom-call(bf16[256,1152]{1,0:T(8,128)(2,1)S(1)} %get-tuple-element, ...), custom_call_target="tpu_custom_call" | custom-call | flops 1000 | bytes 1000 | tf_op jit(solution)/shard_map/mlp/pallas_call | solution.py:243
  141.4 1.7 collective-permute-start.35
  143.1 4.2 %fc2_wgrad.1.refs_6_.refs_0_ = bf16[1152,1152]{1,0:T(8,128)(2,1)S(1)} custom-call(bf16[1024,1152]{1,0:T(8,128)(2,1)S(1)} %get-tuple-element.150.refs_0_, bf16[256,1152]{1,0:T(8,128)(2,1)S(1)} %get-tuple-element.135.refs_5_.refs_1_, bf16[256,1152]{1,0:T(8,128)(2,1)S(1)} %collective-permute-done.26.refs_6_.refs_2_, ...), custom_call_target="tpu_custom_call" | custom-call | flops 1000 | bytes 1000 | tf_op jit(solution)/shard_map/fc2_wgrad/pallas_call | solution.py:243
  147.4 4.0 %fc1_wgrad.1.refs_11_.refs_0_ = bf16[1152,1152]{1,0:T(8,128)(2,1)S(1)} custom-call(bf16[256,1152]{1,0:T(8,128)(2,1)S(1)} %copy-done.18, bf16[256,1152]{1,0:T(8,128)(2,1)S(1)} %collective-permute-done.22.refs_1_, bf16[256,1152]{1,0:T(8,128)(2,1)S(1)} %collective-permute-done.23.refs_2_, bf16[128,1152]{1,0:T(8,128)(2,1)S(1)} %collective-permute-done.24.refs_3_, ...), custom_call_target="tpu_custom_call" | custom-call | flops 1000 | bytes 1000 | tf_op jit(solution)/shard_map/fc1_wgrad/pallas_call | solution.py:243
  151.4 4.4 %collective-permute-done.33.refs_1_ = bf16[256,1152]{1,0:T(8,128)(2,1)S(1)} collective-permute-done((bf16[256,1152]{1,0:T(8,128)(2,1)S(1)}, bf16[256,1152]{1,0:T(8,128)(2,1)S(1)}, u32[]{:S(2)}, u32[]{:S(2)}) %collective-permute-start.33) | collective-permute-done | bytes 589856 | tf_op jit(solution)/shard_map/ppermute | solution.py:52
  155.8 12.2 %collective-permute-done.34.refs_2_ = bf16[256,1152]{1,0:T(8,128)(2,1)S(1)} collective-permute-done((bf16[256,1152]{1,0:T(8,128)(2,1)S(1)}, bf16[256,1152]{1,0:T(8,128)(2,1)S(1)}, u32[]{:S(2)}, u32[]{:S(2)}) %collective-permute-start.34) | collective-permute-done | bytes 589856 | tf_op jit(solution)/shard_map/ppermute | solution.py:52
  168.1 4.1 %turn.1 = (f32[256,1152]{1,0:T(8,128)S(1)}, bf16[256,1152]{1,0:T(8,128)(2,1)S(1)}, f32[16,4608]{1,0:T(8,128)S(1)}, bf16[256,288]{1,0:T(8,128)(2,1)S(1)}, bf16[25...) custom-call(bf16[256,1152]{1,0:T(8,128)(2,1)S(1)} %get-tuple-element.143.refs_0_, ...), custom_call_target="tpu_custom_call" | custom-call | flops 1000 | bytes 1000 | tf_op jit(solution)/shard_map/turn/pallas_call | solution.py:243
  172.9 1.7 collective-permute-start.40
  176.3 3.8 collective-permute-done.38.refs_2_
  180.1 3.3 collective-permute-done.40.refs_4_
  183.5 15.2 %attend_back.1.refs_2_.refs_4_ = bf16[1024,864]{1,0:T(8,128)(2,1)S(1)} custom-call(bf16[1024,864]{1,0:T(8,128)(2,1)S(1)} %copy-done.28, bf16[256,288]{1,0:T(8,128)(2,1)S(1)} %get-tuple-element.157.refs_1_, bf16[256,288]{1,0:T(8,128)(2,1)S(1)} %collective-permute-done.38.refs_2_, bf16[256,288]{1,0:T(8,128)(2,1)S(1)} %collective-permute-done.39.refs_3_, ...), custom_call_target="tpu_custom_call" | custom-call | flops 1000 | bytes 1000 | tf_op jit(solution)/shard_map/attend_back/pallas_call | solution.py:243
  198.7 1.6 convolution_convert_fusion
  204.4 1.6 collective-permute-start.32
  206.2 1.8 collective-permute-start.48
  208.9 3.3 qkv_wgrad.1
  212.2 8.2 %collective-permute-done.37.refs_1_ = bf16[288,1152]{1,0:T(8,128)(2,1)S(1)} collective-permute-done((bf16[288,1152]{1,0:T(8,128)(2,1)S(1)}, bf16[288,1152]{1,0:T(8,128)(2,1)S(1)}, u32[]{:S(2)}, u32[]{:S(2)}) %collective-permute-start.37) | collective-permute-done | bytes 663584 | tf_op jit(solution)/shard_map/ppermute | solution.py:52
  221.3 8.0 %collective-permute-done.31.refs_2_ = bf16[256,1152]{1,0:T(8,128)(2,1)S(1)} collective-permute-done((bf16[256,1152]{1,0:T(8,128)(2,1)S(1)}, bf16[256,1152]{1,0:T(8,128)(2,1)S(1)}, u32[]{:S(2)}, u32[]{:S(2)}) %collective-permute-start.31) | collective-permute-done | bytes 589856 | tf_op jit(solution)/shard_map/ppermute | solution.py:52
  233.0 7.1 %collective-permute-done.48.refs_2_ = bf16[256,1152]{1,0:T(8,128)(2,1)S(1)} collective-permute-done((bf16[256,1152]{1,0:T(8,128)(2,1)S(1)}, bf16[256,1152]{1,0:T(8,128)(2,1)S(1)}, u32[]{:S(2)}, u32[]{:S(2)}) %collective-permute-start.48) | collective-permute-done | bytes 589856 | tf_op jit(solution)/shard_map/ppermute | solution.py:52
  240.1 2.2 finish.1
  245.9 21.7 %collective-permute-done.46.refs_2_ = bf16[288,864]{1,0:T(8,128)(2,1)S(1)} collective-permute-done((bf16[288,864]{1,0:T(8,128)(2,1)S(1)}, bf16[288,864]{1,0:T(8,128)(2,1)S(1)}, u32[]{:S(2)}, u32[]{:S(2)}) %collective-permute-start.46) | collective-permute-done | bytes 497696 | tf_op jit(solution)/shard_map/ppermute | solution.py:52
  269.3 2.3 collective-permute-start.51
  274.4 11.9 %collective-permute-done.54.refs_1_ = bf16[8,6912]{1,0:T(8,128)(2,1)S(1)} collective-permute-done((bf16[8,6912]{1,0:T(8,128)(2,1)S(1)}, bf16[8,6912]{1,0:T(8,128)(2,1)S(1)}, u32[]{:S(2)}, u32[]{:S(2)}) %collective-permute-start.54) | collective-permute-done | bytes 110624 | tf_op jit(solution)/shard_map/ppermute | solution.py:52
  286.3 1.6 collective-permute-start.63
  288.0 5.2 %collective-permute-done.51.refs_1_ = bf16[144,1152]{1,0:T(8,128)(2,1)S(1)} collective-permute-done((bf16[144,1152]{1,0:T(8,128)(2,1)S(1)}, bf16[144,1152]{1,0:T(8,128)(2,1)S(1)}, u32[]{:S(2)}, u32[]{:S(2)}) %collective-permute-start.51) | collective-permute-done | bytes 331808 | tf_op jit(solution)/shard_map/ppermute | solution.py:52
  293.2 3.2 collective-permute-done.63.refs_3_
  296.9 3.4 collective-permute-start.68
  300.4 1.6 collective-permute-start.59
  304.1 4.7 %collective-permute-done.59.refs_3_ = bf16[16,6912]{1,0:T(8,128)(2,1)S(1)} collective-permute-done((bf16[16,6912]{1,0:T(8,128)(2,1)S(1)}, bf16[16,6912]{1,0:T(8,128)(2,1)S(1)}, u32[]{:S(2)}, u32[]{:S(2)}) %collective-permute-start.59) | collective-permute-done | bytes 221216 | tf_op jit(solution)/shard_map/ppermute | solution.py:52
  309.8 3.7 collective-permute-done.58.refs_2_
  313.5 2.0 collective-permute-done.57.refs_1_
  315.5 5.4 %ada.1 = (f32[288,6912]{1,0:T(8,128)}, f32[8,6912]{1,0:T(8,128)S(1)}, f32[8,288]{1,0:T(8,128)S(1)}, f32[8,288]{1,0:T(8,128)S(1)}, f32[8,288]{1,0:T(8,128)S(1)}, /*index=5*/f32[8,288]{1,0:T(8,128)S(1)}) custom-call(bf16[16,6912]{1,0:T(8,128)(2,1)S(1)} %both.1.refs_2_.refs_0_, bf16[16,6912]{1,0:T(8,128)(2,1)S(1)} %collective-permute-done.57.refs_1_, ...), custom_call_target="tpu_custom_call" | custom-call | flops 1000 | bytes 1000 | tf_op jit(solution)/shard_map/ada/pallas_call | solution.py:243
  320.9 2.7 collective-permute-done.68.refs_1_
  328.1 3.1 place_fc2.1.refs_5_
  331.5 2.5 copy-done
  334.7 7.7 %collective-permute-done.56.refs_1_ = bf16[144,1152]{1,0:T(8,128)(2,1)S(1)} collective-permute-done((bf16[144,1152]{1,0:T(8,128)(2,1)S(1)}, bf16[144,1152]{1,0:T(8,128)(2,1)S(1)}, u32[]{:S(2)}, u32[]{:S(2)}) %collective-permute-start.56) | collective-permute-done | bytes 331808 | tf_op jit(solution)/shard_map/ppermute | solution.py:52
  343.3 1.8 collective-permute-start.70
  346.3 3.0 collective-permute-start.43
  352.1 2.7 place_qkv.1.refs_2_
  354.8 11.8 %collective-permute-done.70.refs_1_ = bf16[288,1152]{1,0:T(8,128)(2,1)S(1)} collective-permute-done((bf16[288,1152]{1,0:T(8,128)(2,1)S(1)}, bf16[288,1152]{1,0:T(8,128)(2,1)S(1)}, u32[]{:S(2)}, u32[]{:S(2)}) %collective-permute-start.70) | collective-permute-done | bytes 663584 | tf_op jit(solution)/shard_map/ppermute | solution.py:52
  366.6 2.1 copy-done.2
  374.6 10.7 %collective-permute-done.75.refs_1_ = bf16[128,1152]{1,0:T(8,128)(2,1)S(1)} collective-permute-done((bf16[128,1152]{1,0:T(8,128)(2,1)S(1)}, bf16[128,1152]{1,0:T(8,128)(2,1)S(1)}, u32[]{:S(2)}, u32[]{:S(2)}) %collective-permute-start.75) | collective-permute-done | bytes 294944 | tf_op jit(solution)/shard_map/ppermute | solution.py:52
  391.3 2.9 place_fc1.1
  (271 shorter events, 80.8 us)
Async XLA Ops:
  4.6 31.0 %collective-permute-start = (bf16[128,1152]{1,0:T(8,128)(2,1)S(1)}, bf16[128,1152]{1,0:T(8,128)(2,1)S(1)}, u32[]{:S(2)}, u32[]{:S(2)}) collective-permute-start(bf16[128,1152]{1,0:T(8,128)(2,1)S(1)} %get-tuple-element.109), channel_id=1, source_target_pairs={{0,4},{1,5},{2,6},{3,7},{4,0},{5,1},{6,2},{7,3},{8,12},{9,13},{10,... | collective-permute-start | bytes 884744 | tf_op jit(solution)/shard_map/ppermute | solution.py:52
  13.4 25.4 %collective-permute-start.11 = (bf16[288,864]{1,0:T(8,128)(2,1)S(1)}, bf16[288,864]{1,0:T(8,128)(2,1)S(1)}, u32[]{:S(2)}, u32[]{:S(2)}) collective-permute-start(bf16[288,864]{1,0:T(8,128)(2,1)S(1)} %qkv_cols.1.refs_6_.refs_4_), channel_id=1, source_target_pairs={{0,16},{8,24},{16,0},{24,8},{1,17},{9,25},{17,1},{25,9},{2,18},{10... | collective-permute-start | bytes 1493000 | tf_op jit(solution)/shard_map/ppermute | solution.py:52
  14.9 25.0 %collective-permute-start.10 = (bf16[288,864]{1,0:T(8,128)(2,1)S(1)}, bf16[288,864]{1,0:T(8,128)(2,1)S(1)}, u32[]{:S(2)}, u32[]{:S(2)}) collective-permute-start(bf16[288,864]{1,0:T(8,128)(2,1)S(1)} %qkv_cols.1.refs_6_.refs_4_), channel_id=1, source_target_pairs={{0,8},{8,0},{16,24},{24,16},{1,9},{9,1},{17,25},{25,17},{2,10},{10... | collective-permute-start | bytes 1493000 | tf_op jit(solution)/shard_map/ppermute | solution.py:52
  18.2 11.6 %collective-permute-start.4 = (f32[4,6912]{1,0:T(4,128)S(1)}, f32[4,6912]{1,0:T(4,128)S(1)}, u32[]{:S(2)}, u32[]{:S(2)}) collective-permute-start(f32[4,6912]{1,0:T(4,128)S(1)} %get-tuple-element.114), channel_id=1, source_target_pairs={{0,8},{8,0},{16,24},{24,16},{1,9},{9,1},{17,25},{25,17},{2,10},{10... | collective-permute-start | bytes 331784 | tf_op jit(solution)/shard_map/ppermute | solution.py:52
  18.5 13.0 %collective-permute-start.5 = (f32[4,6912]{1,0:T(4,128)S(1)}, f32[4,6912]{1,0:T(4,128)S(1)}, u32[]{:S(2)}, u32[]{:S(2)}) collective-permute-start(f32[4,6912]{1,0:T(4,128)S(1)} %get-tuple-element.115), channel_id=1, source_target_pairs={{0,16},{8,24},{16,0},{24,8},{1,17},{9,25},{17,1},{25,9},{2,18},{10... | collective-permute-start | bytes 331784 | tf_op jit(solution)/shard_map/ppermute | solution.py:52
  37.0 12.6 %collective-permute-start.7 = (bf16[256,1152]{1,0:T(8,128)(2,1)S(1)}, bf16[256,1152]{1,0:T(8,128)(2,1)S(1)}, u32[]{:S(2)}, u32[]{:S(2)}) collective-permute-start(bf16[256,1152]{1,0:T(8,128)(2,1)S(1)} %get-tuple-element.118.refs_1_.refs_0_), channel_id=1, source_target_pairs={{0,2},{1,3},{2,0},{3,1},{4,6},{5,7},{6,4},{7,5},{8,10},{9,11},{10,... | collective-permute-start | bytes 1769480 | tf_op jit(solution)/shard_map/ppermute | solution.py:52
  38.7 7.1 %collective-permute-start.13 = (bf16[144,864]{1,0:T(8,128)(2,1)S(1)}, bf16[144,864]{1,0:T(8,128)(2,1)S(1)}, u32[]{:S(2)}, u32[]{:S(2)}) collective-permute-start(bf16[144,864]{1,0:T(8,128)(2,1)S(1)} %slice.33), channel_id=1, source_target_pairs={{0,8},{8,0},{16,24},{24,16},{1,9},{9,1},{17,25},{25,17},{2,10},{10... | collective-permute-start | bytes 746504 | tf_op jit(solution)/shard_map/ppermute | solution.py:52
  39.9 7.7 %collective-permute-start.12 = (bf16[144,864]{1,0:T(8,128)(2,1)S(1)}, bf16[144,864]{1,0:T(8,128)(2,1)S(1)}, u32[]{:S(2)}, u32[]{:S(2)}) collective-permute-start(bf16[144,864]{1,0:T(8,128)(2,1)S(1)} %slice.32), channel_id=1, source_target_pairs={{0,16},{8,24},{16,0},{24,8},{1,17},{9,25},{17,1},{25,9},{2,18},{10... | collective-permute-start | bytes 746504 | tf_op jit(solution)/shard_map/ppermute | solution.py:52
  41.3 8.4 %collective-permute-start.8 = (bf16[256,1152]{1,0:T(8,128)(2,1)S(1)}, bf16[256,1152]{1,0:T(8,128)(2,1)S(1)}, u32[]{:S(2)}, u32[]{:S(2)}) collective-permute-start(bf16[256,1152]{1,0:T(8,128)(2,1)S(1)} %get-tuple-element.118.refs_1_.refs_0_), channel_id=1, source_target_pairs={{0,1},{1,0},{2,3},{3,2},{4,5},{5,4},{6,7},{7,6},{8,9},{9,8},{10,11... | collective-permute-start | bytes 1769480 | tf_op jit(solution)/shard_map/ppermute | solution.py:52
  41.3 31.6 %collective-permute-start.17 = (bf16[288,1152]{1,0:T(8,128)(2,1)S(1)}, bf16[288,1152]{1,0:T(8,128)(2,1)S(1)}, u32[]{:S(2)}, u32[]{:S(2)}) collective-permute-start(bf16[288,1152]{1,0:T(8,128)(2,1)S(1)} %get-tuple-element.125), channel_id=1, source_target_pairs={{0,8},{8,0},{16,24},{24,16},{1,9},{9,1},{17,25},{25,17},{2,10},{10... | collective-permute-start | bytes 1990664 | tf_op jit(solution)/shard_map/ppermute | solution.py:52
  45.8 28.9 %collective-permute-start.18 = (bf16[288,1152]{1,0:T(8,128)(2,1)S(1)}, bf16[288,1152]{1,0:T(8,128)(2,1)S(1)}, u32[]{:S(2)}, u32[]{:S(2)}) collective-permute-start(bf16[288,1152]{1,0:T(8,128)(2,1)S(1)} %get-tuple-element.126), channel_id=1, source_target_pairs={{0,16},{8,24},{16,0},{24,8},{1,17},{9,25},{17,1},{25,9},{2,18},{10... | collective-permute-start | bytes 1990664 | tf_op jit(solution)/shard_map/ppermute | solution.py:52
  47.6 27.2 %collective-permute-start.19 = (bf16[288,1152]{1,0:T(8,128)(2,1)S(1)}, bf16[288,1152]{1,0:T(8,128)(2,1)S(1)}, u32[]{:S(2)}, u32[]{:S(2)}) collective-permute-start(bf16[288,1152]{1,0:T(8,128)(2,1)S(1)} %get-tuple-element.127), channel_id=1, source_target_pairs={{0,24},{8,16},{16,8},{24,0},{1,25},{9,17},{17,9},{25,1},{2,26},{10... | collective-permute-start | bytes 1990664 | tf_op jit(solution)/shard_map/ppermute | solution.py:52
  49.7 22.0 %collective-permute-start.20 = (bf16[128,1152]{1,0:T(8,128)(2,1)S(1)}, bf16[128,1152]{1,0:T(8,128)(2,1)S(1)}, u32[]{:S(2)}, u32[]{:S(2)}) collective-permute-start(bf16[128,1152]{1,0:T(8,128)(2,1)S(1)} %get-tuple-element.128), channel_id=1, source_target_pairs={{0,4},{1,5},{2,6},{3,7},{4,0},{5,1},{6,2},{7,3},{8,12},{9,13},{10,... | collective-permute-start | bytes 884744 | tf_op jit(solution)/shard_map/ppermute | solution.py:52
  75.0 10.8 %collective-permute-start.21 = (bf16[4,288,1152]{2,1,0:T(8,128)(2,1)S(1)}, bf16[4,288,1152]{2,1,0:T(8,128)(2,1)S(1)}, u32[]{:S(2)}, u32[]{:S(2)}) collective-permute-start(bf16[4,288,1152]{2,1,0:T(8,128)(2,1)S(1)} %stack.1.refs_4_.refs_10_), channel_id=1, source_target_pairs={{0,1},{1,0},{2,3},{3,2},{4,5},{5,4},{6,7},{7,6},{8,9},{9,8},{10,11... | collective-permute-start | bytes 7962632 | tf_op jit(solution)/shard_map/ppermute | solution.py:52
  75.5 7.8 %collective-permute-start.15 = (bf16[256,288]{1,0:T(8,128)(2,1)S(1)}, bf16[256,288]{1,0:T(8,128)(2,1)S(1)}, u32[]{:S(2)}, u32[]{:S(2)}) collective-permute-start(bf16[256,288]{1,0:T(8,128)(2,1)S(1)} %get-tuple-element.123), channel_id=1, source_target_pairs={{0,2},{1,3},{2,0},{3,1},{4,6},{5,7},{6,4},{7,5},{8,10},{9,11},{10,... | collective-permute-start | bytes 442376 | tf_op jit(solution)/shard_map/ppermute | solution.py:52
  75.9 9.8 %collective-permute-start.16 = (bf16[256,288]{1,0:T(8,128)(2,1)S(1)}, bf16[256,288]{1,0:T(8,128)(2,1)S(1)}, u32[]{:S(2)}, u32[]{:S(2)}) collective-permute-start(bf16[256,288]{1,0:T(8,128)(2,1)S(1)} %get-tuple-element.124), channel_id=1, source_target_pairs={{0,3},{1,2},{2,1},{3,0},{4,7},{5,6},{6,5},{7,4},{8,11},{9,10},{10,... | collective-permute-start | bytes 442376 | tf_op jit(solution)/shard_map/ppermute | solution.py:52
  77.0 17.2 %collective-permute-start.27 = (bf16[256,1152]{1,0:T(8,128)(2,1)S(1)}, bf16[256,1152]{1,0:T(8,128)(2,1)S(1)}, u32[]{:S(2)}, u32[]{:S(2)}) collective-permute-start(bf16[256,1152]{1,0:T(8,128)(2,1)S(1)} %get-tuple-element.135.refs_5_.refs_1_), channel_id=1, source_target_pairs={{0,16},{8,24},{16,0},{24,8},{1,17},{9,25},{17,1},{25,9},{2,18},{10... | collective-permute-start | bytes 1769480 | tf_op jit(solution)/shard_map/ppermute | solution.py:52
  80.3 15.4 %collective-permute-start.26 = (bf16[256,1152]{1,0:T(8,128)(2,1)S(1)}, bf16[256,1152]{1,0:T(8,128)(2,1)S(1)}, u32[]{:S(2)}, u32[]{:S(2)}) collective-permute-start(bf16[256,1152]{1,0:T(8,128)(2,1)S(1)} %get-tuple-element.135.refs_5_.refs_1_), channel_id=1, source_target_pairs={{0,8},{8,0},{16,24},{24,16},{1,9},{9,1},{17,25},{25,17},{2,10},{10... | collective-permute-start | bytes 1769480 | tf_op jit(solution)/shard_map/ppermute | solution.py:52
  91.9 16.2 %collective-permute-start.23 = (bf16[256,1152]{1,0:T(8,128)(2,1)S(1)}, bf16[256,1152]{1,0:T(8,128)(2,1)S(1)}, u32[]{:S(2)}, u32[]{:S(2)}) collective-permute-start(bf16[256,1152]{1,0:T(8,128)(2,1)S(1)} %get-tuple-element.134.refs_0_), channel_id=1, source_target_pairs={{0,16},{8,24},{16,0},{24,8},{1,17},{9,25},{17,1},{25,9},{2,18},{10... | collective-permute-start | bytes 1769480 | tf_op jit(solution)/shard_map/ppermute | solution.py:52
  93.3 16.2 %collective-permute-start.22 = (bf16[256,1152]{1,0:T(8,128)(2,1)S(1)}, bf16[256,1152]{1,0:T(8,128)(2,1)S(1)}, u32[]{:S(2)}, u32[]{:S(2)}) collective-permute-start(bf16[256,1152]{1,0:T(8,128)(2,1)S(1)} %get-tuple-element.134.refs_0_), channel_id=1, source_target_pairs={{0,8},{8,0},{16,24},{24,16},{1,9},{9,1},{17,25},{25,17},{2,10},{10... | collective-permute-start | bytes 1769480 | tf_op jit(solution)/shard_map/ppermute | solution.py:52
  94.2 21.6 %collective-permute-start.29 = (bf16[128,1152]{1,0:T(8,128)(2,1)S(1)}, bf16[128,1152]{1,0:T(8,128)(2,1)S(1)}, u32[]{:S(2)}, u32[]{:S(2)}) collective-permute-start(bf16[128,1152]{1,0:T(8,128)(2,1)S(1)} %slice.37), channel_id=1, source_target_pairs={{0,8},{8,0},{16,24},{24,16},{1,9},{9,1},{17,25},{25,17},{2,10},{10... | collective-permute-start | bytes 884744 | tf_op jit(solution)/shard_map/ppermute | solution.py:52
  95.7 20.1 %collective-permute-start.28 = (bf16[128,1152]{1,0:T(8,128)(2,1)S(1)}, bf16[128,1152]{1,0:T(8,128)(2,1)S(1)}, u32[]{:S(2)}, u32[]{:S(2)}) collective-permute-start(bf16[128,1152]{1,0:T(8,128)(2,1)S(1)} %slice.36), channel_id=1, source_target_pairs={{0,16},{8,24},{16,0},{24,8},{1,17},{9,25},{17,1},{25,9},{2,18},{10... | collective-permute-start | bytes 884744 | tf_op jit(solution)/shard_map/ppermute | solution.py:52
  108.2 13.6 %collective-permute-start.25 = (bf16[128,1152]{1,0:T(8,128)(2,1)S(1)}, bf16[128,1152]{1,0:T(8,128)(2,1)S(1)}, u32[]{:S(2)}, u32[]{:S(2)}) collective-permute-start(bf16[128,1152]{1,0:T(8,128)(2,1)S(1)} %slice.35), channel_id=1, source_target_pairs={{0,8},{8,0},{16,24},{24,16},{1,9},{9,1},{17,25},{25,17},{2,10},{10... | collective-permute-start | bytes 884744 | tf_op jit(solution)/shard_map/ppermute | solution.py:52
  109.5 12.4 %collective-permute-start.24 = (bf16[128,1152]{1,0:T(8,128)(2,1)S(1)}, bf16[128,1152]{1,0:T(8,128)(2,1)S(1)}, u32[]{:S(2)}, u32[]{:S(2)}) collective-permute-start(bf16[128,1152]{1,0:T(8,128)(2,1)S(1)} %slice.34), channel_id=1, source_target_pairs={{0,16},{8,24},{16,0},{24,8},{1,17},{9,25},{17,1},{25,9},{2,18},{10... | collective-permute-start | bytes 884744 | tf_op jit(solution)/shard_map/ppermute | solution.py:52
  139.6 16.3 %collective-permute-start.33 = (bf16[256,1152]{1,0:T(8,128)(2,1)S(1)}, bf16[256,1152]{1,0:T(8,128)(2,1)S(1)}, u32[]{:S(2)}, u32[]{:S(2)}) collective-permute-start(bf16[256,1152]{1,0:T(8,128)(2,1)S(1)} %get-tuple-element.144), channel_id=1, source_target_pairs={{0,8},{8,0},{16,24},{24,16},{1,9},{9,1},{17,25},{25,17},{2,10},{10... | collective-permute-start | bytes 1769480 | tf_op jit(solution)/shard_map/ppermute | solution.py:52
  140.6 27.4 %collective-permute-start.34 = (bf16[256,1152]{1,0:T(8,128)(2,1)S(1)}, bf16[256,1152]{1,0:T(8,128)(2,1)S(1)}, u32[]{:S(2)}, u32[]{:S(2)}) collective-permute-start(bf16[256,1152]{1,0:T(8,128)(2,1)S(1)} %get-tuple-element.145), channel_id=1, source_target_pairs={{0,16},{8,24},{16,0},{24,8},{1,17},{9,25},{17,1},{25,9},{2,18},{10... | collective-permute-start | bytes 1769480 | tf_op jit(solution)/shard_map/ppermute | solution.py:52
  141.4 26.7 %collective-permute-start.35 = (bf16[256,1152]{1,0:T(8,128)(2,1)S(1)}, bf16[256,1152]{1,0:T(8,128)(2,1)S(1)}, u32[]{:S(2)}, u32[]{:S(2)}) collective-permute-start(bf16[256,1152]{1,0:T(8,128)(2,1)S(1)} %get-tuple-element.146), channel_id=1, source_target_pairs={{0,24},{8,16},{16,8},{24,0},{1,25},{9,17},{17,9},{25,1},{2,26},{10... | collective-permute-start | bytes 1769480 | tf_op jit(solution)/shard_map/ppermute | solution.py:52
  172.4 7.8 %collective-permute-start.38 = (bf16[256,288]{1,0:T(8,128)(2,1)S(1)}, bf16[256,288]{1,0:T(8,128)(2,1)S(1)}, u32[]{:S(2)}, u32[]{:S(2)}) collective-permute-start(bf16[256,288]{1,0:T(8,128)(2,1)S(1)} %get-tuple-element.158), channel_id=1, source_target_pairs={{0,2},{1,3},{2,0},{3,1},{4,6},{5,7},{6,4},{7,5},{8,10},{9,11},{10,... | collective-permute-start | bytes 442376 | tf_op jit(solution)/shard_map/ppermute | solution.py:52
  172.7 7.5 %collective-permute-start.39 = (bf16[256,288]{1,0:T(8,128)(2,1)S(1)}, bf16[256,288]{1,0:T(8,128)(2,1)S(1)}, u32[]{:S(2)}, u32[]{:S(2)}) collective-permute-start(bf16[256,288]{1,0:T(8,128)(2,1)S(1)} %get-tuple-element.159), channel_id=1, source_target_pairs={{0,1},{1,0},{2,3},{3,2},{4,5},{5,4},{6,7},{7,6},{8,9},{9,8},{10,11... | collective-permute-start | bytes 442376 | tf_op jit(solution)/shard_map/ppermute | solution.py:52
  172.9 10.6 %collective-permute-start.40 = (bf16[256,288]{1,0:T(8,128)(2,1)S(1)}, bf16[256,288]{1,0:T(8,128)(2,1)S(1)}, u32[]{:S(2)}, u32[]{:S(2)}) collective-permute-start(bf16[256,288]{1,0:T(8,128)(2,1)S(1)} %get-tuple-element.160), channel_id=1, source_target_pairs={{0,3},{1,2},{2,1},{3,0},{4,7},{5,6},{6,5},{7,4},{8,11},{9,10},{10,... | collective-permute-start | bytes 442376 | tf_op jit(solution)/shard_map/ppermute | solution.py:52
  174.8 31.4 %collective-permute-start.41 = (bf16[576,1152]{1,0:T(8,128)(2,1)S(1)}, bf16[576,1152]{1,0:T(8,128)(2,1)S(1)}, u32[]{:S(2)}, u32[]{:S(2)}) collective-permute-start(bf16[576,1152]{1,0:T(8,128)(2,1)S(1)} %fc1_other.1.refs_2_), channel_id=1, source_target_pairs={{0,1},{1,0},{2,3},{3,2},{4,5},{5,4},{6,7},{7,6},{8,9},{9,8},{10,11... | collective-permute-start | bytes 3981320 | tf_op jit(solution)/shard_map/ppermute | solution.py:52
  200.6 20.3 %collective-permute-start.30 = (bf16[256,1152]{1,0:T(8,128)(2,1)S(1)}, bf16[256,1152]{1,0:T(8,128)(2,1)S(1)}, u32[]{:S(2)}, u32[]{:S(2)}) collective-permute-start(bf16[256,1152]{1,0:T(8,128)(2,1)S(1)} %copy-done.50), channel_id=1, source_target_pairs={{0,8},{8,0},{16,24},{24,16},{1,9},{9,1},{17,25},{25,17},{2,10},{10... | collective-permute-start | bytes 1769480 | tf_op jit(solution)/shard_map/ppermute | solution.py:52
  201.7 27.6 %collective-permute-start.31 = (bf16[256,1152]{1,0:T(8,128)(2,1)S(1)}, bf16[256,1152]{1,0:T(8,128)(2,1)S(1)}, u32[]{:S(2)}, u32[]{:S(2)}) collective-permute-start(bf16[256,1152]{1,0:T(8,128)(2,1)S(1)} %copy-done.48), channel_id=1, source_target_pairs={{0,16},{8,24},{16,0},{24,8},{1,17},{9,25},{17,1},{25,9},{2,18},{10... | collective-permute-start | bytes 1769480 | tf_op jit(solution)/shard_map/ppermute | solution.py:52
  202.5 17.8 %collective-permute-start.37 = (bf16[288,1152]{1,0:T(8,128)(2,1)S(1)}, bf16[288,1152]{1,0:T(8,128)(2,1)S(1)}, u32[]{:S(2)}, u32[]{:S(2)}) collective-permute-start(bf16[288,1152]{1,0:T(8,128)(2,1)S(1)} %get-tuple-element.155), channel_id=1, source_target_pairs={{0,2},{1,3},{2,0},{3,1},{4,6},{5,7},{6,4},{7,5},{8,10},{9,11},{10,... | collective-permute-start | bytes 1990664 | tf_op jit(solution)/shard_map/ppermute | solution.py:52
  204.4 27.3 %collective-permute-start.32 = (bf16[256,1152]{1,0:T(8,128)(2,1)S(1)}, bf16[256,1152]{1,0:T(8,128)(2,1)S(1)}, u32[]{:S(2)}, u32[]{:S(2)}) collective-permute-start(bf16[256,1152]{1,0:T(8,128)(2,1)S(1)} %get-tuple-element.140), channel_id=1, source_target_pairs={{0,24},{8,16},{16,8},{24,0},{1,25},{9,17},{17,9},{25,1},{2,26},{10... | collective-permute-start | bytes 1769480 | tf_op jit(solution)/shard_map/ppermute | solution.py:52
  206.2 33.9 %collective-permute-start.48 = (bf16[256,1152]{1,0:T(8,128)(2,1)S(1)}, bf16[256,1152]{1,0:T(8,128)(2,1)S(1)}, u32[]{:S(2)}, u32[]{:S(2)}) collective-permute-start(bf16[256,1152]{1,0:T(8,128)(2,1)S(1)} %attn_sum.1.refs_2_), channel_id=1, source_target_pairs={{0,2},{1,3},{2,0},{3,1},{4,6},{5,7},{6,4},{7,5},{8,10},{9,11},{10,... | collective-permute-start | bytes 1769480 | tf_op jit(solution)/shard_map/ppermute | solution.py:52
  220.6 23.1 %collective-permute-start.50 = (bf16[144,1152]{1,0:T(8,128)(2,1)S(1)}, bf16[144,1152]{1,0:T(8,128)(2,1)S(1)}, u32[]{:S(2)}, u32[]{:S(2)}) collective-permute-start(bf16[144,1152]{1,0:T(8,128)(2,1)S(1)} %get-tuple-element.176), channel_id=1, source_target_pairs={{0,4},{1,5},{2,6},{3,7},{4,0},{5,1},{6,2},{7,3},{8,12},{9,13},{10,... | collective-permute-start | bytes 995336 | tf_op jit(solution)/shard_map/ppermute | solution.py:52
  221.0 46.9 %collective-permute-start.44 = (bf16[288,1152]{1,0:T(8,128)(2,1)S(1)}, bf16[288,1152]{1,0:T(8,128)(2,1)S(1)}, u32[]{:S(2)}, u32[]{:S(2)}) collective-permute-start(bf16[288,1152]{1,0:T(8,128)(2,1)S(1)} %get-tuple-element.168), channel_id=1, source_target_pairs={{0,2},{1,3},{2,0},{3,1},{4,6},{5,7},{6,4},{7,5},{8,10},{9,11},{10,... | collective-permute-start | bytes 1990664 | tf_op jit(solution)/shard_map/ppermute | solution.py:52
  229.3 15.7 %collective-permute-start.45 = (bf16[288,864]{1,0:T(8,128)(2,1)S(1)}, bf16[288,864]{1,0:T(8,128)(2,1)S(1)}, u32[]{:S(2)}, u32[]{:S(2)}) collective-permute-start(bf16[288,864]{1,0:T(8,128)(2,1)S(1)} %get-tuple-element.170), channel_id=1, source_target_pairs={{0,8},{8,0},{16,24},{24,16},{1,9},{9,1},{17,25},{25,17},{2,10},{10... | collective-permute-start | bytes 1493000 | tf_op jit(solution)/shard_map/ppermute | solution.py:52
  242.4 25.2 %collective-permute-start.46 = (bf16[288,864]{1,0:T(8,128)(2,1)S(1)}, bf16[288,864]{1,0:T(8,128)(2,1)S(1)}, u32[]{:S(2)}, u32[]{:S(2)}) collective-permute-start(bf16[288,864]{1,0:T(8,128)(2,1)S(1)} %get-tuple-element.171), channel_id=1, source_target_pairs={{0,16},{8,24},{16,0},{24,8},{1,17},{9,25},{17,1},{25,9},{2,18},{10... | collective-permute-start | bytes 1493000 | tf_op jit(solution)/shard_map/ppermute | solution.py:52
  243.7 24.0 %collective-permute-start.47 = (bf16[288,864]{1,0:T(8,128)(2,1)S(1)}, bf16[288,864]{1,0:T(8,128)(2,1)S(1)}, u32[]{:S(2)}, u32[]{:S(2)}) collective-permute-start(bf16[288,864]{1,0:T(8,128)(2,1)S(1)} %get-tuple-element.172), channel_id=1, source_target_pairs={{0,24},{8,16},{16,8},{24,0},{1,25},{9,17},{17,9},{25,1},{2,26},{10... | collective-permute-start | bytes 1493000 | tf_op jit(solution)/shard_map/ppermute | solution.py:52
  245.0 23.2 %collective-permute-start.53 = (bf16[144,1152]{1,0:T(8,128)(2,1)S(1)}, bf16[144,1152]{1,0:T(8,128)(2,1)S(1)}, u32[]{:S(2)}, u32[]{:S(2)}) collective-permute-start(bf16[144,1152]{1,0:T(8,128)(2,1)S(1)} %fc2_cube.5.refs_2_.refs_0_), channel_id=1, source_target_pairs={{0,4},{1,5},{2,6},{3,7},{4,0},{5,1},{6,2},{7,3},{8,12},{9,13},{10,... | collective-permute-start | bytes 995336 | tf_op jit(solution)/shard_map/ppermute | solution.py:52
  245.1 23.2 %collective-permute-start.52 = (bf16[8,6912]{1,0:T(8,128)(2,1)S(1)}, bf16[8,6912]{1,0:T(8,128)(2,1)S(1)}, u32[]{:S(2)}, u32[]{:S(2)}) collective-permute-start(bf16[8,6912]{1,0:T(8,128)(2,1)S(1)} %sums.2.refs_4_.refs_0_), channel_id=1, source_target_pairs={{0,2},{1,3},{2,0},{3,1},{4,6},{5,7},{6,4},{7,5},{8,10},{9,11},{10,... | collective-permute-start | bytes 331784 | tf_op jit(solution)/shard_map/ppermute | solution.py:52
  268.5 28.1 %collective-permute-start.60 = (bf16[288,1152]{1,0:T(8,128)(2,1)S(1)}, bf16[288,1152]{1,0:T(8,128)(2,1)S(1)}, u32[]{:S(2)}, u32[]{:S(2)}) collective-permute-start(bf16[288,1152]{1,0:T(8,128)(2,1)S(1)} %fc2_cube.6.refs_2_.refs_0_), channel_id=1, source_target_pairs={{0,2},{1,3},{2,0},{3,1},{4,6},{5,7},{6,4},{7,5},{8,10},{9,11},{10,... | collective-permute-start | bytes 1990664 | tf_op jit(solution)/shard_map/ppermute | solution.py:52
  268.6 17.7 %collective-permute-start.54 = (bf16[8,6912]{1,0:T(8,128)(2,1)S(1)}, bf16[8,6912]{1,0:T(8,128)(2,1)S(1)}, u32[]{:S(2)}, u32[]{:S(2)}) collective-permute-start(bf16[8,6912]{1,0:T(8,128)(2,1)S(1)} %sums.3.refs_1_.refs_0_), channel_id=1, source_target_pairs={{0,4},{1,5},{2,6},{3,7},{4,0},{5,1},{6,2},{7,3},{8,12},{9,13},{10,... | collective-permute-start | bytes 331784 | tf_op jit(solution)/shard_map/ppermute | solution.py:52
  269.3 23.9 %collective-permute-start.51 = (bf16[144,1152]{1,0:T(8,128)(2,1)S(1)}, bf16[144,1152]{1,0:T(8,128)(2,1)S(1)}, u32[]{:S(2)}, u32[]{:S(2)}) collective-permute-start(bf16[144,1152]{1,0:T(8,128)(2,1)S(1)} %get-tuple-element.178), channel_id=1, source_target_pairs={{0,4},{1,5},{2,6},{3,7},{4,0},{5,1},{6,2},{7,3},{8,12},{9,13},{10,... | collective-permute-start | bytes 995336 | tf_op jit(solution)/shard_map/ppermute | solution.py:52
  272.2 21.1 %collective-permute-start.61 = (bf16[144,1152]{1,0:T(8,128)(2,1)S(1)}, bf16[144,1152]{1,0:T(8,128)(2,1)S(1)}, u32[]{:S(2)}, u32[]{:S(2)}) collective-permute-start(bf16[144,1152]{1,0:T(8,128)(2,1)S(1)} %get-tuple-element.181), channel_id=1, source_target_pairs={{0,8},{8,0},{16,24},{24,16},{1,9},{9,1},{17,25},{25,17},{2,10},{10... | collective-permute-start | bytes 995336 | tf_op jit(solution)/shard_map/ppermute | solution.py:52
  273.1 20.1 %collective-permute-start.62 = (bf16[144,1152]{1,0:T(8,128)(2,1)S(1)}, bf16[144,1152]{1,0:T(8,128)(2,1)S(1)}, u32[]{:S(2)}, u32[]{:S(2)}) collective-permute-start(bf16[144,1152]{1,0:T(8,128)(2,1)S(1)} %get-tuple-element.182), channel_id=1, source_target_pairs={{0,16},{8,24},{16,0},{24,8},{1,17},{9,25},{17,1},{25,9},{2,18},{10... | collective-permute-start | bytes 995336 | tf_op jit(solution)/shard_map/ppermute | solution.py:52
  286.3 10.2 %collective-permute-start.63 = (bf16[144,1152]{1,0:T(8,128)(2,1)S(1)}, bf16[144,1152]{1,0:T(8,128)(2,1)S(1)}, u32[]{:S(2)}, u32[]{:S(2)}) collective-permute-start(bf16[144,1152]{1,0:T(8,128)(2,1)S(1)} %get-tuple-element.183), channel_id=1, source_target_pairs={{0,24},{8,16},{16,8},{24,0},{1,25},{9,17},{17,9},{25,1},{2,26},{10... | collective-permute-start | bytes 995336 | tf_op jit(solution)/shard_map/ppermute | solution.py:52
  296.8 30.1 %collective-permute-start.67 = (bf16[576,1152]{1,0:T(8,128)(2,1)S(1)}, bf16[576,1152]{1,0:T(8,128)(2,1)S(1)}, u32[]{:S(2)}, u32[]{:S(2)}) collective-permute-start(bf16[576,1152]{1,0:T(8,128)(2,1)S(1)} %fc2_cube.7.refs_6_.refs_0_), channel_id=1, source_target_pairs={{0,1},{1,0},{2,3},{3,2},{4,5},{5,4},{6,7},{7,6},{8,9},{9,8},{10,11... | collective-permute-start | bytes 3981320 | tf_op jit(solution)/shard_map/ppermute | solution.py:52
  296.9 26.7 %collective-permute-start.68 = (bf16[288,864]{1,0:T(8,128)(2,1)S(1)}, bf16[288,864]{1,0:T(8,128)(2,1)S(1)}, u32[]{:S(2)}, u32[]{:S(2)}) collective-permute-start(bf16[288,864]{1,0:T(8,128)(2,1)S(1)} %qkv_sum.2.refs_2_.refs_0_), channel_id=1, source_target_pairs={{0,4},{1,5},{2,6},{3,7},{4,0},{5,1},{6,2},{7,3},{8,12},{9,13},{10,... | collective-permute-start | bytes 1493000 | tf_op jit(solution)/shard_map/ppermute | solution.py:52
  300.4 8.5 %collective-permute-start.59 = (bf16[16,6912]{1,0:T(8,128)(2,1)S(1)}, bf16[16,6912]{1,0:T(8,128)(2,1)S(1)}, u32[]{:S(2)}, u32[]{:S(2)}) collective-permute-start(bf16[16,6912]{1,0:T(8,128)(2,1)S(1)} %both.1.refs_2_.refs_0_), channel_id=1, source_target_pairs={{0,24},{8,16},{16,8},{24,0},{1,25},{9,17},{17,9},{25,1},{2,26},{10... | collective-permute-start | bytes 663560 | tf_op jit(solution)/shard_map/ppermute | solution.py:52
  302.0 18.9 %collective-permute-start.69 = (bf16[144,1152]{1,0:T(8,128)(2,1)S(1)}, bf16[144,1152]{1,0:T(8,128)(2,1)S(1)}, u32[]{:S(2)}, u32[]{:S(2)}) collective-permute-start(bf16[144,1152]{1,0:T(8,128)(2,1)S(1)} %proj_sum.1.refs_2_.refs_0_), channel_id=1, source_target_pairs={{0,2},{1,3},{6,4},{7,5},{8,10},{9,11},{14,12},{15,13},{16,18},{17,... | collective-permute-start | bytes 995336 | tf_op jit(solution)/shard_map/ppermute | solution.py:91
  303.3 10.2 %collective-permute-start.58 = (bf16[16,6912]{1,0:T(8,128)(2,1)S(1)}, bf16[16,6912]{1,0:T(8,128)(2,1)S(1)}, u32[]{:S(2)}, u32[]{:S(2)}) collective-permute-start(bf16[16,6912]{1,0:T(8,128)(2,1)S(1)} %both.1.refs_2_.refs_0_), channel_id=1, source_target_pairs={{0,16},{8,24},{16,0},{24,8},{1,17},{9,25},{17,1},{25,9},{2,18},{10... | collective-permute-start | bytes 663560 | tf_op jit(solution)/shard_map/ppermute | solution.py:52
  323.7 21.4 %collective-permute-start.72 = (bf16[288,864]{1,0:T(8,128)(2,1)S(1)}, bf16[288,864]{1,0:T(8,128)(2,1)S(1)}, u32[]{:S(2)}, u32[]{:S(2)}) collective-permute-start(bf16[288,864]{1,0:T(8,128)(2,1)S(1)} %qkv_sum.3.refs_2_.refs_0_), channel_id=1, source_target_pairs={{0,2},{1,3},{2,0},{3,1},{4,6},{5,7},{6,4},{7,5},{8,10},{9,11},{10,... | collective-permute-start | bytes 1493000 | tf_op jit(solution)/shard_map/ppermute | solution.py:52
  323.8 18.6 %collective-permute-start.56 = (bf16[144,1152]{1,0:T(8,128)(2,1)S(1)}, bf16[144,1152]{1,0:T(8,128)(2,1)S(1)}, u32[]{:S(2)}, u32[]{:S(2)}) collective-permute-start(bf16[144,1152]{1,0:T(8,128)(2,1)S(1)} %fc1_cube.5.refs_4_.refs_0_), channel_id=1, source_target_pairs={{0,4},{1,5},{2,6},{3,7},{4,0},{5,1},{6,2},{7,3},{8,12},{9,13},{10,... | collective-permute-start | bytes 995336 | tf_op jit(solution)/shard_map/ppermute | solution.py:52
  343.3 23.3 %collective-permute-start.70 = (bf16[288,1152]{1,0:T(8,128)(2,1)S(1)}, bf16[288,1152]{1,0:T(8,128)(2,1)S(1)}, u32[]{:S(2)}, u32[]{:S(2)}) collective-permute-start(bf16[288,1152]{1,0:T(8,128)(2,1)S(1)} %fc1_cube.6.refs_2_.refs_0_), channel_id=1, source_target_pairs={{0,2},{1,3},{2,0},{3,1},{4,6},{5,7},{6,4},{7,5},{8,10},{9,11},{10,... | collective-permute-start | bytes 1990664 | tf_op jit(solution)/shard_map/ppermute | solution.py:52
  346.3 26.2 %collective-permute-start.43 = (bf16[128,1152]{1,0:T(8,128)(2,1)S(1)}, bf16[128,1152]{1,0:T(8,128)(2,1)S(1)}, u32[]{:S(2)}, u32[]{:S(2)}) collective-permute-start(bf16[128,1152]{1,0:T(8,128)(2,1)S(1)} %get-tuple-element.167), channel_id=1, source_target_pairs={{0,4},{1,5},{2,6},{3,7},{4,0},{5,1},{6,2},{7,3},{8,12},{9,13},{10,... | collective-permute-start | bytes 884744 | tf_op jit(solution)/shard_map/ppermute | solution.py:52
  349.4 24.0 %collective-permute-start.76 = (bf16[144,1152]{1,0:T(8,128)(2,1)S(1)}, bf16[144,1152]{1,0:T(8,128)(2,1)S(1)}, u32[]{:S(2)}, u32[]{:S(2)}) collective-permute-start(bf16[144,1152]{1,0:T(8,128)(2,1)S(1)} %proj_line.4.refs_1_.refs_0_), channel_id=1, source_target_pairs={{2,0},{3,1},{4,6},{5,7},{10,8},{11,9},{12,14},{13,15},{18,16},{19,... | collective-permute-start | bytes 995336 | tf_op jit(solution)/shard_map/ppermute | solution.py:91
  369.0 16.4 %collective-permute-start.78 = (bf16[144,1152]{1,0:T(8,128)(2,1)S(1)}, bf16[144,1152]{1,0:T(8,128)(2,1)S(1)}, u32[]{:S(2)}, u32[]{:S(2)}) collective-permute-start(bf16[144,1152]{1,0:T(8,128)(2,1)S(1)} %get-tuple-element.196), channel_id=1, source_target_pairs={{0,8},{8,0},{16,24},{24,16},{1,9},{9,1},{17,25},{25,17},{2,10},{10... | collective-permute-start | bytes 995336 | tf_op jit(solution)/shard_map/ppermute | solution.py:52
  370.1 15.8 %collective-permute-start.79 = (bf16[144,1152]{1,0:T(8,128)(2,1)S(1)}, bf16[144,1152]{1,0:T(8,128)(2,1)S(1)}, u32[]{:S(2)}, u32[]{:S(2)}) collective-permute-start(bf16[144,1152]{1,0:T(8,128)(2,1)S(1)} %get-tuple-element.197), channel_id=1, source_target_pairs={{0,16},{8,24},{16,0},{24,8},{1,17},{9,25},{17,1},{25,9},{2,18},{10... | collective-permute-start | bytes 995336 | tf_op jit(solution)/shard_map/ppermute | solution.py:52
  371.4 14.6 %collective-permute-start.80 = (bf16[144,1152]{1,0:T(8,128)(2,1)S(1)}, bf16[144,1152]{1,0:T(8,128)(2,1)S(1)}, u32[]{:S(2)}, u32[]{:S(2)}) collective-permute-start(bf16[144,1152]{1,0:T(8,128)(2,1)S(1)} %get-tuple-element.198), channel_id=1, source_target_pairs={{0,24},{8,16},{16,8},{24,0},{1,25},{9,17},{17,9},{25,1},{2,26},{10... | collective-permute-start | bytes 995336 | tf_op jit(solution)/shard_map/ppermute | solution.py:52
  372.6 12.8 %collective-permute-start.75 = (bf16[128,1152]{1,0:T(8,128)(2,1)S(1)}, bf16[128,1152]{1,0:T(8,128)(2,1)S(1)}, u32[]{:S(2)}, u32[]{:S(2)}) collective-permute-start(bf16[128,1152]{1,0:T(8,128)(2,1)S(1)} %get-tuple-element.192), channel_id=1, source_target_pairs={{0,4},{1,5},{2,6},{3,7},{4,0},{5,1},{6,2},{7,3},{8,12},{9,13},{10,... | collective-permute-start | bytes 884744 | tf_op jit(solution)/shard_map/ppermute | solution.py:52
  373.4 16.6 %collective-permute-start.81 = (bf16[144,1152]{1,0:T(8,128)(2,1)S(1)}, bf16[144,1152]{1,0:T(8,128)(2,1)S(1)}, u32[]{:S(2)}, u32[]{:S(2)}) collective-permute-start(bf16[144,1152]{1,0:T(8,128)(2,1)S(1)} %get-tuple-element.190.refs_2_.refs_0_), channel_id=1, source_target_pairs={{0,1},{1,0},{2,3},{3,2},{4,5},{5,4},{6,7},{7,6},{8,9},{9,8},{10,11... | collective-permute-start | bytes 995336 | tf_op jit(solution)/shard_map/ppermute | solution.py:52
  (72 other events, 670.0 us)
